TPU v7x, 32 devices: a whole 2x2x4 slice. The times are simulated.
32 devices in a mesh: gx: 4 (over y, core), gy: 8 (over z, x).
Axes of the slice: x: 2, y: 2, z: 4, core: 2. Of those that a mesh axis runs over, the one named last changes fastest.
Arguments:
- table: bfloat16 [8192, 128], P(('gx', 'gy')), may hold values from -6 to 6
- request_rows: int32 [32, 32, 32], P(('gx', 'gy')), may hold values from 0 to 255, as said below
- send_counts: int32 [32, 32], P(('gx', 'gy')), may hold values from 1 to 32, as said below
- lookup_owner: int32 [131072], P(('gx', 'gy')), may hold values from 0 to 31
- lookup_rank: int32 [131072], P(('gx', 'gy')), may hold values from 0 to 31
- bag_lengths: int32 [32, 2048], P(('gx', 'gy')), may hold values from 1 to 8, 4096 in all within a row
- labels: int32 [4096], P(('gx', 'gy')), may hold values 0 or 1
- w_first: bfloat16 [2048, 2048], replicated, may hold values from -0.125 to 0.125
- w_second: bfloat16 [2048, 2048], replicated, may hold values from -0.125 to 0.125
- w_out: bfloat16 [2048], replicated, may hold values from -0.625 to 0.625
Outputs:
- grad_first: float32 [2048, 2048], P(('gx', 'gy'))
- grad_second: float32 [2048, 2048], P(('gx', 'gy'))
- grad_out: float32 [2048], P(('gx', 'gy'))
- row_grad: float32 [8192, 128], P(('gx', 'gy'))
Inputs may be any that keep to these rules, and one draw needn't show every extreme that they name: `request_rows`: the 32 local rows of one trainer and one owner are distinct. `send_counts`: each trainer sends 32 live slots to at least one owner.
All inputs are finite; a program needn't handle non-finite values. No bound on the sum of `labels` on one device may be relied on, other than what follows from the above.
Results may differ from a plain program's by a relative error of at most 0.009.
Values may be sent and summed in bfloat16 or wider, within the bound.
A program may use at most 128 MiB of HBM per device.

v0:
```python
import math

import jax
import jax.numpy as jnp
from jax import lax
from jax.sharding import PartitionSpec as P


def silu_slope(value):
    sig = jax.nn.sigmoid(value)
    return sig * (1.0 + value * (1.0 - sig))


def per_device(
    table,
    request_rows,
    send_counts,
    lookup_owner,
    lookup_rank,
    bag_lengths,
    labels,
    w_first,
    w_second,
    w_out,
):
    peers = lax.axis_size(("gx", "gy"))
    slots = request_rows.shape[2]
    width = table.shape[1]
    looks = lookup_owner.shape[0]
    samples = labels.shape[0]
    bags = bag_lengths.shape[1]
    inputs = w_first.shape[0]
    incoming = lax.all_to_all(
        request_rows, ("gx", "gy"), split_axis=1, concat_axis=0, tiled=True
    ).reshape(peers * slots)
    served = table[incoming]
    fetched = lax.all_to_all(
        served.reshape(peers, 1, slots, width),
        ("gx", "gy"),
        split_axis=0,
        concat_axis=1,
        tiled=True,
    )
    fetched = fetched.reshape(peers * slots, width)
    owner_ids = jnp.arange(peers, dtype=jnp.int32)
    counts = send_counts[0]
    match = lookup_owner[:, None] == owner_ids[None, :]
    lookup_count = jnp.sum(jnp.where(match, counts[None, :], 0), axis=1)
    slot_index = lookup_owner * slots + lookup_rank % lookup_count
    rows = fetched[slot_index]
    lengths = bag_lengths[0]
    starts = jnp.cumsum(lengths) - lengths
    marks = jnp.zeros((looks,), jnp.int32).at[starts].add(1)
    bag_of = jnp.cumsum(marks) - 1
    scale = lax.rsqrt(lengths.astype(jnp.float32))[:, None]
    block = math.gcd(512, looks)
    blocks = looks // block
    within = jnp.arange(block, dtype=jnp.int32)

    def block_table(index):
        ids = lax.dynamic_slice_in_dim(bag_of, index * block, block)
        base = ids[0]
        onehot = (ids[None, :] - base == within[:, None]).astype(jnp.bfloat16)
        return (base, onehot)

    def pool_step(index, acc):
        base, onehot = block_table(index)
        block_rows = lax.dynamic_slice_in_dim(rows, index * block, block, 0)
        part = jnp.dot(onehot, block_rows, preferred_element_type=jnp.float32)
        window = lax.dynamic_slice_in_dim(acc, base, block, 0) + part
        return lax.dynamic_update_slice_in_dim(acc, window, base, 0)

    pooled = lax.fori_loop(0, blocks, pool_step, jnp.zeros((bags + block, width), jnp.float32))
    x = (pooled[:bags] * scale).reshape(samples, inputs).astype(jnp.bfloat16)
    z1 = jnp.dot(x, w_first, preferred_element_type=jnp.float32)
    h1 = jax.nn.silu(z1).astype(jnp.bfloat16)
    z2 = jnp.dot(h1, w_second, preferred_element_type=jnp.float32)
    h2 = jax.nn.silu(z2).astype(jnp.bfloat16)
    logit = jnp.dot(h2, w_out, preferred_element_type=jnp.float32)
    dlogit = jax.nn.sigmoid(logit) - labels.astype(jnp.float32)
    dz2 = (dlogit[:, None] * w_out.astype(jnp.float32)[None, :] * silu_slope(z2)).astype(
        jnp.bfloat16
    )
    head_term = jnp.dot(dlogit, h2.astype(jnp.float32), precision=lax.Precision.HIGHEST)
    second_term = lax.dot_general(
        h1, dz2, (((0,), (0,)), ((), ())), preferred_element_type=jnp.float32
    )
    grad_second, grad_out = (
        lax.psum_scatter(second_term, ("gx", "gy"), scatter_dimension=0, tiled=True),
        lax.psum_scatter(head_term, ("gx", "gy"), scatter_dimension=0, tiled=True),
    )
    back_two = lax.dot_general(
        dz2, w_second, (((1,), (1,)), ((), ())), preferred_element_type=jnp.float32
    )
    dz1 = (back_two * silu_slope(z1)).astype(jnp.bfloat16)
    grad_first = lax.psum_scatter(
        lax.dot_general(x, dz1, (((0,), (0,)), ((), ())), preferred_element_type=jnp.float32),
        ("gx", "gy"),
        scatter_dimension=0,
        tiled=True,
    )
    back_one = lax.dot_general(
        dz1, w_first, (((1,), (1,)), ((), ())), preferred_element_type=jnp.float32
    )
    bag_grad = (back_one.reshape(bags, width) * scale).astype(jnp.bfloat16)
    padded_grad = jnp.concatenate([bag_grad, jnp.zeros((block, width), jnp.bfloat16)], axis=0)

    def spread_block(index):
        base, onehot = block_table(index)
        window = lax.dynamic_slice_in_dim(padded_grad, base, block, 0)
        return lax.dot_general(
            onehot, window, (((0,), (0,)), ((), ())), preferred_element_type=jnp.float32
        )

    lookup_grad = lax.map(spread_block, jnp.arange(blocks, dtype=jnp.int32)).reshape(looks, width)
    slot_grad = jax.ops.segment_sum(lookup_grad, slot_index, num_segments=peers * slots)
    returned = lax.all_to_all(
        slot_grad.reshape(1, peers, slots, width),
        ("gx", "gy"),
        split_axis=1,
        concat_axis=0,
        tiled=True,
    )
    returned = returned.reshape(peers * slots, width)
    row_grad = jax.ops.segment_sum(returned, incoming, num_segments=table.shape[0])
    return (grad_first, grad_second, grad_out, row_grad)


def solution(mesh):
    in_specs = (
        P(("gx", "gy"), None),
        P(("gx", "gy"), None, None),
        P(("gx", "gy"), None),
        P(("gx", "gy")),
        P(("gx", "gy")),
        P(("gx", "gy"), None),
        P(("gx", "gy")),
        P(),
        P(),
        P(),
    )
    out_specs = (
        P(("gx", "gy"), None),
        P(("gx", "gy"), None),
        P(("gx", "gy")),
        P(("gx", "gy"), None),
    )
    return jax.shard_map(
        per_device, mesh=mesh, in_specs=in_specs, out_specs=out_specs, check_vma=False
    )
```

profile of v0, /device:TPU:0, one launch (start us, length us, event | category | flops | bytes accessed | tf_op | source)
XLA Modules:
  0.0 861.2 jit_solution(3398454096774602286)
XLA Ops:
  7.2 7.3 all-to-all-start
  14.5 1.0 reduce-window.16
  15.8 0.7 compare_select_fusion
  16.5 14.7 %scatter_custom_fusion = s32[4096]{0:T(1024)S(1)} fusion(s32[2048]{0:T(1024)S(1)} %bitcast.76, s32[2048]{0:T(1024)S(1)} %broadcast.71, s32[]{:T(128)} %constant.80.clone.1), kind=kCustom, calls=%fused_computation.53 | custom fusion | flops 2048 | bytes 16388 | tf_op jit(solution)/shard_map/scatter-add | solution.py:53
  31.6 0.9 select_reduce_fusion
  32.5 1.0 fusion.22
  34.1 0.7 reduce.9
  34.9 4.3 gather_fusion
  39.2 5.8 all-to-all-start.1
  45.2 0.7 convert_element_type.46
  45.9 0.7 reshape.213
  46.6 0.7 convert_rsqrt_fusion
  47.3 8.4 all-to-all-done.1
  55.7 12.1 %gather_fusion.1 = bf16[4096,128]{1,0:T(8,128)(2,1)S(1)} fusion(bf16[1024,128]{1,0:T(8,128)(2,1)S(1)} %bitcast.65, s32[4096]{0:T(1024)S(1)} %get-tuple-element.172), kind=kCustom, calls=%fused_computation.1 | custom fusion | bytes 2113536 | tf_op jit(solution)/shard_map/gather | solution.py:50
  67.9 43.8 %while.25 = (s32[]{:T(128)}, f32[2560,128]{1,0:T(8,128)S(1)}, s32[4096]{0:T(1024)S(1)}, bf16[4096,128]{1,0:T(8,128)(2,1)S(1)}, s32[]{:T(128)}, /*index=5*/s32[]{:T(128)}, s32[]{:T(128)}, s32[]{:T(128)}, s32[]{:T(128)}) while((s32[]{:T(128)}, f32[2560,128]{1,0:T(8,128)S(1)}, s32[4096]{0:T(1024)S(1)}, ...), condition=%wide.region_7.8_spmd.clone, body=%wide.region_6.7_spmd.clone.sunk | while | flops 67437064 | bytes 1190093 | solution.py:73
  70.5 0.7 broadcast_subtract_fusion.4
  71.5 1.9 dynamic_update_slice.16
  76.0 0.7 broadcast_subtract_fusion.4
  77.1 1.9 dynamic_update_slice.16
  81.5 0.7 broadcast_subtract_fusion.4
  82.6 1.9 dynamic_update_slice.16
  87.1 0.7 broadcast_subtract_fusion.4
  88.1 1.9 dynamic_update_slice.16
  92.6 0.7 broadcast_subtract_fusion.4
  93.6 1.9 dynamic_update_slice.16
  98.1 0.7 broadcast_subtract_fusion.4
  99.2 1.9 dynamic_update_slice.16
  103.7 0.7 broadcast_subtract_fusion.4
  104.7 1.9 dynamic_update_slice.16
  109.2 0.7 broadcast_subtract_fusion.4
  110.2 1.5 dynamic_update_slice.16
  112.3 4.7 fusion.30
  117.0 4.8 multiply_convert_fusion.2
  122.1 0.7 copy-done.1
  122.9 8.3 fusion.27
  131.5 6.7 fusion.11
  138.2 8.1 fusion.31
  146.3 6.4 fusion.32
  153.3 45.3 %while.26 = (s32[]{:T(128)}, f32[8,512,128]{2,1,0:T(8,128)}, s32[8]{0:T(128)S(1)}, s32[4096]{0:T(1024)S(1)}, bf16[2560,128]{1,0:T(8,128)(2,1)S(1)}, /*index=5*/s...) while((s32[]{:T(128)}, f32[8,512,128]{2,1,0:T(8,128)}, s32[8]{0:T(128)S(1)}, ...), condition=%wide.region_12.13_spmd.clone, body=%wide.region_11.12_spmd.clone.sunk | while | flops 67371528 | bytes 403685 | solution.py:115
  153.3 0.6 dynamic_slice.58
  157.1 0.7 broadcast_subtract_fusion.5
  157.8 1.2 fusion.49
  159.0 0.6 dynamic_slice.58
  162.7 0.7 broadcast_subtract_fusion.5
  163.5 1.2 fusion.49
  168.4 0.7 broadcast_subtract_fusion.5
  169.1 1.2 fusion.49
  174.0 0.7 broadcast_subtract_fusion.5
  174.8 1.2 fusion.49
  179.7 0.7 broadcast_subtract_fusion.5
  180.4 1.2 fusion.49
  185.4 0.7 broadcast_subtract_fusion.5
  186.1 1.2 fusion.49
  191.1 0.7 broadcast_subtract_fusion.5
  191.8 1.2 fusion.49
  196.7 0.7 broadcast_subtract_fusion.5
  197.4 1.2 fusion.49
  198.6 23.5 %scatter_custom_fusion.1 = f32[1024,128]{1,0:T(8,128)} fusion(s32[4096]{0:T(1024)S(1)} %get-tuple-element.173, f32[4096,128]{1,0:T(8,128)} %bitcast.78, f32[]{:T(128)} %constant.81.clone.1), kind=kCustom, calls=%fused_computation.37 | custom fusion | flops 524288 | bytes 524800 | tf_op jit(solution)/shard_map/scatter-add | solution.py:116
  222.1 2.6 all-to-all-start.2
  225.1 53.1 %all-reduce.1 = f32[2048]{0:T(1024)S(1)} all-reduce(f32[2048]{0:T(1024)S(1)} %bitcast.72), channel_id=4, replica_groups=mesh['gx'=4,'gy'=8] {'gx','gy'}, use_global_device_ids=true, to_apply=%region_10.11.clone | all-reduce | flops 2048 | bytes 16384
  278.2 0.6 dynamic-slice
  278.8 6.6 scatter_custom_fusion.2
  285.4 208.7 %reduce-scatter.5.cloned.1.call-done = f32[64,2048]{1,0:T(8,128)} async-done(((f32[2048,2048]{1,0:T(8,128)}), f32[64,2048]{1,0:T(8,128)}) %reduce-scatter.5.cloned.1.call-update) | async-done | bytes 524304 | tf_op jit(solution)/shard_map/reduce_scatter | solution.py:89
  494.1 360.3 %reduce-scatter.3.cloned.1.call-done = f32[64,2048]{1,0:T(8,128)} async-done(((f32[2048,2048]{1,0:T(8,128)}), f32[64,2048]{1,0:T(8,128)}) %reduce-scatter.3.cloned.1.call-update) | async-done | bytes 524304 | tf_op jit(solution)/shard_map/reduce_scatter | solution.py:96
  (82 shorter events, 19.2 us)
Async XLA Ops:
  7.2 27.7 %copy-start = (bf16[256,128]{1,0:T(8,128)(2,1)S(1)}, bf16[256,128]{1,0:T(8,128)(2,1)}, u32[]{:S(2)}) copy-start(bf16[256,128]{1,0:T(8,128)(2,1)} %param.14) | copy-start | bytes 196612
  7.2 26.4 %all-to-all-start = ((s32[1,32,32]{2,0,1:T(1,128)}), s32[1,32,32]{2,0,1:T(1,128)S(1)}, u32[]{:S(2)}, u32[]{:S(2)}) async-start(s32[1,32,32]{2,0,1:T(1,128)} %bitcast.74), calls=%async_computation | async-start | bytes 32768 | tf_op jit(solution)/shard_map/all_to_all | solution.py:33
  39.2 16.5 %all-to-all-start.1 = ((bf16[32,1,32,128]{3,2,1,0:T(8,128)(2,1)}), bf16[32,1,32,128]{3,2,1,0:T(8,128)(2,1)S(1)}, u32[]{:S(2)}, u32[]{:S(2)}) async-start(bf16[32,1,32,128]{3,2,1,0:T(8,128)(2,1)} %bitcast.9), calls=%async_computation.1 | async-start | bytes 524288 | tf_op jit(solution)/shard_map/all_to_all | solution.py:37
  45.1 449.1 %reduce-scatter.5.cloned.1.call-start = ((), (), s32[]{:S(2)}) async-start(), calls=%async_computation.6 | async-start | bytes 17301504 | tf_op jit(solution)/shard_map/reduce_scatter | solution.py:89
  117.0 4.9 copy-start.2
  121.9 1.0 copy-start.1
  131.2 723.2 %reduce-scatter.3.cloned.1.call-start = ((), (), s32[]{:S(2)}) async-start(), calls=%async_computation.5 | async-start | bytes 17301504 | tf_op jit(solution)/shard_map/reduce_scatter | solution.py:96
  222.1 56.7 %all-to-all-start.2 = ((f32[1,32,32,128]{3,2,0,1:T(8,128)}), f32[1,32,32,128]{3,2,0,1:T(8,128)S(1)}, u32[]{:S(2)}, u32[]{:S(2)}) async-start(f32[1,32,32,128]{3,2,0,1:T(8,128)} %bitcast.17), calls=%async_computation.4 | async-start | bytes 1048576 | tf_op jit(solution)/shard_map/all_to_all | solution.py:117
Sparse Core Ops, SparseCore 0:
  131.4 362.7 reduce-scatter.4
  497.0 357.3 reduce-scatter.2
where the time goes:
time: 863 us; the launch traced here: 861 us
  waiting for transfers between devices  577 us (67%)
  other arithmetic  63.2 us (7%)
  blocking collectives  53.1 us (6%)
  matrix products  51.4 us (6%)
  local copies, waits for them, and re-layouts  49.1 us (6%)
  loops' own time  36.7 us (4%)
  starting transfers between devices  16 us (2%)
  between operations  14.3 us (2%)
    reduce_scatter x1, waiting for transfers between devices, per_device(): lax.psum_scatter(lax.dot_general(x, dz1, (((0,), (0,)), ((), ())), prefer...  360 us
    reduce_scatter x1, waiting for transfers between devices, per_device(): lax.psum_scatter(second_term, ('gx', 'gy'), scatter_dimension=0, tiled=True)  209 us
    unnamed x1, blocking collectives  53.1 us
    scatter-add x1, other arithmetic, per_device(): jax.ops.segment_sum(lookup_grad, slot_index, num_segments=peers * slots)  23.5 us
    another operation x1, loops' own time, per_device(): lax.map(spread_block, jnp.arange(blocks, dtype=jnp.int32))  20.8 us
  transfers between devices with their start and end apart: 5, of which 3 were waited for; matrix products, arithmetic and copies ran while one was open for 11% of the time, Pallas kernels for 0%

commit v1 on v0

v1 whole, which is shorter than its diff:
```python
import jax
import jax.numpy as jnp
from jax import lax
from jax.sharding import PartitionSpec as P

AXES = ("gx", "gy")


def silu_slope(value):
    sig = jax.nn.sigmoid(value)
    return sig * (1.0 + value * (1.0 - sig))


def swap(value, mask):
    peers = lax.axis_size(AXES)
    return lax.ppermute(value, AXES, [(d, d ^ mask) for d in range(peers)])


def pick(value, dim, index):
    return lax.dynamic_index_in_dim(value, index, dim, keepdims=False)


def gather_left(left, core_bit):
    peers = lax.axis_size(AXES)
    me = lax.axis_index(AXES)
    samples, total = left.shape
    core, low = (me >> core_bit) & 1, me & 1
    split = left.T.reshape(
        peers >> (core_bit + 1), 2, 1 << (core_bit - 1), 2, total // peers, samples
    )

    def quarter(c, x):
        return pick(pick(split, 3, x), 1, c)

    return jnp.concatenate(
        [
            quarter(core, low),
            swap(quarter(1 - core, low), 1 << core_bit),
            swap(quarter(core, 1 - low), 1),
            swap(quarter(1 - core, 1 - low), 1 + (1 << core_bit)),
        ],
        axis=-1,
    )


def reduce_gradient(left, right, core_bit):
    peers = lax.axis_size(AXES)
    me = lax.axis_index(AXES)
    across = swap(right, 1)
    right = jnp.concatenate(
        [right, swap(right, 1 << core_bit), across, swap(across, 1 << core_bit)], axis=0
    )
    high = [b for b in range(peers.bit_length() - 2, core_bit, -1)]
    mid = [b for b in range(core_bit - 1, 0, -1)]
    bits = high + mid
    rows, depth = left.shape[-2:]
    left = left.reshape([2] * len(bits) + [rows, depth])

    def product(part):
        out = jnp.dot(part.reshape(-1, depth), right, preferred_element_type=jnp.float32)
        return out.reshape(part.shape[:-1] + (right.shape[1],))

    current = None
    for bit in high[::-1] + mid[::-1]:
        dim = bits.index(bit)
        mine = (me >> bit) & 1
        if current is None:
            sent = product(pick(left, dim, 1 - mine)).astype(jnp.bfloat16)
            got = swap(sent, 1 << bit)
            kept = product(pick(left, dim, mine))
        else:
            got = swap(pick(current, dim, 1 - mine).astype(jnp.bfloat16), 1 << bit)
            kept = pick(current, dim, mine)
        current = kept + got.astype(jnp.float32)
        bits.remove(bit)
    return current.reshape(rows, -1)


def per_device(
    table,
    request_rows,
    send_counts,
    lookup_owner,
    lookup_rank,
    bag_lengths,
    labels,
    w_first,
    w_second,
    w_out,
):
    peers = lax.axis_size(AXES)
    core_bit = lax.axis_size("gy").bit_length() - 1
    slots = request_rows.shape[2]
    width = table.shape[1]
    looks = lookup_owner.shape[0]
    samples = labels.shape[0]
    bags = bag_lengths.shape[1]
    inputs = w_first.shape[0]
    most = 8
    incoming = lax.all_to_all(
        request_rows, AXES, split_axis=1, concat_axis=0, tiled=True
    ).reshape(peers * slots)
    served = table[incoming]
    fetched = lax.all_to_all(
        served.reshape(peers, 1, slots, width), AXES, split_axis=0, concat_axis=1, tiled=True
    ).reshape(peers * slots, width)

    owner_ids = jnp.arange(peers, dtype=jnp.int32)
    match = lookup_owner[:, None] == owner_ids[None, :]
    lookup_count = jnp.sum(jnp.where(match, send_counts[0][None, :], 0), axis=1)
    slot = lookup_rank % lookup_count
    lengths = bag_lengths[0]
    starts = jnp.cumsum(lengths) - lengths
    scale = lax.rsqrt(lengths.astype(jnp.float32))[:, None]
    owner_pad = jnp.pad(lookup_owner, (0, most)).astype(jnp.bfloat16)
    slot_pad = jnp.pad(slot, (0, most)).astype(jnp.bfloat16)
    shifted = jnp.stack(
        [owner_pad[j : j + looks] for j in range(most)]
        + [slot_pad[j : j + looks] for j in range(most)]
    )
    first = (starts[:, None] == jnp.arange(looks, dtype=jnp.int32)[None, :]).astype(jnp.bfloat16)
    found = lax.dot_general(
        first, shifted, (((1,), (1,)), ((), ())), preferred_element_type=jnp.float32
    )
    code = found[:, :most] * slots + found[:, most:]
    place = jnp.arange(most, dtype=jnp.int32)[None, :]
    code = jnp.where(place < lengths[:, None], code, -1.0)
    names = jnp.arange(peers * slots, dtype=jnp.int32).astype(jnp.float32)[None, :]
    counted = jnp.zeros((bags, peers * slots), jnp.float32)
    for j in range(most):
        counted = counted + (code[:, j : j + 1] == names).astype(jnp.float32)
    counted = counted.astype(jnp.bfloat16)

    pooled = jnp.dot(counted, fetched, preferred_element_type=jnp.float32)
    x = (pooled * scale).astype(jnp.bfloat16).reshape(samples, inputs)
    x_left = gather_left(x, core_bit)
    z1 = jnp.dot(x, w_first, preferred_element_type=jnp.float32)
    h1 = jax.nn.silu(z1).astype(jnp.bfloat16)
    h1_left = gather_left(h1, core_bit)
    z2 = jnp.dot(h1, w_second, preferred_element_type=jnp.float32)
    h2 = jax.nn.silu(z2).astype(jnp.bfloat16)
    logit = jnp.dot(h2, w_out, preferred_element_type=jnp.float32)
    dlogit = jax.nn.sigmoid(logit) - labels.astype(jnp.float32)
    dz2 = (dlogit[:, None] * w_out.astype(jnp.float32)[None, :] * silu_slope(z2)).astype(
        jnp.bfloat16
    )
    head_term = jnp.sum(dlogit[:, None] * h2.astype(jnp.float32), axis=0)
    grad_second = reduce_gradient(h1_left, dz2, core_bit)
    back_two = lax.dot_general(
        dz2, w_second, (((1,), (1,)), ((), ())), preferred_element_type=jnp.float32
    )
    dz1 = (back_two * silu_slope(z1)).astype(jnp.bfloat16)
    grad_first = reduce_gradient(x_left, dz1, core_bit)
    back_one = lax.dot_general(
        dz1, w_first, (((1,), (1,)), ((), ())), preferred_element_type=jnp.float32
    )
    bag_grad = (back_one.reshape(bags, width) * scale).astype(jnp.bfloat16)
    slot_grad = lax.dot_general(
        counted, bag_grad, (((0,), (0,)), ((), ())), preferred_element_type=jnp.float32
    )
    share = head_term.shape[0] // peers
    extra = -(-share // width)
    head = jnp.pad(head_term.reshape(peers, share), ((0, 0), (0, extra * width - share)))
    outgoing = jnp.concatenate(
        [slot_grad.reshape(peers, slots, width), head.reshape(peers, extra, width)], axis=1
    ).astype(jnp.bfloat16)
    returned = lax.all_to_all(outgoing[None], AXES, split_axis=1, concat_axis=0, tiled=True)[:, 0]
    grad_out = jnp.sum(returned[:, slots:].astype(jnp.float32), axis=0).reshape(-1)[:share]
    home = (
        jnp.arange(table.shape[0], dtype=jnp.int32)[:, None] == incoming[None, :]
    ).astype(jnp.bfloat16)
    row_grad = jnp.dot(
        home, returned[:, :slots].reshape(peers * slots, width), preferred_element_type=jnp.float32
    )
    return (grad_first, grad_second, grad_out, row_grad)


def solution(mesh):
    in_specs = (
        P(AXES, None),
        P(AXES, None, None),
        P(AXES, None),
        P(AXES),
        P(AXES),
        P(AXES, None),
        P(AXES),
        P(),
        P(),
        P(),
    )
    out_specs = (P(AXES, None), P(AXES, None), P(AXES), P(AXES, None))
    return jax.shard_map(
        per_device, mesh=mesh, in_specs=in_specs, out_specs=out_specs, check_vma=False
    )
```

time: 863 us -> 193 us (0.22)
  waiting for transfers between devices: 577 us -> 85.2 us
  blocking collectives: 53.1 us -> 0 us
  other arithmetic: 63.2 us -> 11.1 us
  local copies, waits for them, and re-layouts: 49.1 us -> 8.43 us
  loops' own time: 36.7 us -> 0 us
  starting transfers between devices: 16 us -> 34.2 us
  between operations: 14.3 us -> 1.4 us
    reduce_scatter x2 -> x0, waiting for transfers between devices: 569 us -> none  [the longest x1 360 us: per_device(): lax.psum_scatter(lax.dot_general(x, dz1, (((0,), (0,)), ((), ())), prefer...]
    ppermute x0 -> x18, waiting for transfers between devices: none -> 74.7 us  [swap(): return lax.ppermute(value, AXES, [(d, d ^ mask) for d in range(peers)])]
    unnamed x1 -> x0, blocking collectives: 53.1 us -> none
    scatter-add x3 -> x0, other arithmetic: 44.8 us -> none  [the longest x1 23.5 us: per_device(): jax.ops.segment_sum(lookup_grad, slot_index, num_segments=peers * slots)]
    another operation x2 -> x0, loops' own time: 36.7 us -> none  [the longest x1 20.8 us: per_device(): lax.map(spread_block, jnp.arange(blocks, dtype=jnp.int32))]
    ppermute x0 -> x18, starting transfers between devices: none -> 18.3 us  [swap(): return lax.ppermute(value, AXES, [(d, d ^ mask) for d in range(peers)])]
    dynamic_update_slice x8 -> x0, local copies, waits for them, and re-layouts: 15 us -> none  [pool_step(): return lax.dynamic_update_slice_in_dim(acc, window, base, 0)]
    gather x1 -> x0, local copies, waits for them, and re-layouts: 12.1 us -> none  [per_device(): rows = fetched[slot_index]]
  transfers between devices with their start and end apart: 5 -> 21, of which waited for: 3 -> 10; matrix products, arithmetic and copies ran while one was open for 11% -> 22% of each run, Pallas kernels for 0% -> 0%
where the time goes in v1:
time: 193 us; the launch traced here: 192 us
  waiting for transfers between devices  85.2 us (44%)
  matrix products  52.2 us (27%)
  starting transfers between devices  34.2 us (18%)
  other arithmetic  11.1 us (6%)
  local copies, waits for them, and re-layouts  8.43 us (4%)
    ppermute x18, waiting for transfers between devices, swap(): return lax.ppermute(value, AXES, [(d, d ^ mask) for d in range(peers)])  74.7 us
    ppermute x18, starting transfers between devices, swap(): return lax.ppermute(value, AXES, [(d, d ^ mask) for d in range(peers)])  18.3 us
    all_to_all x1, waiting for transfers between devices, per_device(): lax.all_to_all(served.reshape(peers, 1, slots, width), AXES, split_axis=0...  10.3 us
    dot_general x4, matrix products, product(): jnp.dot(part.reshape(-1, depth), right, preferred_element_type=jnp.float32)  9.6 us
    dot_general x1, matrix products, per_device(): pooled = jnp.dot(counted, fetched, preferred_element_type=jnp.float32)  8.07 us
    dot_general x1, matrix products, per_device(): lax.dot_general(counted, bag_grad, (((0,), (0,)), ((), ())), preferred_el...  7.72 us
    all_to_all x1, starting transfers between devices, per_device(): lax.all_to_all(request_rows, AXES, split_axis=1, concat_axis=0, tiled=True)  7.3 us
    dot_general x1, matrix products, per_device(): lax.dot_general(dz1, w_first, (((1,), (1,)), ((), ())), preferred_element...  6.48 us
  transfers between devices with their start and end apart: 21, of which 10 were waited for; matrix products, arithmetic and copies ran while one was open for 22% of the time, Pallas kernels for 0%

profile of v1, /device:TPU:0, one launch (start us, length us, event | category | flops | bytes accessed | tf_op | source)
XLA Modules:
  0.0 192.5 jit_solution(3989396119293861889)
XLA Ops:
  0.6 7.3 %all-to-all-start = ((s32[1,32,32]{2,0,1:T(1,128)}), s32[1,32,32]{2,0,1:T(1,128)S(1)}, u32[]{:S(2)}, u32[]{:S(2)}) async-start(s32[1,32,32]{2,0,1:T(1,128)} %bitcast.157), calls=%async_computation | async-start | bytes 32768 | tf_op jit(solution)/shard_map/all_to_all | solution.py:100
  8.0 0.7 slice.99
  8.8 0.9 select_reduce_fusion
  9.7 0.9 fusion.44
  11.0 0.7 rsqrt_reduce_fusion
  11.7 1.0 reduce-window.9
  12.9 0.7 convert_rsqrt_fusion
  13.6 0.8 bitcast_subtract_fusion
  14.4 0.4 stack.67
  14.8 6.2 %fusion = f32[2048,16]{0,1:T(8,128)S(1)} fusion(bf16[16,4096]{1,0:T(8,128)(2,1)S(1)} %stack.67, s32[2048]{0:T(1024)S(1)} %bitcast_subtract_fusion), kind=kOutput, calls=%fused_computation.2 | convolution fusion | flops 276824064 | bytes 270336 | tf_op jit(solution)/shard_map/dot_general | solution.py:122
  21.1 0.6 add_convert_fusion.12
  21.8 0.5 broadcast.178
  22.3 0.7 reduce.12
  23.2 4.3 %gather_fusion = bf16[1024,128]{1,0:T(8,128)(2,1)} fusion(bf16[256,128]{1,0:T(8,128)(2,1)S(1)} %copy-done, s32[1024]{0:T(1024)S(1)} %broadcast_clamp_fusion), kind=kCustom, calls=%fused_computation | custom fusion | bytes 528384 | tf_op jit(solution)/shard_map/gather | solution.py:103
  27.5 6.0 %all-to-all-start.1 = ((bf16[32,1,32,128]{3,2,1,0:T(8,128)(2,1)}), bf16[32,1,32,128]{3,2,1,0:T(8,128)(2,1)S(1)}, u32[]{:S(2)}, u32[]{:S(2)}) async-start(bf16[32,1,32,128]{3,2,1,0:T(8,128)(2,1)} %bitcast.15), calls=%async_computation.1 | async-start | bytes 524288 | tf_op jit(solution)/shard_map/all_to_all | solution.py:104
  33.6 10.3 %all-to-all-done.1 = bf16[32,1,32,128]{3,2,1,0:T(8,128)(2,1)S(1)} async-done(((bf16[32,1,32,128]{3,2,1,0:T(8,128)(2,1)}), bf16[32,1,32,128]{3,2,1,0:T(8,128)(2,1)S(1)}, u32[]{:S(2)}, u32[]{:S(2)}) %all-to-all-start.1) | async-done | bytes 262176 | tf_op jit(solution)/shard_map/all_to_all | solution.py:104
  44.0 8.1 %fusion.13 = bf16[2048,128]{1,0:T(8,128)(2,1)S(1)} fusion(bf16[1024,128]{1,0:T(8,128)(2,1)S(1)} %bitcast.144, f32[1024]{0:T(1024)S(1)} %iota_convert_fusion, f32[2048]{0:T(1024)S(1)} %bitcast.161, f32[2048]{0:T(1024)S(1)} %bitcast.163, f32[2048]{0:T(1024)S(1)} %bitcast.165, f32[2048]{0:T(1024)S(1)} %bitcast.167, f32[2048]{0:T(1024)S(1)} %bitcast.169, ...), kind=kOutput, calls=%fused_computation.23 | convolution fusion | flops 587726848 | bytes 864256 | tf_op jit(solution)/shard_map/dot_general | solution.py:134
  52.1 0.2 reshape.328
  52.4 4.9 %fusion.26 = (bf16[2048,128]{0,1:T(8,128)(2,1)S(1)}, f32[128,2048]{1,0:T(8,128)S(1)}) fusion(bf16[128,2048]{1,0:T(8,128)(2,1)S(1)} %reshape.328, bf16[2048,2048]{1,0:T(8,128)(2,1)} %param.17), kind=kOutput, calls=%fused_computation.52 | convolution fusion | flops 1075052544 | bytes 10485760 | tf_op jit(solution)/shard_map/dot_general | solution.py:137
  57.3 5.0 %multiply_convert_fusion.1 = (bf16[128,2048]{1,0:T(8,128)(2,1)S(1)}, f32[128,2048]{1,0:T(8,128)S(1)}) fusion(bf16[2048,2048]{1,0:T(8,128)(2,1)} %param.18, f32[128,2048]{1,0:T(8,128)S(1)} %get-tuple-element.39), kind=kOutput, calls=%fused_computation.48 | convolution fusion | flops 1076363264 | bytes 11010048 | tf_op jit(solution)/shard_map/dot_general | solution.py:140
  62.3 0.2 fusion.22
  62.5 1.1 multiply_reduce_fusion
  63.6 3.0 %fusion.14 = bf16[128,2048]{1,0:T(8,128)(2,1)S(1)} fusion(bf16[128,2048]{1,0:T(8,128)(2,1)S(1)} %get-tuple-element.35, bf16[2048,2048]{1,0:T(8,128)(2,1)S(1)} %bitcast.178, f32[128,2048]{1,0:T(8,128)S(1)} %get-tuple-element.39), kind=kOutput, calls=%fused_computation.24 | convolution fusion | flops 1076101120 | bytes 10485760 | tf_op jit(solution)/shard_map/dot_general | solution.py:149
  66.6 1.1 collective-permute-start.4
  67.7 0.3 copy.32
  68.0 1.1 collective-permute-start.13
  69.1 0.9 collective-permute-start.2
  70.0 1.0 collective-permute-start.1
  71.1 0.3 mul.95
  71.4 6.5 %fusion.15 = bf16[128,2048]{1,0:T(8,128)(2,1)S(1)} fusion(bf16[128,2048]{1,0:T(8,128)(2,1)S(1)} %fusion.14, bf16[2048,2048]{1,0:T(8,128)(2,1)} %param.17, f32[16,8,16,128]{3,2,1,0:T(8,128)S(1)} %bitcast.137), kind=kOutput, calls=%fused_computation.25 | convolution fusion | flops 1074266112 | bytes 10485760 | tf_op jit(solution)/shard_map/dot_general | solution.py:154
  77.9 0.2 reshape.345
  78.2 3.4 %collective-permute-done.4 = bf16[128,2048]{1,0:T(8,128)(2,1)} collective-permute-done((bf16[128,2048]{1,0:T(8,128)(2,1)S(1)}, bf16[128,2048]{1,0:T(8,128)(2,1)}, u32[]{:S(2)}, u32[]{:S(2)}) %collective-permute-start.4) | collective-permute-done | bytes 524320 | tf_op jit(solution)/shard_map/ppermute | solution.py:16
  81.7 7.7 %fusion.17 = bf16[1,32,32,128]{3,2,1,0:T(8,128)(2,1)S(1)} fusion(bf16[2048,128,1]{1,0,2:T(8,128)(2,1)S(1)} %reshape.345, f32[2048]{0:T(1024)S(1)} %bitcast.162, f32[2048]{0:T(1024)S(1)} %bitcast.164, f32[2048]{0:T(1024)S(1)} %bitcast.166, f32[2048]{0:T(1024)S(1)} %bitcast.168, f32[2048]{0:T(1024)} %bitcast.170, f32[2048]{0:T(1024)} %bitcast.172, ...), kind=kOutput, calls=%fused_computation.29 | convolution fusion | flops 587333632 | bytes 856064 | tf_op jit(solution)/shard_map/dot_general | solution.py:158
  89.5 4.5 %collective-permute-done.2 = bf16[2,4,64,128]{3,2,1,0:T(8,128)(2,1)S(1)} collective-permute-done((bf16[2,4,64,128]{3,2,1,0:T(8,128)(2,1)S(1)}, bf16[2,4,64,128]{3,2,1,0:T(8,128)(2,1)S(1)}, u32[]{:S(2)}, u32[]{:S(2)}) %collective-permute-start.2) | collective-permute-done | bytes 131104 | tf_op jit(solution)/shard_map/ppermute | solution.py:16
  94.1 1.3 collective-permute-start
  95.4 0.8 maximum_bitcast_fusion.6
  96.2 0.3 copy.33
  96.4 2.6 %all-to-all-start.2 = ((bf16[1,32,33,128]{3,2,0,1:T(8,128)(2,1)}), bf16[1,32,33,128]{3,2,0,1:T(8,128)(2,1)S(1)}, u32[]{:S(2)}, u32[]{:S(2)}) async-start(bf16[1,32,33,128]{3,2,0,1:T(8,128)(2,1)} %maximum_bitcast_fusion.6), calls=%async_computation.2 | async-start | bytes 655360 | tf_op jit(solution)/shard_map/all_to_all | solution.py:167
  99.1 0.2 collective-permute-start.12
  99.3 1.6 collective-permute-start.11
  101.0 0.5 collective-permute-start.10
  101.5 0.5 collective-permute-start.14
  102.0 3.0 %convolution_convert_fusion.1 = bf16[2,2,64,2048]{3,2,1,0:T(8,128)(2,1)} fusion(bf16[128,2048]{1,0:T(8,128)(2,1)} %collective-permute-done.5, bf16[128,2048]{1,0:T(8,128)(2,1)} %collective-permute-done.4, bf16[128,2048]{1,0:T(8,128)(2,1)} %collective-permute-done.3, bf16[128,2048]{1,0:T(8,128)(2,1)S(1)} %fusion.14, ...), kind=kOutput, calls=%fused_computation.19 | convolution fusion | flops 545783808 | bytes 3407876 | tf_op jit(solution)/shard_map/dot_general | solution.py:60
  105.1 2.2 %collective-permute-done.11 = bf16[2,4,64,128]{3,2,1,0:T(8,128)(2,1)S(1)} collective-permute-done((bf16[2,4,64,128]{3,2,1,0:T(8,128)(2,1)S(1)}, bf16[2,4,64,128]{3,2,1,0:T(8,128)(2,1)S(1)}, u32[]{:S(2)}, u32[]{:S(2)}) %collective-permute-start.11) | collective-permute-done | bytes 131104 | tf_op jit(solution)/shard_map/ppermute | solution.py:16
  107.2 1.9 collective-permute-start.6
  109.2 1.8 collective-permute-done.10
  111.1 0.1 all-to-all-done.2
  111.3 2.1 %convolution_convert_fusion = bf16[2,2,64,2048]{3,2,1,0:T(8,128)(2,1)S(1)} fusion(bf16[128,2048]{1,0:T(8,128)(2,1)} %collective-permute-done.14, bf16[128,2048]{1,0:T(8,128)(2,1)} %collective-permute-done.13, bf16[128,2048]{1,0:T(8,128)(2,1)} %collective-permute-done.12, bf16[128,2048]{1,0:T(8,128)(2,1)S(1)} %get-tuple-element.35, ...), kind=kOutput, calls=%fused_computation.18 | convolution fusion | flops 545783808 | bytes 3407876 | tf_op jit(solution)/shard_map/dot_general | solution.py:60
  113.4 1.5 collective-permute-start.15
  114.8 0.5 slice_bitcast_fusion
  115.3 1.0 fusion.27
  116.3 17.1 %collective-permute-done.6 = bf16[2,2,64,2048]{3,2,1,0:T(8,128)(2,1)} collective-permute-done((bf16[2,2,64,2048]{3,2,1,0:T(8,128)(2,1)}, bf16[2,2,64,2048]{3,2,1,0:T(8,128)(2,1)}, u32[]{:S(2)}, u32[]{:S(2)}) %collective-permute-start.6) | collective-permute-done | bytes 1048608 | tf_op jit(solution)/shard_map/ppermute | solution.py:16
  133.4 2.4 %convolution_add_fusion.1 = f32[2,2,64,2048]{3,2,1,0:T(8,128)S(1)} fusion(bf16[2,2,64,2048]{3,2,1,0:T(8,128)(2,1)} %collective-permute-done.6, bf16[128,2048]{1,0:T(8,128)(2,1)} %collective-permute-done.5, bf16[128,2048]{1,0:T(8,128)(2,1)} %collective-permute-done.4, bf16[128,2048]{1,0:T(8,128)(2,1)} %collective-permute-done.3, ...), kind=kOutput, calls=%fused_computation.17 | convolution fusion | flops 546308096 | bytes 5505028 | tf_op jit(solution)/shard_map/dot_general | solution.py:60
  135.9 1.5 collective-permute-start.7
  137.4 18.4 %collective-permute-done.15 = bf16[2,2,64,2048]{3,2,1,0:T(8,128)(2,1)S(1)} collective-permute-done((bf16[2,2,64,2048]{3,2,1,0:T(8,128)(2,1)S(1)}, bf16[2,2,64,2048]{3,2,1,0:T(8,128)(2,1)S(1)}, u32[]{:S(2)}, u32[]{:S(2)}) %collective-permute-start.15) | collective-permute-done | bytes 1048608 | tf_op jit(solution)/shard_map/ppermute | solution.py:16
  155.8 2.1 %convolution_add_fusion = f32[2,2,64,2048]{3,2,1,0:T(8,128)S(1)} fusion(bf16[2,2,64,2048]{3,2,1,0:T(8,128)(2,1)S(1)} %collective-permute-done.15, bf16[128,2048]{1,0:T(8,128)(2,1)} %collective-permute-done.14, bf16[128,2048]{1,0:T(8,128)(2,1)} %collective-permute-done.13, bf16[128,2048]{1,0:T(8,128)(2,1)} %collective-permute-done.12, ...), kind=kOutput, calls=%fused_computation.16 | convolution fusion | flops 546308096 | bytes 5505028 | tf_op jit(solution)/shard_map/dot_general | solution.py:60
  157.9 1.2 collective-permute-start.16
  159.3 2.9 %collective-permute-start.8 = (bf16[64,2048]{1,0:T(8,128)(2,1)S(1)}, bf16[64,2048]{1,0:T(8,128)(2,1)S(1)}, u32[]{:S(2)}, u32[]{:S(2)}) collective-permute-start(bf16[64,2048]{1,0:T(8,128)(2,1)S(1)} %fusion.33), channel_id=1, source_target_pairs={{0,4},{1,5},{2,6},{3,7},{4,0},{5,1},{6,2},{7,3},{8,12},{9,13},{10,... | collective-permute-start | bytes 786440 | tf_op jit(solution)/shard_map/ppermute | solution.py:16
  162.2 15.4 %collective-permute-done.16 = bf16[2,64,2048]{2,1,0:T(8,128)(2,1)S(1)} collective-permute-done((bf16[2,64,2048]{2,1,0:T(8,128)(2,1)S(1)}, bf16[2,64,2048]{2,1,0:T(8,128)(2,1)S(1)}, u32[]{:S(2)}, u32[]{:S(2)}) %collective-permute-start.16) | collective-permute-done | bytes 524320 | tf_op jit(solution)/shard_map/ppermute | solution.py:16
  177.6 0.1 bitcast_add_fusion
  177.7 1.1 collective-permute-start.17
  178.9 0.8 bitcast_add_fusion.3
  179.7 11.9 %collective-permute-done.17 = bf16[64,2048]{1,0:T(8,128)(2,1)S(1)} collective-permute-done((bf16[64,2048]{1,0:T(8,128)(2,1)S(1)}, bf16[64,2048]{1,0:T(8,128)(2,1)S(1)}, u32[]{:S(2)}, u32[]{:S(2)}) %collective-permute-start.17) | collective-permute-done | bytes 262176 | tf_op jit(solution)/shard_map/ppermute | solution.py:16
  191.7 0.8 bitcast_add_fusion.2
  (102 shorter events, 1.8 us)
Async XLA Ops:
  0.6 22.5 %copy-start = (bf16[256,128]{1,0:T(8,128)(2,1)S(1)}, bf16[256,128]{1,0:T(8,128)(2,1)}, u32[]{:S(2)}) copy-start(bf16[256,128]{1,0:T(8,128)(2,1)} %param.10) | copy-start | bytes 196612
  0.6 21.2 %all-to-all-start = ((s32[1,32,32]{2,0,1:T(1,128)}), s32[1,32,32]{2,0,1:T(1,128)S(1)}, u32[]{:S(2)}, u32[]{:S(2)}) async-start(s32[1,32,32]{2,0,1:T(1,128)} %bitcast.157), calls=%async_computation | async-start | bytes 32768 | tf_op jit(solution)/shard_map/all_to_all | solution.py:100
  14.8 6.2 %copy-start.1 = (s32[1,2048]{1,0:T(1,128)S(1)}, s32[1,2048]{1,0:T(1,128)}, u32[]{:S(2)}) copy-start(s32[1,2048]{1,0:T(1,128)} %param.15) | copy-start | bytes 24580
  14.8 6.9 %copy-start.3 = (bf16[2048]{0:T(1024)(128)(2,1)S(1)}, bf16[2048]{0:T(1024)(128)(2,1)}, u32[]{:S(2)}) copy-start(bf16[2048]{0:T(1024)(128)(2,1)} %param.19) | copy-start | bytes 12292
  27.5 16.5 %all-to-all-start.1 = ((bf16[32,1,32,128]{3,2,1,0:T(8,128)(2,1)}), bf16[32,1,32,128]{3,2,1,0:T(8,128)(2,1)S(1)}, u32[]{:S(2)}, u32[]{:S(2)}) async-start(bf16[32,1,32,128]{3,2,1,0:T(8,128)(2,1)} %bitcast.15), calls=%async_computation.1 | async-start | bytes 524288 | tf_op jit(solution)/shard_map/all_to_all | solution.py:104
  33.6 18.5 %copy-start.5 = (f32[2048,1]{0,1:T(1,128)}, f32[2048,1]{0,1:T(1,128)S(1)}, u32[]{:S(2)}) copy-start(f32[2048,1]{0,1:T(1,128)S(1)} %get-tuple-element.12) | copy-start | bytes 24580
  33.6 18.5 %copy-start.7 = (f32[2048,1]{0,1:T(1,128)}, f32[2048,1]{0,1:T(1,128)S(1)}, u32[]{:S(2)}) copy-start(f32[2048,1]{0,1:T(1,128)S(1)} %get-tuple-element.13) | copy-start | bytes 24580
  33.6 18.5 %copy-start.9 = (f32[2048,1]{0,1:T(1,128)}, f32[2048,1]{0,1:T(1,128)S(1)}, u32[]{:S(2)}) copy-start(f32[2048,1]{0,1:T(1,128)S(1)} %get-tuple-element.14) | copy-start | bytes 24580
  33.6 18.5 %copy-start.11 = (f32[2048,1]{0,1:T(1,128)}, f32[2048,1]{0,1:T(1,128)S(1)}, u32[]{:S(2)}) copy-start(f32[2048,1]{0,1:T(1,128)S(1)} %get-tuple-element.15) | copy-start | bytes 24580
  33.6 18.5 %copy-start.13 = (f32[2048,1]{0,1:T(1,128)}, f32[2048,1]{0,1:T(1,128)S(1)}, u32[]{:S(2)}) copy-start(f32[2048,1]{0,1:T(1,128)S(1)} %get-tuple-element.16) | copy-start | bytes 24580
  33.6 18.5 %copy-start.15 = (f32[2048,1]{0,1:T(1,128)}, f32[2048,1]{0,1:T(1,128)S(1)}, u32[]{:S(2)}) copy-start(f32[2048,1]{0,1:T(1,128)S(1)} %get-tuple-element.17) | copy-start | bytes 24580
  33.6 18.5 %copy-start.16 = (f32[2048,1]{0,1:T(1,128)}, f32[2048,1]{0,1:T(1,128)S(1)}, u32[]{:S(2)}) copy-start(f32[2048,1]{0,1:T(1,128)S(1)} %get-tuple-element.18) | copy-start | bytes 24580
  33.6 18.5 %copy-start.17 = (f32[2048,1]{0,1:T(1,128)}, f32[2048,1]{0,1:T(1,128)S(1)}, u32[]{:S(2)}) copy-start(f32[2048,1]{0,1:T(1,128)S(1)} %get-tuple-element.19) | copy-start | bytes 24580
  52.3 11.3 %slice-start = ((s8[8388608]{0:T(1024)(128)(4,1)}), s8[4194304]{0:T(1024)(128)(4,1)S(1)}, s32[]{:S(2)}) async-start(s8[8388608]{0:T(1024)(128)(4,1)} %bitcast.177), calls=%async_computation.3 | async-start | bytes 8388608
  57.3 5.0 %copy-start.18 = (s32[128]{0:T(128)S(1)}, s32[128]{0:T(128)}, u32[]{:S(2)}) copy-start(s32[128]{0:T(128)} %param.16) | copy-start | bytes 1540
  57.3 6.4 %slice-start.1 = ((s8[8388608]{0:T(1024)(128)(4,1)}), s8[4194304]{0:T(1024)(128)(4,1)S(1)}, s32[]{:S(2)}) async-start(s8[8388608]{0:T(1024)(128)(4,1)} %bitcast.177), calls=%async_computation.4 | async-start | bytes 8388608
  66.6 15.0 %collective-permute-start.4 = (bf16[128,2048]{1,0:T(8,128)(2,1)S(1)}, bf16[128,2048]{1,0:T(8,128)(2,1)}, u32[]{:S(2)}, u32[]{:S(2)}) collective-permute-start(bf16[128,2048]{1,0:T(8,128)(2,1)S(1)} %fusion.14), channel_id=1, source_target_pairs={{0,1},{1,0},{2,3},{3,2},{4,5},{5,4},{6,7},{7,6},{8,9},{9,8},{10,11... | collective-permute-start | bytes 1572872 | tf_op jit(solution)/shard_map/ppermute | solution.py:16
  67.7 33.3 %collective-permute-start.3 = (bf16[128,2048]{1,0:T(8,128)(2,1)S(1)}, bf16[128,2048]{1,0:T(8,128)(2,1)}, u32[]{:S(2)}, u32[]{:S(2)}) collective-permute-start(bf16[128,2048]{1,0:T(8,128)(2,1)S(1)} %fusion.14), channel_id=1, source_target_pairs={{0,8},{1,9},{2,10},{3,11},{4,12},{5,13},{6,14},{7,15},{8,0},{9,1},... | collective-permute-start | bytes 1572872 | tf_op jit(solution)/shard_map/ppermute | solution.py:16
  68.0 33.5 %collective-permute-start.13 = (bf16[128,2048]{1,0:T(8,128)(2,1)S(1)}, bf16[128,2048]{1,0:T(8,128)(2,1)}, u32[]{:S(2)}, u32[]{:S(2)}) collective-permute-start(bf16[128,2048]{1,0:T(8,128)(2,1)S(1)} %get-tuple-element.35), channel_id=1, source_target_pairs={{0,1},{1,0},{2,3},{3,2},{4,5},{5,4},{6,7},{7,6},{8,9},{9,8},{10,11... | collective-permute-start | bytes 1572872 | tf_op jit(solution)/shard_map/ppermute | solution.py:16
  69.1 24.9 %collective-permute-start.2 = (bf16[2,4,64,128]{3,2,1,0:T(8,128)(2,1)S(1)}, bf16[2,4,64,128]{3,2,1,0:T(8,128)(2,1)S(1)}, u32[]{:S(2)}, u32[]{:S(2)}) collective-permute-start(bf16[2,4,64,128]{3,2,1,0:T(8,128)(2,1)S(1)} %get-tuple-element.9), channel_id=1, source_target_pairs={{0,9},{1,8},{2,11},{3,10},{4,13},{5,12},{6,15},{7,14},{8,1},{9,0},... | collective-permute-start | bytes 393224 | tf_op jit(solution)/shard_map/ppermute | solution.py:16
  70.0 29.1 %collective-permute-start.1 = (bf16[2,4,64,128]{3,2,1,0:T(8,128)(2,1)S(1)}, bf16[2,4,64,128]{3,2,1,0:T(8,128)(2,1)S(1)}, u32[]{:S(2)}, u32[]{:S(2)}) collective-permute-start(bf16[2,4,64,128]{3,2,1,0:T(8,128)(2,1)S(1)} %get-tuple-element.10), channel_id=1, source_target_pairs={{0,1},{1,0},{2,3},{3,2},{4,5},{5,4},{6,7},{7,6},{8,9},{9,8},{10,11... | collective-permute-start | bytes 393224 | tf_op jit(solution)/shard_map/ppermute | solution.py:16
  71.4 10.3 %copy-start.4 = (f32[32,32]{1,0:T(8,128)S(1)}, f32[32,32]{1,0:T(8,128)}, u32[]{:S(2)}) copy-start(f32[32,32]{1,0:T(8,128)} %add_convert_fusion.12) | copy-start | bytes 12292
  71.4 10.3 %copy-start.6 = (f32[2048,1]{0,1:T(1,128)S(1)}, f32[2048,1]{0,1:T(1,128)}, u32[]{:S(2)}) copy-start(f32[2048,1]{0,1:T(1,128)} %copy-done.5) | copy-start | bytes 24580
  71.4 10.2 %copy-start.8 = (f32[2048,1]{0,1:T(1,128)S(1)}, f32[2048,1]{0,1:T(1,128)}, u32[]{:S(2)}) copy-start(f32[2048,1]{0,1:T(1,128)} %copy-done.7) | copy-start | bytes 24580
  71.4 10.2 %copy-start.10 = (f32[2048,1]{0,1:T(1,128)S(1)}, f32[2048,1]{0,1:T(1,128)}, u32[]{:S(2)}) copy-start(f32[2048,1]{0,1:T(1,128)} %copy-done.9) | copy-start | bytes 24580
  71.4 10.2 %copy-start.12 = (f32[2048,1]{0,1:T(1,128)S(1)}, f32[2048,1]{0,1:T(1,128)}, u32[]{:S(2)}) copy-start(f32[2048,1]{0,1:T(1,128)} %copy-done.11) | copy-start | bytes 24580
  71.4 10.2 %copy-start.14 = (f32[2048,1]{0,1:T(1,128)S(1)}, f32[2048,1]{0,1:T(1,128)}, u32[]{:S(2)}) copy-start(f32[2048,1]{0,1:T(1,128)} %copy-done.13) | copy-start | bytes 24580
  78.2 11.2 %copy-start.2 = (bf16[2048]{0:T(1024)(128)(2,1)S(1)}, bf16[2048]{0:T(1024)(128)(2,1)}, u32[]{:S(2)}) copy-start(bf16[2048]{0:T(1024)(128)(2,1)} %get-tuple-element.34) | copy-start | bytes 12292
  81.6 19.9 %collective-permute-start.5 = (bf16[128,2048]{1,0:T(8,128)(2,1)}, bf16[128,2048]{1,0:T(8,128)(2,1)}, u32[]{:S(2)}, u32[]{:S(2)}) collective-permute-start(bf16[128,2048]{1,0:T(8,128)(2,1)} %collective-permute-done.4), channel_id=1, source_target_pairs={{0,8},{1,9},{2,10},{3,11},{4,12},{5,13},{6,14},{7,15},{8,0},{9,1},... | collective-permute-start | bytes 1572872 | tf_op jit(solution)/shard_map/ppermute | solution.py:16
  94.1 5.2 %collective-permute-start = (bf16[2,4,64,128]{3,2,1,0:T(8,128)(2,1)S(1)}, bf16[2,4,64,128]{3,2,1,0:T(8,128)(2,1)S(1)}, u32[]{:S(2)}, u32[]{:S(2)}) collective-permute-start(bf16[2,4,64,128]{3,2,1,0:T(8,128)(2,1)S(1)} %get-tuple-element.11), channel_id=1, source_target_pairs={{0,8},{1,9},{2,10},{3,11},{4,12},{5,13},{6,14},{7,15},{8,0},{9,1},... | collective-permute-start | bytes 393224 | tf_op jit(solution)/shard_map/ppermute | solution.py:16
  96.4 14.8 %all-to-all-start.2 = ((bf16[1,32,33,128]{3,2,0,1:T(8,128)(2,1)}), bf16[1,32,33,128]{3,2,0,1:T(8,128)(2,1)S(1)}, u32[]{:S(2)}, u32[]{:S(2)}) async-start(bf16[1,32,33,128]{3,2,0,1:T(8,128)(2,1)} %maximum_bitcast_fusion.6), calls=%async_computation.2 | async-start | bytes 655360 | tf_op jit(solution)/shard_map/all_to_all | solution.py:167
  99.1 12.2 %collective-permute-start.12 = (bf16[128,2048]{1,0:T(8,128)(2,1)S(1)}, bf16[128,2048]{1,0:T(8,128)(2,1)}, u32[]{:S(2)}, u32[]{:S(2)}) collective-permute-start(bf16[128,2048]{1,0:T(8,128)(2,1)S(1)} %get-tuple-element.35), channel_id=1, source_target_pairs={{0,8},{1,9},{2,10},{3,11},{4,12},{5,13},{6,14},{7,15},{8,0},{9,1},... | collective-permute-start | bytes 1572872 | tf_op jit(solution)/shard_map/ppermute | solution.py:16
  99.3 7.9 %collective-permute-start.11 = (bf16[2,4,64,128]{3,2,1,0:T(8,128)(2,1)S(1)}, bf16[2,4,64,128]{3,2,1,0:T(8,128)(2,1)S(1)}, u32[]{:S(2)}, u32[]{:S(2)}) collective-permute-start(bf16[2,4,64,128]{3,2,1,0:T(8,128)(2,1)S(1)} %get-tuple-element.5), channel_id=1, source_target_pairs={{0,9},{1,8},{2,11},{3,10},{4,13},{5,12},{6,15},{7,14},{8,1},{9,0},... | collective-permute-start | bytes 393224 | tf_op jit(solution)/shard_map/ppermute | solution.py:16
  101.0 10.0 %collective-permute-start.10 = (bf16[2,4,64,128]{3,2,1,0:T(8,128)(2,1)S(1)}, bf16[2,4,64,128]{3,2,1,0:T(8,128)(2,1)S(1)}, u32[]{:S(2)}, u32[]{:S(2)}) collective-permute-start(bf16[2,4,64,128]{3,2,1,0:T(8,128)(2,1)S(1)} %get-tuple-element.6), channel_id=1, source_target_pairs={{0,1},{1,0},{2,3},{3,2},{4,5},{5,4},{6,7},{7,6},{8,9},{9,8},{10,11... | collective-permute-start | bytes 393224 | tf_op jit(solution)/shard_map/ppermute | solution.py:16
  101.5 9.5 %collective-permute-start.9 = (bf16[2,4,64,128]{3,2,1,0:T(8,128)(2,1)S(1)}, bf16[2,4,64,128]{3,2,1,0:T(8,128)(2,1)S(1)}, u32[]{:S(2)}, u32[]{:S(2)}) collective-permute-start(bf16[2,4,64,128]{3,2,1,0:T(8,128)(2,1)S(1)} %get-tuple-element.7), channel_id=1, source_target_pairs={{0,8},{1,9},{2,10},{3,11},{4,12},{5,13},{6,14},{7,15},{8,0},{9,1},... | collective-permute-start | bytes 393224 | tf_op jit(solution)/shard_map/ppermute | solution.py:16
  101.5 9.8 %collective-permute-start.14 = (bf16[128,2048]{1,0:T(8,128)(2,1)}, bf16[128,2048]{1,0:T(8,128)(2,1)}, u32[]{:S(2)}, u32[]{:S(2)}) collective-permute-start(bf16[128,2048]{1,0:T(8,128)(2,1)} %collective-permute-done.13), channel_id=1, source_target_pairs={{0,8},{1,9},{2,10},{3,11},{4,12},{5,13},{6,14},{7,15},{8,0},{9,1},... | collective-permute-start | bytes 1572872 | tf_op jit(solution)/shard_map/ppermute | solution.py:16
  107.2 26.2 %collective-permute-start.6 = (bf16[2,2,64,2048]{3,2,1,0:T(8,128)(2,1)}, bf16[2,2,64,2048]{3,2,1,0:T(8,128)(2,1)}, u32[]{:S(2)}, u32[]{:S(2)}) collective-permute-start(bf16[2,2,64,2048]{3,2,1,0:T(8,128)(2,1)} %convolution_convert_fusion.1), channel_id=1, source_target_pairs={{0,16},{1,17},{2,18},{3,19},{4,20},{5,21},{6,22},{7,23},{8,24},{9,... | collective-permute-start | bytes 3145736 | tf_op jit(solution)/shard_map/ppermute | solution.py:16
  113.4 42.4 %collective-permute-start.15 = (bf16[2,2,64,2048]{3,2,1,0:T(8,128)(2,1)S(1)}, bf16[2,2,64,2048]{3,2,1,0:T(8,128)(2,1)S(1)}, u32[]{:S(2)}, u32[]{:S(2)}) collective-permute-start(bf16[2,2,64,2048]{3,2,1,0:T(8,128)(2,1)S(1)} %convolution_convert_fusion), channel_id=1, source_target_pairs={{0,16},{1,17},{2,18},{3,19},{4,20},{5,21},{6,22},{7,23},{8,24},{9,... | collective-permute-start | bytes 3145736 | tf_op jit(solution)/shard_map/ppermute | solution.py:16
  135.9 23.2 %collective-permute-start.7 = (bf16[2,64,2048]{2,1,0:T(8,128)(2,1)S(1)}, bf16[2,64,2048]{2,1,0:T(8,128)(2,1)S(1)}, u32[]{:S(2)}, u32[]{:S(2)}) collective-permute-start(bf16[2,64,2048]{2,1,0:T(8,128)(2,1)S(1)} %fusion.29), channel_id=1, source_target_pairs={{0,2},{1,3},{2,0},{3,1},{4,6},{5,7},{6,4},{7,5},{8,10},{9,11},{10,... | collective-permute-start | bytes 1572872 | tf_op jit(solution)/shard_map/ppermute | solution.py:16
  157.9 19.6 %collective-permute-start.16 = (bf16[2,64,2048]{2,1,0:T(8,128)(2,1)S(1)}, bf16[2,64,2048]{2,1,0:T(8,128)(2,1)S(1)}, u32[]{:S(2)}, u32[]{:S(2)}) collective-permute-start(bf16[2,64,2048]{2,1,0:T(8,128)(2,1)S(1)} %fusion.30), channel_id=1, source_target_pairs={{0,2},{1,3},{2,0},{3,1},{4,6},{5,7},{6,4},{7,5},{8,10},{9,11},{10,... | collective-permute-start | bytes 1572872 | tf_op jit(solution)/shard_map/ppermute | solution.py:16
  159.3 19.6 %collective-permute-start.8 = (bf16[64,2048]{1,0:T(8,128)(2,1)S(1)}, bf16[64,2048]{1,0:T(8,128)(2,1)S(1)}, u32[]{:S(2)}, u32[]{:S(2)}) collective-permute-start(bf16[64,2048]{1,0:T(8,128)(2,1)S(1)} %fusion.33), channel_id=1, source_target_pairs={{0,4},{1,5},{2,6},{3,7},{4,0},{5,1},{6,2},{7,3},{8,12},{9,13},{10,... | collective-permute-start | bytes 786440 | tf_op jit(solution)/shard_map/ppermute | solution.py:16
  177.7 13.9 %collective-permute-start.17 = (bf16[64,2048]{1,0:T(8,128)(2,1)S(1)}, bf16[64,2048]{1,0:T(8,128)(2,1)S(1)}, u32[]{:S(2)}, u32[]{:S(2)}) collective-permute-start(bf16[64,2048]{1,0:T(8,128)(2,1)S(1)} %fusion.34), channel_id=1, source_target_pairs={{0,4},{1,5},{2,6},{3,7},{4,0},{5,1},{6,2},{7,3},{8,12},{9,13},{10,... | collective-permute-start | bytes 786440 | tf_op jit(solution)/shard_map/ppermute | solution.py:16

commit v2 on v1

--- a/solution.py
+++ b/solution.py
@@ -20,39 +20,48 @@
     return lax.dynamic_index_in_dim(value, index, dim, keepdims=False)
 
 
-def gather_left(left, core_bit):
-    peers = lax.axis_size(AXES)
-    me = lax.axis_index(AXES)
+def group(core_bit, side):
+    core, near = 1 << core_bit, 1 << side
+    return core, near, (lax.axis_index(AXES) >> core_bit) & 1, (lax.axis_index(AXES) >> side) & 1
+
+
+def gather_left(left, core_bit, side):
+    peers = lax.axis_size(AXES)
+    core, near, my_core, my_near = group(core_bit, side)
     samples, total = left.shape
-    core, low = (me >> core_bit) & 1, me & 1
+    bits = peers.bit_length() - 1
+    one, two = bits - 1 - max(core_bit, side), bits - 1 - min(core_bit, side)
     split = left.T.reshape(
-        peers >> (core_bit + 1), 2, 1 << (core_bit - 1), 2, total // peers, samples
-    )
-
-    def quarter(c, x):
-        return pick(pick(split, 3, x), 1, c)
+        1 << one, 2, 1 << (two - one - 1), 2, 1 << (bits - 1 - two), total // peers, samples
+    )
+
+    def quarter(c, n):
+        outer, inner = (c, n) if core_bit > side else (n, c)
+        return pick(pick(split, 3, inner), 1, outer)
 
     return jnp.concatenate(
         [
-            quarter(core, low),
-            swap(quarter(1 - core, low), 1 << core_bit),
-            swap(quarter(core, 1 - low), 1),
-            swap(quarter(1 - core, 1 - low), 1 + (1 << core_bit)),
+            quarter(my_core, my_near),
+            swap(quarter(1 - my_core, my_near), core),
+            swap(quarter(my_core, 1 - my_near), near),
+            swap(quarter(1 - my_core, 1 - my_near), core + near),
         ],
         axis=-1,
     )
 
 
-def reduce_gradient(left, right, core_bit):
+def gather_right(right, core_bit, side):
+    core, near, _, _ = group(core_bit, side)
+    across = swap(right, near)
+    return jnp.concatenate([right, swap(right, core), across, swap(across, core)], axis=0)
+
+
+def halving(left, right, core_bit, side):
     peers = lax.axis_size(AXES)
     me = lax.axis_index(AXES)
-    across = swap(right, 1)
-    right = jnp.concatenate(
-        [right, swap(right, 1 << core_bit), across, swap(across, 1 << core_bit)], axis=0
-    )
-    high = [b for b in range(peers.bit_length() - 2, core_bit, -1)]
-    mid = [b for b in range(core_bit - 1, 0, -1)]
-    bits = high + mid
+    bits = [b for b in range(peers.bit_length() - 2, -1, -1) if b not in (core_bit, side)]
+    order = [b for b in (0,) + tuple(range(core_bit + 1, peers.bit_length() - 1)) if b in bits]
+    order = order + [b for b in bits[::-1] if b not in order]
     rows, depth = left.shape[-2:]
     left = left.reshape([2] * len(bits) + [rows, depth])
 
@@ -60,20 +69,27 @@
         out = jnp.dot(part.reshape(-1, depth), right, preferred_element_type=jnp.float32)
         return out.reshape(part.shape[:-1] + (right.shape[1],))
 
-    current = None
-    for bit in high[::-1] + mid[::-1]:
-        dim = bits.index(bit)
-        mine = (me >> bit) & 1
-        if current is None:
-            sent = product(pick(left, dim, 1 - mine)).astype(jnp.bfloat16)
-            got = swap(sent, 1 << bit)
-            kept = product(pick(left, dim, mine))
-        else:
-            got = swap(pick(current, dim, 1 - mine).astype(jnp.bfloat16), 1 << bit)
-            kept = pick(current, dim, mine)
-        current = kept + got.astype(jnp.float32)
-        bits.remove(bit)
-    return current.reshape(rows, -1)
+    dim = bits.index(order[0])
+    mine = (me >> order[0]) & 1
+    sent = product(pick(left, dim, 1 - mine)).astype(jnp.bfloat16)
+
+    def rest(sent):
+        left_bits = list(bits)
+        current = None
+        for bit in order:
+            dim = left_bits.index(bit)
+            mine = (me >> bit) & 1
+            if current is None:
+                got = swap(sent, 1 << bit)
+                kept = product(pick(left, dim, mine))
+            else:
+                got = swap(pick(current, dim, 1 - mine).astype(jnp.bfloat16), 1 << bit)
+                kept = pick(current, dim, mine)
+            current = kept + got.astype(jnp.float32)
+            left_bits.remove(bit)
+        return current.reshape(rows, -1)
+
+    return sent, rest
 
 
 def per_device(
@@ -101,9 +117,6 @@
         request_rows, AXES, split_axis=1, concat_axis=0, tiled=True
     ).reshape(peers * slots)
     served = table[incoming]
-    fetched = lax.all_to_all(
-        served.reshape(peers, 1, slots, width), AXES, split_axis=0, concat_axis=1, tiled=True
-    ).reshape(peers * slots, width)
 
     owner_ids = jnp.arange(peers, dtype=jnp.int32)
     match = lookup_owner[:, None] == owner_ids[None, :]
@@ -118,6 +131,10 @@
         [owner_pad[j : j + looks] for j in range(most)]
         + [slot_pad[j : j + looks] for j in range(most)]
     )
+    served, shifted = lax.optimization_barrier((served, shifted))
+    fetched = lax.all_to_all(
+        served.reshape(peers, 1, slots, width), AXES, split_axis=0, concat_axis=1, tiled=True
+    ).reshape(peers * slots, width)
     first = (starts[:, None] == jnp.arange(looks, dtype=jnp.int32)[None, :]).astype(jnp.bfloat16)
     found = lax.dot_general(
         first, shifted, (((1,), (1,)), ((), ())), preferred_element_type=jnp.float32
@@ -129,14 +146,14 @@
     counted = jnp.zeros((bags, peers * slots), jnp.float32)
     for j in range(most):
         counted = counted + (code[:, j : j + 1] == names).astype(jnp.float32)
-    counted = counted.astype(jnp.bfloat16)
+    counted = lax.optimization_barrier(counted.astype(jnp.bfloat16))
 
     pooled = jnp.dot(counted, fetched, preferred_element_type=jnp.float32)
     x = (pooled * scale).astype(jnp.bfloat16).reshape(samples, inputs)
-    x_left = gather_left(x, core_bit)
+    x_left = gather_left(x, core_bit, core_bit + 1)
     z1 = jnp.dot(x, w_first, preferred_element_type=jnp.float32)
     h1 = jax.nn.silu(z1).astype(jnp.bfloat16)
-    h1_left = gather_left(h1, core_bit)
+    h1_left = gather_left(h1, core_bit, 0)
     z2 = jnp.dot(h1, w_second, preferred_element_type=jnp.float32)
     h2 = jax.nn.silu(z2).astype(jnp.bfloat16)
     logit = jnp.dot(h2, w_out, preferred_element_type=jnp.float32)
@@ -145,12 +162,17 @@
         jnp.bfloat16
     )
     head_term = jnp.sum(dlogit[:, None] * h2.astype(jnp.float32), axis=0)
-    grad_second = reduce_gradient(h1_left, dz2, core_bit)
+    dz2_all = gather_right(dz2, core_bit, 0)
     back_two = lax.dot_general(
         dz2, w_second, (((1,), (1,)), ((), ())), preferred_element_type=jnp.float32
     )
     dz1 = (back_two * silu_slope(z1)).astype(jnp.bfloat16)
-    grad_first = reduce_gradient(x_left, dz1, core_bit)
+    dz1_all = gather_right(dz1, core_bit, core_bit + 1)
+    sent, second = halving(h1_left, dz2_all, core_bit, 0)
+    sent, dz1 = lax.optimization_barrier((sent, dz1))
+    grad_second = second(sent)
+    sent, first = halving(x_left, dz1_all, core_bit, core_bit + 1)
+    grad_first = first(sent)
     back_one = lax.dot_general(
         dz1, w_first, (((1,), (1,)), ((), ())), preferred_element_type=jnp.float32
     )

time: 193 us -> 184 us (0.953)
  waiting for transfers between devices: 85.2 us -> 70.7 us
  other arithmetic: 11.1 us -> 18.8 us
  matrix products: 52.2 us -> 48.6 us
    convert_element_type x0 -> x1, other arithmetic: none -> 8.02 us  [per_device(): counted = lax.optimization_barrier(counted.astype(jnp.bfloat16))]
    all_to_all x1, waiting for transfers between devices: 10.3 us -> 2.63 us  [per_device(): lax.all_to_all(served.reshape(peers, 1, slots, width), AXES, split_axis=0...]
    ppermute x18, waiting for transfers between devices: 74.7 us -> 68.1 us  [swap(): return lax.ppermute(value, AXES, [(d, d ^ mask) for d in range(peers)])]
    dot_general x1, matrix products: 8.07 us -> 3.64 us  [per_device(): pooled = jnp.dot(counted, fetched, preferred_element_type=jnp.float32)]
    dot_general x1, matrix products: 7.72 us -> 3.66 us  [per_device(): lax.dot_general(counted, bag_grad, (((0,), (0,)), ((), ())), preferred_el...]
    dot_general x1, matrix products: 2.99 us -> 6.57 us  [per_device(): lax.dot_general(dz2, w_second, (((1,), (1,)), ((), ())), preferred_elemen...]
  transfers between devices with their start and end apart: 21 -> 21, of which waited for: 10 -> 11; matrix products, arithmetic and copies ran while one was open for 22% -> 27% of each run, Pallas kernels for 0% -> 0%
where the time goes in v2:
time: 184 us; the launch traced here: 183 us
  waiting for transfers between devices  70.7 us (38%)
  matrix products  48.6 us (26%)
  starting transfers between devices  34.5 us (19%)
  other arithmetic  18.8 us (10%)
  local copies, waits for them, and re-layouts  9.03 us (5%)
    ppermute x18, waiting for transfers between devices, swap(): return lax.ppermute(value, AXES, [(d, d ^ mask) for d in range(peers)])  68.1 us
    ppermute x18, starting transfers between devices, swap(): return lax.ppermute(value, AXES, [(d, d ^ mask) for d in range(peers)])  17.7 us
    dot_general x4, matrix products, product(): jnp.dot(part.reshape(-1, depth), right, preferred_element_type=jnp.float32)  11 us
    convert_element_type x1, other arithmetic, per_device(): counted = lax.optimization_barrier(counted.astype(jnp.bfloat16))  8.02 us
    all_to_all x1, starting transfers between devices, per_device(): lax.all_to_all(request_rows, AXES, split_axis=1, concat_axis=0, tiled=True)  7.3 us
    dot_general x1, matrix products, per_device(): lax.dot_general(dz2, w_second, (((1,), (1,)), ((), ())), preferred_elemen...  6.57 us
    dot_general x1, matrix products, per_device(): lax.dot_general(dz1, w_first, (((1,), (1,)), ((), ())), preferred_element...  6.45 us
    dot_general x1, matrix products, per_device(): lax.dot_general(first, shifted, (((1,), (1,)), ((), ())), preferred_eleme...  6.2 us
  transfers between devices with their start and end apart: 21, of which 11 were waited for; matrix products, arithmetic and copies ran while one was open for 27% of the time, Pallas kernels for 0%

profile of v2, /device:TPU:0, one launch (start us, length us, event | category | flops | bytes accessed | tf_op | source)
XLA Modules:
  0.0 182.9 jit_solution(5334309832315970014)
XLA Ops:
  0.6 7.3 %all-to-all-start = ((s32[1,32,32]{2,0,1:T(1,128)}), s32[1,32,32]{2,0,1:T(1,128)S(1)}, u32[]{:S(2)}, u32[]{:S(2)}) async-start(s32[1,32,32]{2,0,1:T(1,128)} %bitcast.170), calls=%async_computation | async-start | bytes 32768 | tf_op jit(solution)/shard_map/all_to_all | solution.py:116
  8.0 0.7 slice.99
  8.7 0.9 select_reduce_fusion
  9.6 0.9 fusion.32
  10.7 1.0 reduce-window.9
  11.9 0.7 convert_rsqrt_fusion
  12.6 0.8 bitcast_subtract_fusion
  13.4 0.7 reshape.235
  14.1 0.7 convert_element_type.172
  15.1 0.4 stack.67
  15.5 0.5 broadcast.55
  16.0 0.7 reduce.12
  16.8 4.3 %gather_fusion = bf16[1024,128]{1,0:T(8,128)(2,1)} fusion(bf16[256,128]{1,0:T(8,128)(2,1)S(1)} %copy-done, s32[1024]{0:T(1024)S(1)} %broadcast_clamp_fusion), kind=kCustom, calls=%fused_computation | custom fusion | bytes 528384 | tf_op jit(solution)/shard_map/gather | solution.py:119
  21.1 6.2 %fusion = f32[2048,16]{0,1:T(8,128)S(1)} fusion(bf16[16,4096]{1,0:T(8,128)(2,1)S(1)} %stack.67, s32[2048]{0:T(1024)S(1)} %bitcast_subtract_fusion), kind=kOutput, calls=%fused_computation.2 | convolution fusion | flops 276824064 | bytes 270336 | tf_op jit(solution)/shard_map/dot_general | solution.py:139
  27.4 5.8 %all-to-all-start.1 = ((bf16[32,1,32,128]{3,2,1,0:T(8,128)(2,1)}), bf16[32,1,32,128]{3,2,1,0:T(8,128)(2,1)S(1)}, u32[]{:S(2)}, u32[]{:S(2)}) async-start(bf16[32,1,32,128]{3,2,1,0:T(8,128)(2,1)} %bitcast.15), calls=%async_computation.1 | async-start | bytes 524288 | tf_op jit(solution)/shard_map/all_to_all | solution.py:135
  33.3 8.0 %add_convert_fusion = bf16[2048,1024]{0,1:T(8,128)(2,1)} fusion(f32[2048]{0:T(1024)S(1)} %bitcast.163, f32[2048]{0:T(1024)S(1)} %bitcast.164, f32[2048]{0:T(1024)S(1)} %bitcast.165, f32[2048]{0:T(1024)S(1)} %bitcast.166, f32[2048]{0:T(1024)S(1)} %bitcast.167, f32[2048]{0:T(1024)S(1)} %bitcast.168, f32[2048]{0:T(1024)S(1)} %bitcast.169, ...), kind=kLoop, calls=%fused_computation.4 | loop fusion | flops 50331648 | bytes 4263936 | tf_op jit(solution)/shard_map/convert_element_type | solution.py:149
  41.3 2.6 %all-to-all-done.1 = bf16[32,1,32,128]{3,2,1,0:T(8,128)(2,1)S(1)} async-done(((bf16[32,1,32,128]{3,2,1,0:T(8,128)(2,1)}), bf16[32,1,32,128]{3,2,1,0:T(8,128)(2,1)S(1)}, u32[]{:S(2)}, u32[]{:S(2)}) %all-to-all-start.1) | async-done | bytes 262176 | tf_op jit(solution)/shard_map/all_to_all | solution.py:135
  43.9 3.6 %fusion.2 = bf16[2048,128]{1,0:T(8,128)(2,1)S(1)} fusion(bf16[2048,1024]{0,1:T(8,128)(2,1)} %add_convert_fusion, bf16[1024,128]{1,0:T(8,128)(2,1)S(1)} %bitcast.150, f32[2048]{0:T(1024)S(1)} %convert_rsqrt_fusion), kind=kOutput, calls=%fused_computation.12 | convolution fusion | flops 537395200 | bytes 4988928 | tf_op jit(solution)/shard_map/dot_general | solution.py:151
  47.6 0.2 reshape.222
  47.8 4.7 %fusion.14 = (bf16[2048,128]{0,1:T(8,128)(2,1)S(1)}, f32[128,2048]{1,0:T(8,128)S(1)}) fusion(bf16[128,2048]{1,0:T(8,128)(2,1)S(1)} %reshape.222, bf16[2048,2048]{1,0:T(8,128)(2,1)} %param.17), kind=kOutput, calls=%fused_computation.41 | convolution fusion | flops 1075052544 | bytes 10485760 | tf_op jit(solution)/shard_map/dot_general | solution.py:154
  52.6 5.2 %multiply_convert_fusion.1 = (bf16[128,2048]{1,0:T(8,128)(2,1)S(1)}, f32[128,2048]{1,0:T(8,128)S(1)}) fusion(bf16[2048,2048]{1,0:T(8,128)(2,1)} %param.18, f32[128,2048]{1,0:T(8,128)S(1)} %get-tuple-element.47), kind=kOutput, calls=%fused_computation.37 | convolution fusion | flops 1076363264 | bytes 11010048 | tf_op jit(solution)/shard_map/dot_general | solution.py:157
  57.8 0.2 fusion.10
  58.0 0.5 multiply_reduce_fusion
  58.6 1.1 collective-permute-start.13
  59.7 0.3 copy.32
  59.9 6.6 %fusion.3 = bf16[128,2048]{1,0:T(8,128)(2,1)S(1)} fusion(bf16[128,2048]{1,0:T(8,128)(2,1)S(1)} %get-tuple-element.43, bf16[2048,2048]{1,0:T(8,128)(2,1)} %param.18, f32[128,2048]{1,0:T(8,128)} %copy-done.3), kind=kOutput, calls=%fused_computation.13 | convolution fusion | flops 1076101120 | bytes 10485760 | tf_op jit(solution)/shard_map/dot_general | solution.py:166
  66.5 0.6 collective-permute-start.4
  67.1 5.2 %collective-permute-done.13 = bf16[128,2048]{1,0:T(8,128)(2,1)} collective-permute-done((bf16[128,2048]{1,0:T(8,128)(2,1)S(1)}, bf16[128,2048]{1,0:T(8,128)(2,1)}, u32[]{:S(2)}, u32[]{:S(2)}) %collective-permute-start.13) | collective-permute-done | bytes 524320 | tf_op jit(solution)/shard_map/ppermute | solution.py:16
  72.4 0.6 collective-permute-start.9
  73.1 1.4 collective-permute-start.10
  74.6 0.9 collective-permute-start.11
  75.6 0.3 copy.31
  75.9 3.6 %collective-permute-done.10 = bf16[2,4,1,64,128]{4,3,1,0,2:T(8,128)(2,1)S(1)} collective-permute-done((bf16[2,4,1,64,128]{4,3,1,0,2:T(8,128)(2,1)S(1)}, bf16[2,4,1,64,128]{4,3,1,0,2:T(8,128)(2,1)S(1)}, u32[]{:S(2)}, u32[]{:S(2)}) %collective-permute-start.10) | collective-permute-done | bytes 131104 | tf_op jit(solution)/shard_map/ppermute | solution.py:16
  79.5 1.0 collective-permute-done.11
  80.6 0.8 collective-permute-start
  81.3 1.0 pad_maximum_fusion.1
  82.4 3.0 %convolution_convert_fusion = bf16[2,2,64,2048]{3,2,1,0:T(8,128)(2,1)} fusion(bf16[128,2048]{1,0:T(8,128)(2,1)} %collective-permute-done.14, bf16[128,2048]{1,0:T(8,128)(2,1)} %collective-permute-done.13, bf16[128,2048]{1,0:T(8,128)(2,1)} %collective-permute-done.12, bf16[128,2048]{1,0:T(8,128)(2,1)S(1)} %get-tuple-element.43, ...), kind=kOutput, calls=%fused_computation.7 | convolution fusion | flops 545783808 | bytes 3407876 | tf_op jit(solution)/shard_map/dot_general | solution.py:69
  85.4 0.3 mul.97
  85.8 6.4 %fusion.4 = bf16[128,2048]{1,0:T(8,128)(2,1)S(1)} fusion(bf16[128,2048]{1,0:T(8,128)(2,1)S(1)} %fusion.3, bf16[2048,2048]{1,0:T(8,128)(2,1)} %param.17, f32[16,8,16,128]{3,2,1,0:T(8,128)S(1)} %bitcast.142), kind=kOutput, calls=%fused_computation.14 | convolution fusion | flops 1074266112 | bytes 10485760 | tf_op jit(solution)/shard_map/dot_general | solution.py:176
  92.2 0.2 reshape.239
  92.5 3.7 %fusion.5 = bf16[1,32,32,128]{3,2,1,0:T(8,128)(2,1)S(1)} fusion(bf16[32,32,2048]{2,1,0:T(8,128)(2,1)} %bitcast.143, bf16[2048,128,1]{1,0,2:T(8,128)(2,1)S(1)} %reshape.239), kind=kOutput, calls=%fused_computation.18 | convolution fusion | flops 537001984 | bytes 4980736 | tf_op jit(solution)/shard_map/dot_general | solution.py:180
  96.1 0.8 maximum_bitcast_fusion.6
  96.9 3.7 %all-to-all-start.2 = ((bf16[1,32,33,128]{3,2,0,1:T(8,128)(2,1)}), bf16[1,32,33,128]{3,2,0,1:T(8,128)(2,1)S(1)}, u32[]{:S(2)}, u32[]{:S(2)}) async-start(bf16[1,32,33,128]{3,2,0,1:T(8,128)(2,1)} %maximum_bitcast_fusion.6), calls=%async_computation.2 | async-start | bytes 655360 | tf_op jit(solution)/shard_map/all_to_all | solution.py:189
  100.6 1.8 %collective-permute-start.1 = (bf16[1,1,8,64,128]{4,3,2,1,0:T(8,128)(2,1)S(1)}, bf16[1,1,8,64,128]{4,3,2,1,0:T(8,128)(2,1)S(1)}, u32[]{:S(2)}, u32[]{:S(2)}) collective-permute-start(bf16[1,1,8,64,128]{4,3,2,1,0:T(8,128)(2,1)S(1)} %get-tuple-element.18), channel_id=1, source_target_pairs={{0,16},{1,17},{2,18},{3,19},{4,20},{5,21},{6,22},{7,23},{8,24},{9,... | collective-permute-start | bytes 393224 | tf_op jit(solution)/shard_map/ppermute | solution.py:16
  102.4 1.5 collective-permute-start.15
  104.0 5.8 %collective-permute-done.1 = bf16[1,1,8,64,128]{4,3,2,1,0:T(8,128)(2,1)S(1)} collective-permute-done((bf16[1,1,8,64,128]{4,3,2,1,0:T(8,128)(2,1)S(1)}, bf16[1,1,8,64,128]{4,3,2,1,0:T(8,128)(2,1)S(1)}, u32[]{:S(2)}, u32[]{:S(2)}) %collective-permute-start.1) | collective-permute-done | bytes 131104 | tf_op jit(solution)/shard_map/ppermute | solution.py:16
  109.8 2.4 %collective-permute-done.2 = bf16[1,1,8,64,128]{4,3,2,1,0:T(8,128)(2,1)S(1)} collective-permute-done((bf16[1,1,8,64,128]{4,3,2,1,0:T(8,128)(2,1)S(1)}, bf16[1,1,8,64,128]{4,3,2,1,0:T(8,128)(2,1)S(1)}, u32[]{:S(2)}, u32[]{:S(2)}) %collective-permute-start.2) | collective-permute-done | bytes 131104 | tf_op jit(solution)/shard_map/ppermute | solution.py:16
  112.3 3.1 %convolution_convert_fusion.1 = bf16[2,2,64,2048]{3,2,1,0:T(8,128)(2,1)} fusion(bf16[128,2048]{1,0:T(8,128)(2,1)} %collective-permute-done.5, bf16[128,2048]{1,0:T(8,128)(2,1)} %collective-permute-done.4, bf16[128,2048]{1,0:T(8,128)(2,1)} %collective-permute-done.3, bf16[128,2048]{1,0:T(8,128)(2,1)S(1)} %fusion.3, ...), kind=kOutput, calls=%fused_computation.8 | convolution fusion | flops 545783808 | bytes 3407876 | tf_op jit(solution)/shard_map/dot_general | solution.py:69
  115.4 1.7 collective-permute-start.6
  117.2 0.5 slice_bitcast_fusion
  117.7 1.0 fusion.15
  118.6 16.6 %collective-permute-done.15 = bf16[2,2,64,2048]{3,2,1,0:T(8,128)(2,1)} collective-permute-done((bf16[2,2,64,2048]{3,2,1,0:T(8,128)(2,1)}, bf16[2,2,64,2048]{3,2,1,0:T(8,128)(2,1)}, u32[]{:S(2)}, u32[]{:S(2)}) %collective-permute-start.15) | collective-permute-done | bytes 1048608 | tf_op jit(solution)/shard_map/ppermute | solution.py:16
  135.2 2.4 %convolution_add_fusion = f32[2,2,64,2048]{3,2,1,0:T(8,128)S(1)} fusion(bf16[2,2,64,2048]{3,2,1,0:T(8,128)(2,1)} %collective-permute-done.15, bf16[128,2048]{1,0:T(8,128)(2,1)} %collective-permute-done.14, bf16[128,2048]{1,0:T(8,128)(2,1)} %collective-permute-done.13, bf16[128,2048]{1,0:T(8,128)(2,1)} %collective-permute-done.12, ...), kind=kOutput, calls=%fused_computation.5 | convolution fusion | flops 546308096 | bytes 5505028 | tf_op jit(solution)/shard_map/dot_general | solution.py:69
  137.8 1.5 collective-permute-start.16
  139.3 2.1 %collective-permute-done.6 = bf16[2,2,64,2048]{3,2,1,0:T(8,128)(2,1)} collective-permute-done((bf16[2,2,64,2048]{3,2,1,0:T(8,128)(2,1)}, bf16[2,2,64,2048]{3,2,1,0:T(8,128)(2,1)}, u32[]{:S(2)}, u32[]{:S(2)}) %collective-permute-start.6) | collective-permute-done | bytes 1048608 | tf_op jit(solution)/shard_map/ppermute | solution.py:16
  141.4 2.4 %convolution_add_fusion.1 = f32[2,2,64,2048]{3,2,1,0:T(8,128)S(1)} fusion(bf16[2,2,64,2048]{3,2,1,0:T(8,128)(2,1)} %collective-permute-done.6, bf16[128,2048]{1,0:T(8,128)(2,1)} %collective-permute-done.5, bf16[128,2048]{1,0:T(8,128)(2,1)} %collective-permute-done.4, bf16[128,2048]{1,0:T(8,128)(2,1)} %collective-permute-done.3, ...), kind=kOutput, calls=%fused_computation.6 | convolution fusion | flops 546308096 | bytes 5505028 | tf_op jit(solution)/shard_map/dot_general | solution.py:69
  143.9 1.6 collective-permute-start.7
  145.5 7.1 %collective-permute-done.16 = bf16[2,64,2048]{2,1,0:T(8,128)(2,1)S(1)} collective-permute-done((bf16[2,64,2048]{2,1,0:T(8,128)(2,1)S(1)}, bf16[2,64,2048]{2,1,0:T(8,128)(2,1)S(1)}, u32[]{:S(2)}, u32[]{:S(2)}) %collective-permute-start.16) | collective-permute-done | bytes 524320 | tf_op jit(solution)/shard_map/ppermute | solution.py:16
  152.8 2.5 %collective-permute-start.17 = (bf16[64,2048]{1,0:T(8,128)(2,1)S(1)}, bf16[64,2048]{1,0:T(8,128)(2,1)S(1)}, u32[]{:S(2)}, u32[]{:S(2)}) collective-permute-start(bf16[64,2048]{1,0:T(8,128)(2,1)S(1)} %fusion.22), channel_id=1, source_target_pairs={{0,4},{1,5},{2,6},{3,7},{4,0},{5,1},{6,2},{7,3},{8,12},{9,13},{10,... | collective-permute-start | bytes 786440 | tf_op jit(solution)/shard_map/ppermute | solution.py:16
  155.3 13.0 %collective-permute-done.7 = bf16[2,64,2048]{2,1,0:T(8,128)(2,1)S(1)} collective-permute-done((bf16[2,64,2048]{2,1,0:T(8,128)(2,1)S(1)}, bf16[2,64,2048]{2,1,0:T(8,128)(2,1)S(1)}, u32[]{:S(2)}, u32[]{:S(2)}) %collective-permute-start.7) | collective-permute-done | bytes 524320 | tf_op jit(solution)/shard_map/ppermute | solution.py:16
  168.4 1.6 collective-permute-start.8
  170.0 0.8 bitcast_add_fusion.2
  170.8 11.2 %collective-permute-done.8 = bf16[64,2048]{1,0:T(8,128)(2,1)S(1)} collective-permute-done((bf16[64,2048]{1,0:T(8,128)(2,1)S(1)}, bf16[64,2048]{1,0:T(8,128)(2,1)S(1)}, u32[]{:S(2)}, u32[]{:S(2)}) %collective-permute-start.8) | collective-permute-done | bytes 262176 | tf_op jit(solution)/shard_map/ppermute | solution.py:16
  182.1 0.8 bitcast_add_fusion.3
  (67 shorter events, 1.8 us)
Async XLA Ops:
  0.6 16.2 %copy-start = (bf16[256,128]{1,0:T(8,128)(2,1)S(1)}, bf16[256,128]{1,0:T(8,128)(2,1)}, u32[]{:S(2)}) copy-start(bf16[256,128]{1,0:T(8,128)(2,1)} %param.10) | copy-start | bytes 196612
  0.6 14.9 %all-to-all-start = ((s32[1,32,32]{2,0,1:T(1,128)}), s32[1,32,32]{2,0,1:T(1,128)S(1)}, u32[]{:S(2)}, u32[]{:S(2)}) async-start(s32[1,32,32]{2,0,1:T(1,128)} %bitcast.170), calls=%async_computation | async-start | bytes 32768 | tf_op jit(solution)/shard_map/all_to_all | solution.py:116
  21.1 6.2 %copy-start.1 = (s32[1,2048]{1,0:T(1,128)S(1)}, s32[1,2048]{1,0:T(1,128)}, u32[]{:S(2)}) copy-start(s32[1,2048]{1,0:T(1,128)} %param.15) | copy-start | bytes 24580
  27.4 16.5 %all-to-all-start.1 = ((bf16[32,1,32,128]{3,2,1,0:T(8,128)(2,1)}), bf16[32,1,32,128]{3,2,1,0:T(8,128)(2,1)S(1)}, u32[]{:S(2)}, u32[]{:S(2)}) async-start(bf16[32,1,32,128]{3,2,1,0:T(8,128)(2,1)} %bitcast.15), calls=%async_computation.1 | async-start | bytes 524288 | tf_op jit(solution)/shard_map/all_to_all | solution.py:135
  52.6 5.2 %copy-start.3 = (f32[128,2048]{1,0:T(8,128)}, f32[128,2048]{1,0:T(8,128)S(1)}, u32[]{:S(2)}) copy-start(f32[128,2048]{1,0:T(8,128)S(1)} %get-tuple-element.47) | copy-start | bytes 3145732
  52.6 5.2 %copy-start.2 = (s32[128]{0:T(128)S(1)}, s32[128]{0:T(128)}, u32[]{:S(2)}) copy-start(s32[128]{0:T(128)} %param.16) | copy-start | bytes 1540
  58.6 13.8 %collective-permute-start.13 = (bf16[128,2048]{1,0:T(8,128)(2,1)S(1)}, bf16[128,2048]{1,0:T(8,128)(2,1)}, u32[]{:S(2)}, u32[]{:S(2)}) collective-permute-start(bf16[128,2048]{1,0:T(8,128)(2,1)S(1)} %get-tuple-element.43), channel_id=1, source_target_pairs={{0,1},{1,0},{2,3},{3,2},{4,5},{5,4},{6,7},{7,6},{8,9},{9,8},{10,11... | collective-permute-start | bytes 1572872 | tf_op jit(solution)/shard_map/ppermute | solution.py:16
  59.7 22.7 %collective-permute-start.12 = (bf16[128,2048]{1,0:T(8,128)(2,1)S(1)}, bf16[128,2048]{1,0:T(8,128)(2,1)}, u32[]{:S(2)}, u32[]{:S(2)}) collective-permute-start(bf16[128,2048]{1,0:T(8,128)(2,1)S(1)} %get-tuple-element.43), channel_id=1, source_target_pairs={{0,8},{1,9},{2,10},{3,11},{4,12},{5,13},{6,14},{7,15},{8,0},{9,1},... | collective-permute-start | bytes 1572872 | tf_op jit(solution)/shard_map/ppermute | solution.py:16
  66.5 15.8 %collective-permute-start.4 = (bf16[128,2048]{1,0:T(8,128)(2,1)S(1)}, bf16[128,2048]{1,0:T(8,128)(2,1)}, u32[]{:S(2)}, u32[]{:S(2)}) collective-permute-start(bf16[128,2048]{1,0:T(8,128)(2,1)S(1)} %fusion.3), channel_id=1, source_target_pairs={{0,16},{1,17},{2,18},{3,19},{4,20},{5,21},{6,22},{7,23},{8,24},{9,... | collective-permute-start | bytes 1572872 | tf_op jit(solution)/shard_map/ppermute | solution.py:16
  72.3 10.1 %collective-permute-start.14 = (bf16[128,2048]{1,0:T(8,128)(2,1)}, bf16[128,2048]{1,0:T(8,128)(2,1)}, u32[]{:S(2)}, u32[]{:S(2)}) collective-permute-start(bf16[128,2048]{1,0:T(8,128)(2,1)} %collective-permute-done.13), channel_id=1, source_target_pairs={{0,8},{1,9},{2,10},{3,11},{4,12},{5,13},{6,14},{7,15},{8,0},{9,1},... | collective-permute-start | bytes 1572872 | tf_op jit(solution)/shard_map/ppermute | solution.py:16
  72.4 2.2 %collective-permute-start.9 = (bf16[2,4,1,64,128]{4,3,1,0,2:T(8,128)(2,1)S(1)}, bf16[2,4,1,64,128]{4,3,1,0,2:T(8,128)(2,1)S(1)}, u32[]{:S(2)}, u32[]{:S(2)}) collective-permute-start(bf16[2,4,1,64,128]{4,3,1,0,2:T(8,128)(2,1)S(1)} %get-tuple-element.15), channel_id=1, source_target_pairs={{0,8},{1,9},{2,10},{3,11},{4,12},{5,13},{6,14},{7,15},{8,0},{9,1},... | collective-permute-start | bytes 393224 | tf_op jit(solution)/shard_map/ppermute | solution.py:16
  73.1 6.4 %collective-permute-start.10 = (bf16[2,4,1,64,128]{4,3,1,0,2:T(8,128)(2,1)S(1)}, bf16[2,4,1,64,128]{4,3,1,0,2:T(8,128)(2,1)S(1)}, u32[]{:S(2)}, u32[]{:S(2)}) collective-permute-start(bf16[2,4,1,64,128]{4,3,1,0,2:T(8,128)(2,1)S(1)} %get-tuple-element.14), channel_id=1, source_target_pairs={{0,1},{1,0},{2,3},{3,2},{4,5},{5,4},{6,7},{7,6},{8,9},{9,8},{10,11... | collective-permute-start | bytes 393224 | tf_op jit(solution)/shard_map/ppermute | solution.py:16
  74.6 5.9 %collective-permute-start.11 = (bf16[2,4,1,64,128]{4,3,1,0,2:T(8,128)(2,1)S(1)}, bf16[2,4,1,64,128]{4,3,1,0,2:T(8,128)(2,1)}, u32[]{:S(2)}, u32[]{:S(2)}) collective-permute-start(bf16[2,4,1,64,128]{4,3,1,0,2:T(8,128)(2,1)S(1)} %get-tuple-element.13), channel_id=1, source_target_pairs={{0,9},{1,8},{2,11},{3,10},{4,13},{5,12},{6,15},{7,14},{8,1},{9,0},... | collective-permute-start | bytes 393224 | tf_op jit(solution)/shard_map/ppermute | solution.py:16
  79.5 32.7 %collective-permute-start.3 = (bf16[128,2048]{1,0:T(8,128)(2,1)S(1)}, bf16[128,2048]{1,0:T(8,128)(2,1)}, u32[]{:S(2)}, u32[]{:S(2)}) collective-permute-start(bf16[128,2048]{1,0:T(8,128)(2,1)S(1)} %fusion.3), channel_id=1, source_target_pairs={{0,8},{1,9},{2,10},{3,11},{4,12},{5,13},{6,14},{7,15},{8,0},{9,1},... | collective-permute-start | bytes 1572872 | tf_op jit(solution)/shard_map/ppermute | solution.py:16
  80.6 21.9 %collective-permute-start = (bf16[1,1,8,64,128]{4,3,2,1,0:T(8,128)(2,1)S(1)}, bf16[1,1,8,64,128]{4,3,2,1,0:T(8,128)(2,1)S(1)}, u32[]{:S(2)}, u32[]{:S(2)}) collective-permute-start(bf16[1,1,8,64,128]{4,3,2,1,0:T(8,128)(2,1)S(1)} %get-tuple-element.19), channel_id=1, source_target_pairs={{0,8},{1,9},{2,10},{3,11},{4,12},{5,13},{6,14},{7,15},{8,0},{9,1},... | collective-permute-start | bytes 393224 | tf_op jit(solution)/shard_map/ppermute | solution.py:16
  82.3 30.0 %collective-permute-start.5 = (bf16[128,2048]{1,0:T(8,128)(2,1)}, bf16[128,2048]{1,0:T(8,128)(2,1)}, u32[]{:S(2)}, u32[]{:S(2)}) collective-permute-start(bf16[128,2048]{1,0:T(8,128)(2,1)} %collective-permute-done.4), channel_id=1, source_target_pairs={{0,8},{1,9},{2,10},{3,11},{4,12},{5,13},{6,14},{7,15},{8,0},{9,1},... | collective-permute-start | bytes 1572872 | tf_op jit(solution)/shard_map/ppermute | solution.py:16
  96.9 20.2 %all-to-all-start.2 = ((bf16[1,32,33,128]{3,2,0,1:T(8,128)(2,1)}), bf16[1,32,33,128]{3,2,0,1:T(8,128)(2,1)S(1)}, u32[]{:S(2)}, u32[]{:S(2)}) async-start(bf16[1,32,33,128]{3,2,0,1:T(8,128)(2,1)} %maximum_bitcast_fusion.6), calls=%async_computation.2 | async-start | bytes 655360 | tf_op jit(solution)/shard_map/all_to_all | solution.py:189
  100.6 9.2 %collective-permute-start.1 = (bf16[1,1,8,64,128]{4,3,2,1,0:T(8,128)(2,1)S(1)}, bf16[1,1,8,64,128]{4,3,2,1,0:T(8,128)(2,1)S(1)}, u32[]{:S(2)}, u32[]{:S(2)}) collective-permute-start(bf16[1,1,8,64,128]{4,3,2,1,0:T(8,128)(2,1)S(1)} %get-tuple-element.18), channel_id=1, source_target_pairs={{0,16},{1,17},{2,18},{3,19},{4,20},{5,21},{6,22},{7,23},{8,24},{9,... | collective-permute-start | bytes 393224 | tf_op jit(solution)/shard_map/ppermute | solution.py:16
  102.4 9.7 %collective-permute-start.2 = (bf16[1,1,8,64,128]{4,3,2,1,0:T(8,128)(2,1)S(1)}, bf16[1,1,8,64,128]{4,3,2,1,0:T(8,128)(2,1)S(1)}, u32[]{:S(2)}, u32[]{:S(2)}) collective-permute-start(bf16[1,1,8,64,128]{4,3,2,1,0:T(8,128)(2,1)S(1)} %get-tuple-element.17), channel_id=1, source_target_pairs={{0,24},{1,25},{2,26},{3,27},{4,28},{5,29},{6,30},{7,31},{8,16},{9,... | collective-permute-start | bytes 393224 | tf_op jit(solution)/shard_map/ppermute | solution.py:16
  102.4 32.8 %collective-permute-start.15 = (bf16[2,2,64,2048]{3,2,1,0:T(8,128)(2,1)}, bf16[2,2,64,2048]{3,2,1,0:T(8,128)(2,1)}, u32[]{:S(2)}, u32[]{:S(2)}) collective-permute-start(bf16[2,2,64,2048]{3,2,1,0:T(8,128)(2,1)} %convolution_convert_fusion), channel_id=1, source_target_pairs={{0,16},{1,17},{2,18},{3,19},{4,20},{5,21},{6,22},{7,23},{8,24},{9,... | collective-permute-start | bytes 3145736 | tf_op jit(solution)/shard_map/ppermute | solution.py:16
  115.4 26.1 %collective-permute-start.6 = (bf16[2,2,64,2048]{3,2,1,0:T(8,128)(2,1)}, bf16[2,2,64,2048]{3,2,1,0:T(8,128)(2,1)}, u32[]{:S(2)}, u32[]{:S(2)}) collective-permute-start(bf16[2,2,64,2048]{3,2,1,0:T(8,128)(2,1)} %convolution_convert_fusion.1), channel_id=1, source_target_pairs={{0,1},{1,0},{2,3},{3,2},{4,5},{5,4},{6,7},{7,6},{8,9},{9,8},{10,11... | collective-permute-start | bytes 3145736 | tf_op jit(solution)/shard_map/ppermute | solution.py:16
  137.8 14.9 %collective-permute-start.16 = (bf16[2,64,2048]{2,1,0:T(8,128)(2,1)S(1)}, bf16[2,64,2048]{2,1,0:T(8,128)(2,1)S(1)}, u32[]{:S(2)}, u32[]{:S(2)}) collective-permute-start(bf16[2,64,2048]{2,1,0:T(8,128)(2,1)S(1)} %fusion.18), channel_id=1, source_target_pairs={{0,2},{1,3},{2,0},{3,1},{4,6},{5,7},{6,4},{7,5},{8,10},{9,11},{10,... | collective-permute-start | bytes 1572872 | tf_op jit(solution)/shard_map/ppermute | solution.py:16
  143.9 24.3 %collective-permute-start.7 = (bf16[2,64,2048]{2,1,0:T(8,128)(2,1)S(1)}, bf16[2,64,2048]{2,1,0:T(8,128)(2,1)S(1)}, u32[]{:S(2)}, u32[]{:S(2)}) collective-permute-start(bf16[2,64,2048]{2,1,0:T(8,128)(2,1)S(1)} %fusion.17), channel_id=1, source_target_pairs={{0,2},{1,3},{2,0},{3,1},{4,6},{5,7},{6,4},{7,5},{8,10},{9,11},{10,... | collective-permute-start | bytes 1572872 | tf_op jit(solution)/shard_map/ppermute | solution.py:16
  152.8 17.2 %collective-permute-start.17 = (bf16[64,2048]{1,0:T(8,128)(2,1)S(1)}, bf16[64,2048]{1,0:T(8,128)(2,1)S(1)}, u32[]{:S(2)}, u32[]{:S(2)}) collective-permute-start(bf16[64,2048]{1,0:T(8,128)(2,1)S(1)} %fusion.22), channel_id=1, source_target_pairs={{0,4},{1,5},{2,6},{3,7},{4,0},{5,1},{6,2},{7,3},{8,12},{9,13},{10,... | collective-permute-start | bytes 786440 | tf_op jit(solution)/shard_map/ppermute | solution.py:16
  168.4 13.6 %collective-permute-start.8 = (bf16[64,2048]{1,0:T(8,128)(2,1)S(1)}, bf16[64,2048]{1,0:T(8,128)(2,1)S(1)}, u32[]{:S(2)}, u32[]{:S(2)}) collective-permute-start(bf16[64,2048]{1,0:T(8,128)(2,1)S(1)} %fusion.21), channel_id=1, source_target_pairs={{0,4},{1,5},{2,6},{3,7},{4,0},{5,1},{6,2},{7,3},{8,12},{9,13},{10,... | collective-permute-start | bytes 786440 | tf_op jit(solution)/shard_map/ppermute | solution.py:16

commit v3 on v2

--- a/solution.py
+++ b/solution.py
@@ -1,6 +1,10 @@
+import functools
+
 import jax
 import jax.numpy as jnp
 from jax import lax
+from jax.experimental import pallas as pl
+from jax.experimental.pallas import tpu as pltpu
 from jax.sharding import PartitionSpec as P
 
 AXES = ("gx", "gy")
@@ -56,40 +60,127 @@
     return jnp.concatenate([right, swap(right, core), across, swap(across, core)], axis=0)
 
 
-def halving(left, right, core_bit, side):
+def orders(peers, core_bit):
+    bits = [b for b in range(peers.bit_length() - 1) if b != core_bit]
+    high = [b for b in bits if b > core_bit]
+    low = [b for b in bits if 0 < b < core_bit]
+    return (high + low, [0] + high[1:] + low)
+
+
+def arrange(left, core_bit, side, order):
     peers = lax.axis_size(AXES)
-    me = lax.axis_index(AXES)
     bits = [b for b in range(peers.bit_length() - 2, -1, -1) if b not in (core_bit, side)]
-    order = [b for b in (0,) + tuple(range(core_bit + 1, peers.bit_length() - 1)) if b in bits]
-    order = order + [b for b in bits[::-1] if b not in order]
     rows, depth = left.shape[-2:]
     left = left.reshape([2] * len(bits) + [rows, depth])
-
-    def product(part):
-        out = jnp.dot(part.reshape(-1, depth), right, preferred_element_type=jnp.float32)
-        return out.reshape(part.shape[:-1] + (right.shape[1],))
-
-    dim = bits.index(order[0])
-    mine = (me >> order[0]) & 1
-    sent = product(pick(left, dim, 1 - mine)).astype(jnp.bfloat16)
-
-    def rest(sent):
-        left_bits = list(bits)
-        current = None
-        for bit in order:
-            dim = left_bits.index(bit)
-            mine = (me >> bit) & 1
-            if current is None:
-                got = swap(sent, 1 << bit)
-                kept = product(pick(left, dim, mine))
-            else:
-                got = swap(pick(current, dim, 1 - mine).astype(jnp.bfloat16), 1 << bit)
-                kept = pick(current, dim, mine)
-            current = kept + got.astype(jnp.float32)
-            left_bits.remove(bit)
-        return current.reshape(rows, -1)
-
-    return sent, rest
+    left = left.transpose([bits.index(b) for b in order] + [len(bits), len(bits) + 1])
+    return left.reshape(-1, depth)
+
+
+def flip(bit, core_bit):
+    gx, gy = lax.axis_index("gx"), lax.axis_index("gy")
+    if bit < core_bit:
+        mine = (gy // (1 << bit)) % 2
+        return mine, (gx, gy + (1 - 2 * mine) * (1 << bit))
+    up = 1 << (bit - core_bit)
+    mine = (gx // up) % 2
+    return mine, (gx + (1 - 2 * mine) * up, gy)
+
+
+def halving_kernel(core_bit, both, l2, r2, l1, r1, o2, o1, *scratch):
+    send_sem, recv_sem = scratch[-2:]
+    steps = len(both[0])
+    per = 3 * steps
+    lefts, rights, outs = (l2, l1), (r2, r1), (o2, o1)
+    accs = [scratch[g * per : g * per + steps] for g in range(2)]
+    sends = [scratch[g * per + steps : g * per + 2 * steps] for g in range(2)]
+    recvs = [scratch[g * per + 2 * steps : g * per + 3 * steps] for g in range(2)]
+    chunks, _, wide = sends[0][0].shape
+    union = sorted(set(both[0]) | set(both[1]))
+    barrier = pltpu.get_barrier_semaphore()
+    for bit in union:
+        pl.semaphore_signal(
+            barrier, inc=1, device_id=flip(bit, core_bit)[1], device_id_type=pl.DeviceIdType.MESH
+        )
+    pl.semaphore_wait(barrier, len(union))
+
+    def copy(g, k, c):
+        return pltpu.make_async_remote_copy(
+            src_ref=sends[g][k].at[c],
+            dst_ref=recvs[g][k].at[c],
+            send_sem=send_sem.at[g, k, c],
+            recv_sem=recv_sem.at[g, k, c],
+            device_id=flip(both[g][k], core_bit)[1],
+            device_id_type=pl.DeviceIdType.MESH,
+        )
+
+    def product(g, c, part):
+        half = lefts[g].shape[0] // 2
+        rows = lefts[g][pl.ds(pl.multiple_of(part * half, half), half), :]
+        return jnp.dot(
+            rows, rights[g][:, c * wide : (c + 1) * wide], preferred_element_type=jnp.float32
+        )
+
+    for c in range(chunks):
+        for g in range(2):
+            mine = flip(both[g][0], core_bit)[0]
+            sends[g][0][c] = product(g, c, 1 - mine).astype(jnp.bfloat16)
+            copy(g, 0, c).start()
+    for c in range(chunks):
+        for g in range(2):
+            mine = flip(both[g][0], core_bit)[0]
+            accs[g][0][c] = product(g, c, mine)
+    for k in range(1, steps + 1):
+        for c in range(chunks):
+            for g in range(2):
+                copy(g, k - 1, c).wait_recv()
+                if k == steps:
+                    outs[g][:, c * wide : (c + 1) * wide] = accs[g][k - 1][c] + recvs[g][k - 1][
+                        c
+                    ].astype(jnp.float32)
+                    continue
+                mine = flip(both[g][k], core_bit)[0]
+                half = sends[g][k].shape[1]
+
+                def total(part):
+                    at = pl.ds(pl.multiple_of(part * half, half), half)
+                    return accs[g][k - 1][c, at, :] + recvs[g][k - 1][c, at, :].astype(jnp.float32)
+
+                sends[g][k][c] = total(1 - mine).astype(jnp.bfloat16)
+                copy(g, k, c).start()
+                accs[g][k][c] = total(mine)
+    for k in range(steps):
+        for c in range(chunks):
+            for g in range(2):
+                copy(g, k, c).wait_send()
+
+
+def halve(l2, r2, l1, r1, core_bit, both):
+    steps, chunks = len(both[0]), 2
+    rows, depth = l2.shape
+    columns = r2.shape[1]
+    wide = columns // chunks
+    scratch = []
+    for _ in range(2):
+        for kind in (jnp.float32, jnp.bfloat16, jnp.bfloat16):
+            scratch += [pltpu.VMEM((chunks, rows >> (k + 1), wide), kind) for k in range(steps)]
+    scratch += [pltpu.SemaphoreType.DMA((2, steps, chunks))] * 2
+    whole = pl.BlockSpec(memory_space=pltpu.VMEM)
+    out = jax.ShapeDtypeStruct((rows >> steps, columns), jnp.float32)
+    return pl.pallas_call(
+        functools.partial(halving_kernel, core_bit, both),
+        out_shape=(out, out),
+        in_specs=[whole] * 4,
+        out_specs=(whole, whole),
+        scratch_shapes=scratch,
+        compiler_params=pltpu.CompilerParams(
+            collective_id=0, has_side_effects=True, vmem_limit_bytes=40 << 20
+        ),
+        cost_estimate=pl.CostEstimate(
+            flops=4 * rows * depth * columns,
+            bytes_accessed=2 * (rows * depth + depth * columns) * 2,
+            transcendentals=0,
+        ),
+    )(l2, r2, l1, r1)
 
 
 def per_device(
@@ -150,10 +241,12 @@
 
     pooled = jnp.dot(counted, fetched, preferred_element_type=jnp.float32)
     x = (pooled * scale).astype(jnp.bfloat16).reshape(samples, inputs)
-    x_left = gather_left(x, core_bit, core_bit + 1)
+    both = orders(peers, core_bit)
+    x_left = arrange(gather_left(x, core_bit, core_bit + 1), core_bit, core_bit + 1, both[1])
     z1 = jnp.dot(x, w_first, preferred_element_type=jnp.float32)
     h1 = jax.nn.silu(z1).astype(jnp.bfloat16)
-    h1_left = gather_left(h1, core_bit, 0)
+    x_left, h1 = lax.optimization_barrier((x_left, h1))
+    h1_left = arrange(gather_left(h1, core_bit, 0), core_bit, 0, both[0])
     z2 = jnp.dot(h1, w_second, preferred_element_type=jnp.float32)
     h2 = jax.nn.silu(z2).astype(jnp.bfloat16)
     logit = jnp.dot(h2, w_out, preferred_element_type=jnp.float32)
@@ -161,6 +254,7 @@
     dz2 = (dlogit[:, None] * w_out.astype(jnp.float32)[None, :] * silu_slope(z2)).astype(
         jnp.bfloat16
     )
+    h1_left, dz2 = lax.optimization_barrier((h1_left, dz2))
     head_term = jnp.sum(dlogit[:, None] * h2.astype(jnp.float32), axis=0)
     dz2_all = gather_right(dz2, core_bit, 0)
     back_two = lax.dot_general(
@@ -168,11 +262,7 @@
     )
     dz1 = (back_two * silu_slope(z1)).astype(jnp.bfloat16)
     dz1_all = gather_right(dz1, core_bit, core_bit + 1)
-    sent, second = halving(h1_left, dz2_all, core_bit, 0)
-    sent, dz1 = lax.optimization_barrier((sent, dz1))
-    grad_second = second(sent)
-    sent, first = halving(x_left, dz1_all, core_bit, core_bit + 1)
-    grad_first = first(sent)
+    grad_second, grad_first = halve(h1_left, dz2_all, x_left, dz1_all, core_bit, both)
     back_one = lax.dot_general(
         dz1, w_first, (((1,), (1,)), ((), ())), preferred_element_type=jnp.float32
     )

time: 184 us -> 168 us (0.913)
  Pallas kernels: 0 us -> 55.4 us
  waiting for transfers between devices: 70.7 us -> 21.6 us
  matrix products: 48.6 us -> 32.5 us
  starting transfers between devices: 34.5 us -> 22.9 us
  local copies, waits for them, and re-layouts: 9.03 us -> 12.4 us
  other arithmetic: 18.8 us -> 20.8 us
    ppermute x18 -> x12, waiting for transfers between devices: 68.1 us -> 9.81 us  [swap(): return lax.ppermute(value, AXES, [(d, d ^ mask) for d in range(peers)])]
    pallas_call x0 -> x1, Pallas kernels: none -> 55.4 us  [halve(): pl.pallas_call(functools.partial(halving_kernel, core_bit, both), out_sha...]
    ppermute x18 -> x12, starting transfers between devices: 17.7 us -> 6.33 us  [swap(): return lax.ppermute(value, AXES, [(d, d ^ mask) for d in range(peers)])]
    dot_general x4 -> x0, matrix products: 11 us -> none  [product(): jnp.dot(part.reshape(-1, depth), right, preferred_element_type=jnp.float32)]
    all_to_all x1, waiting for transfers between devices: 0.01 us -> 9.13 us  [per_device(): lax.all_to_all(outgoing[None], AXES, split_axis=1, concat_axis=0, tiled=T...]
    dot_general x1, matrix products: 5.2 us -> 1.44 us  [per_device(): z2 = jnp.dot(h1, w_second, preferred_element_type=jnp.float32)]
    dot_general x1, matrix products: 6.45 us -> 3.08 us  [per_device(): lax.dot_general(dz1, w_first, (((1,), (1,)), ((), ())), preferred_element...]
    unnamed x9 -> x17, local copies, waits for them, and re-layouts: 0.72 us -> 2.92 us
  transfers between devices with their start and end apart: 21 -> 15, of which waited for: 11 -> 7; matrix products, arithmetic and copies ran while one was open for 27% -> 22% of each run, Pallas kernels for 0% -> 0%
where the time goes in v3:
time: 168 us; the launch traced here: 167 us
  Pallas kernels  55.4 us (33%)
  matrix products  32.5 us (19%)
  starting transfers between devices  22.9 us (14%)
  waiting for transfers between devices  21.6 us (13%)
  other arithmetic  20.8 us (12%)
  local copies, waits for them, and re-layouts  12.4 us (7%)
    pallas_call x1, Pallas kernels, halve(): pl.pallas_call(functools.partial(halving_kernel, core_bit, both), out_sha...  55.4 us
    ppermute x12, waiting for transfers between devices, swap(): return lax.ppermute(value, AXES, [(d, d ^ mask) for d in range(peers)])  9.81 us
    all_to_all x1, waiting for transfers between devices, per_device(): lax.all_to_all(outgoing[None], AXES, split_axis=1, concat_axis=0, tiled=T...  9.13 us
    convert_element_type x1, other arithmetic, per_device(): counted = lax.optimization_barrier(counted.astype(jnp.bfloat16))  8.02 us
    all_to_all x1, starting transfers between devices, per_device(): lax.all_to_all(request_rows, AXES, split_axis=1, concat_axis=0, tiled=True)  7.3 us
    dot_general x1, matrix products, per_device(): lax.dot_general(dz2, w_second, (((1,), (1,)), ((), ())), preferred_elemen...  6.71 us
    ppermute x12, starting transfers between devices, swap(): return lax.ppermute(value, AXES, [(d, d ^ mask) for d in range(peers)])  6.33 us
    dot_general x1, matrix products, per_device(): lax.dot_general(first, shifted, (((1,), (1,)), ((), ())), preferred_eleme...  6.2 us
  transfers between devices with their start and end apart: 15, of which 7 were waited for; matrix products, arithmetic and copies ran while one was open for 22% of the time, Pallas kernels for 0%

profile of v3, /device:TPU:0, one launch (start us, length us, event | category | flops | bytes accessed | tf_op | source)
XLA Modules:
  0.0 166.7 jit_solution(10477901357201229558)
XLA Ops:
  0.7 7.3 %all-to-all-start = ((s32[1,32,32]{2,0,1:T(1,128)}), s32[1,32,32]{2,0,1:T(1,128)S(1)}, u32[]{:S(2)}, u32[]{:S(2)}) async-start(s32[1,32,32]{2,0,1:T(1,128)} %bitcast.131), calls=%async_computation | async-start | bytes 32768 | tf_op jit(solution)/shard_map/all_to_all | solution.py:207
  8.0 0.7 slice.99
  8.7 0.9 select_reduce_fusion
  9.6 0.9 fusion.14
  10.5 0.1 pad_slice_fusion
  10.6 0.1 pad_slice_fusion.7
  10.7 0.7 rsqrt_reduce_fusion
  11.4 1.0 reduce-window.9
  12.4 0.1 slice.131
  12.5 0.1 slice_reduce_fusion
  12.6 0.7 convert_rsqrt_fusion
  13.3 0.8 bitcast_subtract_fusion
  14.2 1.3 reshape.219
  15.5 1.3 convert_element_type.121
  17.0 0.1 rsqrt.15
  17.1 0.4 stack.67
  17.5 0.5 broadcast.54
  18.1 0.7 reduce.12
  18.7 0.1 reshape.201
  18.9 4.3 %gather_fusion = bf16[1024,128]{1,0:T(8,128)(2,1)} fusion(bf16[256,128]{1,0:T(8,128)(2,1)S(1)} %copy-done, s32[1024]{0:T(1024)S(1)} %broadcast_clamp_fusion), kind=kCustom, calls=%fused_computation | custom fusion | bytes 528384 | tf_op jit(solution)/shard_map/gather | solution.py:210
  23.2 6.2 %fusion = f32[2048,16]{0,1:T(8,128)S(1)} fusion(bf16[16,4096]{1,0:T(8,128)(2,1)S(1)} %stack.67, s32[2048]{0:T(1024)S(1)} %bitcast_subtract_fusion), kind=kOutput, calls=%fused_computation.2 | convolution fusion | flops 276824064 | bytes 270336 | tf_op jit(solution)/shard_map/dot_general | solution.py:230
  29.5 5.8 %all-to-all-start.1 = ((bf16[32,1,32,128]{3,2,1,0:T(8,128)(2,1)}), bf16[32,1,32,128]{3,2,1,0:T(8,128)(2,1)S(1)}, u32[]{:S(2)}, u32[]{:S(2)}) async-start(bf16[32,1,32,128]{3,2,1,0:T(8,128)(2,1)} %bitcast.15), calls=%async_computation.1 | async-start | bytes 524288 | tf_op jit(solution)/shard_map/all_to_all | solution.py:226
  35.3 8.0 %add_convert_fusion = bf16[2048,1024]{0,1:T(8,128)(2,1)} fusion(f32[2048]{0:T(1024)S(1)} %bitcast.124, f32[2048]{0:T(1024)S(1)} %bitcast.125, f32[2048]{0:T(1024)S(1)} %bitcast.126, f32[2048]{0:T(1024)S(1)} %bitcast.127, f32[2048]{0:T(1024)S(1)} %bitcast.128, f32[2048]{0:T(1024)S(1)} %bitcast.129, f32[2048]{0:T(1024)S(1)} %bitcast.130, ...), kind=kLoop, calls=%fused_computation.4 | loop fusion | flops 50331648 | bytes 4263936 | tf_op jit(solution)/shard_map/convert_element_type | solution.py:240
  43.3 2.6 %all-to-all-done.1 = bf16[32,1,32,128]{3,2,1,0:T(8,128)(2,1)S(1)} async-done(((bf16[32,1,32,128]{3,2,1,0:T(8,128)(2,1)}), bf16[32,1,32,128]{3,2,1,0:T(8,128)(2,1)S(1)}, u32[]{:S(2)}, u32[]{:S(2)}) %all-to-all-start.1) | async-done | bytes 262176 | tf_op jit(solution)/shard_map/all_to_all | solution.py:226
  46.0 3.6 %fusion.2 = bf16[2048,128]{1,0:T(8,128)(2,1)S(1)} fusion(bf16[2048,1024]{0,1:T(8,128)(2,1)} %add_convert_fusion, bf16[1024,128]{1,0:T(8,128)(2,1)S(1)} %bitcast.110, f32[2048]{0:T(1024)S(1)} %convert_rsqrt_fusion), kind=kOutput, calls=%fused_computation.8 | convolution fusion | flops 537395200 | bytes 4988928 | tf_op jit(solution)/shard_map/dot_general | solution.py:242
  49.6 0.2 reshape.204
  49.8 0.3 copy.37
  50.2 0.1 collective-permute-start
  50.2 0.9 collective-permute-start.1
  51.2 0.9 collective-permute-start.2
  52.1 6.1 %multiply_convert_fusion.2 = (bf16[128,2048]{1,0:T(8,128)(2,1)S(1)}, f32[128,2048]{1,0:T(8,128)}) fusion(bf16[128,2048]{1,0:T(8,128)(2,1)S(1)} %reshape.204, bf16[2048,2048]{1,0:T(8,128)(2,1)} %param.17), kind=kOutput, calls=%fused_computation.26 | convolution fusion | flops 1075052544 | bytes 10485760 | tf_op jit(solution)/shard_map/dot_general | solution.py:246
  58.2 0.3 collective-permute-done.2
  58.7 1.4 multiply_convert_fusion.1
  60.1 0.3 copy.39
  60.4 0.8 constant_dynamic-slice_fusion
  61.1 0.3 collective-permute-start.3
  61.4 1.1 collective-permute-start.4
  62.5 0.5 collective-permute-start.5
  63.0 0.9 fusion.10
  63.9 1.2 multiply_reduce_fusion
  65.2 0.1 reshape.209
  65.3 0.6 copy.41
  65.9 2.1 %collective-permute-done.4 = bf16[2,4,1,64,128]{4,3,1,0,2:T(8,128)(2,1)S(1)} collective-permute-done((bf16[2,4,1,64,128]{4,3,1,0,2:T(8,128)(2,1)}, bf16[2,4,1,64,128]{4,3,1,0,2:T(8,128)(2,1)S(1)}, u32[]{:S(2)}, u32[]{:S(2)}) %collective-permute-start.4) | collective-permute-done | bytes 131104 | tf_op jit(solution)/shard_map/ppermute | solution.py:20
  68.0 1.4 collective-permute-done.5
  69.5 6.7 %fusion.3 = bf16[128,2048]{1,0:T(8,128)(2,1)S(1)} fusion(bf16[128,2048]{1,0:T(8,128)(2,1)S(1)} %get-tuple-element.16, bf16[2048,2048]{1,0:T(8,128)(2,1)} %param.18, f32[128,2048]{1,0:T(8,128)} %get-tuple-element.53), kind=kOutput, calls=%fused_computation.9 | convolution fusion | flops 1076101120 | bytes 10485760 | tf_op jit(solution)/shard_map/dot_general | solution.py:260
  76.2 0.2 collective-permute-start.10
  76.4 0.3 mul.91
  76.8 3.1 %fusion.4 = bf16[128,2048]{1,0:T(8,128)(2,1)S(1)} fusion(bf16[128,2048]{1,0:T(8,128)(2,1)S(1)} %fusion.3, bf16[2048,2048]{1,0:T(8,128)(2,1)S(1)} %bitcast.100, f32[16,8,16,128]{3,2,1,0:T(8,128)S(1)} %bitcast.101), kind=kOutput, calls=%fused_computation.10 | convolution fusion | flops 1074266112 | bytes 10485760 | tf_op jit(solution)/shard_map/dot_general | solution.py:266
  79.9 0.2 reshape.221
  80.1 3.4 %fusion.5 = bf16[1,32,32,128]{3,2,1,0:T(8,128)(2,1)S(1)} fusion(bf16[32,32,2048]{2,1,0:T(8,128)(2,1)} %bitcast.102, bf16[2048,128,1]{1,0,2:T(8,128)(2,1)S(1)} %reshape.221), kind=kOutput, calls=%fused_computation.14 | convolution fusion | flops 537001984 | bytes 4980736 | tf_op jit(solution)/shard_map/dot_general | solution.py:270
  83.6 0.8 maximum_bitcast_fusion.2
  84.3 3.4 %all-to-all-start.2 = ((bf16[1,32,33,128]{3,2,0,1:T(8,128)(2,1)}), bf16[1,32,33,128]{3,2,0,1:T(8,128)(2,1)S(1)}, u32[]{:S(2)}, u32[]{:S(2)}) async-start(bf16[1,32,33,128]{3,2,0,1:T(8,128)(2,1)} %maximum_bitcast_fusion.2), calls=%async_computation.2 | async-start | bytes 655360 | tf_op jit(solution)/shard_map/all_to_all | solution.py:279
  87.7 1.8 %collective-permute-start.7 = (bf16[128,2048]{1,0:T(8,128)(2,1)S(1)}, bf16[128,2048]{1,0:T(8,128)(2,1)S(1)}, u32[]{:S(2)}, u32[]{:S(2)}) collective-permute-start(bf16[128,2048]{1,0:T(8,128)(2,1)S(1)} %get-tuple-element.16), channel_id=1, source_target_pairs={{0,1},{1,0},{2,3},{3,2},{4,5},{5,4},{6,7},{7,6},{8,9},{9,8},{10,11... | collective-permute-start | bytes 1572872 | tf_op jit(solution)/shard_map/ppermute | solution.py:20
  89.6 0.5 collective-permute-start.6
  90.2 0.6 collective-permute-done.10
  90.7 9.1 %all-to-all-done.2 = bf16[1,32,33,128]{3,2,0,1:T(8,128)(2,1)S(1)} async-done(((bf16[1,32,33,128]{3,2,0,1:T(8,128)(2,1)}), bf16[1,32,33,128]{3,2,0,1:T(8,128)(2,1)S(1)}, u32[]{:S(2)}, u32[]{:S(2)}) %all-to-all-start.2) | async-done | bytes 270368 | tf_op jit(solution)/shard_map/all_to_all | solution.py:279
  99.9 5.4 %collective-permute-done.7 = bf16[128,2048]{1,0:T(8,128)(2,1)S(1)} collective-permute-done((bf16[128,2048]{1,0:T(8,128)(2,1)S(1)}, bf16[128,2048]{1,0:T(8,128)(2,1)S(1)}, u32[]{:S(2)}, u32[]{:S(2)}) %collective-permute-start.7) | collective-permute-done | bytes 524320 | tf_op jit(solution)/shard_map/ppermute | solution.py:20
  105.4 0.5 slice_bitcast_fusion
  105.9 1.0 fusion.11
  106.9 1.6 pad_maximum_fusion.1.r1
  108.5 1.2 pad_maximum_fusion.r2
  109.7 55.4 %shard_map.129 = (f32[64,2048]{1,0:T(8,128)S(1)}, f32[64,2048]{1,0:T(8,128)S(1)}) custom-call(bf16[512,512]{1,0:T(8,128)(2,1)S(1)} %bitcast.98, bf16[512,2048]{1,0:T(8,128)(2,1)S(1)} %pad_maximum_fusion.r2, bf16[512,512]{1,0:T(8,128)(2,1)S(1)} %bitcast.97, bf16[512,2048]{1,0:T(8,128)(2,1)S(1)} %pad_maximum_fusion.1.r1), custom_call_target="tpu_custom_call" | custom-call | flops 2147483648 | bytes 5242880 | tf_op jit(solution)/shard_map/pallas_call | solution.py:169
  165.1 0.8 copy.47
  165.9 0.8 copy.48
  (58 shorter events, 0.8 us)
Async XLA Ops:
  0.6 18.2 %copy-start = (bf16[256,128]{1,0:T(8,128)(2,1)S(1)}, bf16[256,128]{1,0:T(8,128)(2,1)}, u32[]{:S(2)}) copy-start(bf16[256,128]{1,0:T(8,128)(2,1)} %param.10) | copy-start | bytes 196612
  0.6 28.7 %copy-start.1 = (s32[1,2048]{1,0:T(1,128)S(1)}, s32[1,2048]{1,0:T(1,128)}, u32[]{:S(2)}) copy-start(s32[1,2048]{1,0:T(1,128)} %param.15) | copy-start | bytes 24580
  0.7 16.9 %all-to-all-start = ((s32[1,32,32]{2,0,1:T(1,128)}), s32[1,32,32]{2,0,1:T(1,128)S(1)}, u32[]{:S(2)}, u32[]{:S(2)}) async-start(s32[1,32,32]{2,0,1:T(1,128)} %bitcast.131), calls=%async_computation | async-start | bytes 32768 | tf_op jit(solution)/shard_map/all_to_all | solution.py:207
  29.5 16.5 %all-to-all-start.1 = ((bf16[32,1,32,128]{3,2,1,0:T(8,128)(2,1)}), bf16[32,1,32,128]{3,2,1,0:T(8,128)(2,1)S(1)}, u32[]{:S(2)}, u32[]{:S(2)}) async-start(bf16[32,1,32,128]{3,2,1,0:T(8,128)(2,1)} %bitcast.15), calls=%async_computation.1 | async-start | bytes 524288 | tf_op jit(solution)/shard_map/all_to_all | solution.py:226
  50.2 8.0 %collective-permute-start = (bf16[1,1,8,64,128]{4,3,2,1,0:T(8,128)(2,1)S(1)}, bf16[1,1,8,64,128]{4,3,2,1,0:T(8,128)(2,1)S(1)}, u32[]{:S(2)}, u32[]{:S(2)}) collective-permute-start(bf16[1,1,8,64,128]{4,3,2,1,0:T(8,128)(2,1)S(1)} %get-tuple-element.27), channel_id=1, source_target_pairs={{0,8},{1,9},{2,10},{3,11},{4,12},{5,13},{6,14},{7,15},{8,0},{9,1},... | collective-permute-start | bytes 393224 | tf_op jit(solution)/shard_map/ppermute | solution.py:20
  50.2 8.0 %collective-permute-start.1 = (bf16[1,1,8,64,128]{4,3,2,1,0:T(8,128)(2,1)S(1)}, bf16[1,1,8,64,128]{4,3,2,1,0:T(8,128)(2,1)S(1)}, u32[]{:S(2)}, u32[]{:S(2)}) collective-permute-start(bf16[1,1,8,64,128]{4,3,2,1,0:T(8,128)(2,1)S(1)} %get-tuple-element.26), channel_id=1, source_target_pairs={{0,16},{1,17},{2,18},{3,19},{4,20},{5,21},{6,22},{7,23},{8,24},{9,... | collective-permute-start | bytes 393224 | tf_op jit(solution)/shard_map/ppermute | solution.py:20
  51.2 7.5 %slice-start.2 = ((s8[8388608]{0:T(1024)(128)(4,1)}), s8[4194304]{0:T(1024)(128)(4,1)S(1)}, s32[]{:S(2)}) async-start(s8[8388608]{0:T(1024)(128)(4,1)} %bitcast.135), calls=%async_computation.5 | async-start | bytes 8388608
  51.2 7.5 %slice-start.3 = ((s8[8388608]{0:T(1024)(128)(4,1)}), s8[4194304]{0:T(1024)(128)(4,1)S(1)}, s32[]{:S(2)}) async-start(s8[8388608]{0:T(1024)(128)(4,1)} %bitcast.135), calls=%async_computation.6 | async-start | bytes 8388608
  51.2 7.3 %collective-permute-start.2 = (bf16[1,1,8,64,128]{4,3,2,1,0:T(8,128)(2,1)S(1)}, bf16[1,1,8,64,128]{4,3,2,1,0:T(8,128)(2,1)S(1)}, u32[]{:S(2)}, u32[]{:S(2)}) collective-permute-start(bf16[1,1,8,64,128]{4,3,2,1,0:T(8,128)(2,1)S(1)} %get-tuple-element.25), channel_id=1, source_target_pairs={{0,24},{1,25},{2,26},{3,27},{4,28},{5,29},{6,30},{7,31},{8,16},{9,... | collective-permute-start | bytes 393224 | tf_op jit(solution)/shard_map/ppermute | solution.py:20
  61.1 4.7 %collective-permute-start.3 = (bf16[2,4,1,64,128]{4,3,1,0,2:T(8,128)(2,1)}, bf16[2,4,1,64,128]{4,3,1,0,2:T(8,128)(2,1)S(1)}, u32[]{:S(2)}, u32[]{:S(2)}) collective-permute-start(bf16[2,4,1,64,128]{4,3,1,0,2:T(8,128)(2,1)} %get-tuple-element.23), channel_id=1, source_target_pairs={{0,8},{1,9},{2,10},{3,11},{4,12},{5,13},{6,14},{7,15},{8,0},{9,1},... | collective-permute-start | bytes 393224 | tf_op jit(solution)/shard_map/ppermute | solution.py:20
  61.4 6.5 %collective-permute-start.4 = (bf16[2,4,1,64,128]{4,3,1,0,2:T(8,128)(2,1)}, bf16[2,4,1,64,128]{4,3,1,0,2:T(8,128)(2,1)S(1)}, u32[]{:S(2)}, u32[]{:S(2)}) collective-permute-start(bf16[2,4,1,64,128]{4,3,1,0,2:T(8,128)(2,1)} %get-tuple-element.22), channel_id=1, source_target_pairs={{0,1},{1,0},{2,3},{3,2},{4,5},{5,4},{6,7},{7,6},{8,9},{9,8},{10,11... | collective-permute-start | bytes 393224 | tf_op jit(solution)/shard_map/ppermute | solution.py:20
  62.5 6.9 %collective-permute-start.5 = (bf16[2,4,1,64,128]{4,3,1,0,2:T(8,128)(2,1)S(1)}, bf16[2,4,1,64,128]{4,3,1,0,2:T(8,128)(2,1)S(1)}, u32[]{:S(2)}, u32[]{:S(2)}) collective-permute-start(bf16[2,4,1,64,128]{4,3,1,0,2:T(8,128)(2,1)S(1)} %get-tuple-element.21), channel_id=1, source_target_pairs={{0,9},{1,8},{2,11},{3,10},{4,13},{5,12},{6,15},{7,14},{8,1},{9,0},... | collective-permute-start | bytes 393224 | tf_op jit(solution)/shard_map/ppermute | solution.py:20
  69.4 7.4 %slice-start = ((s8[8388608]{0:T(1024)(128)(4,1)}), s8[4194304]{0:T(1024)(128)(4,1)S(1)}, s32[]{:S(2)}) async-start(s8[8388608]{0:T(1024)(128)(4,1)} %bitcast.99), calls=%async_computation.3 | async-start | bytes 8388608
  69.5 7.3 %slice-start.1 = ((s8[8388608]{0:T(1024)(128)(4,1)}), s8[4194304]{0:T(1024)(128)(4,1)S(1)}, s32[]{:S(2)}) async-start(s8[8388608]{0:T(1024)(128)(4,1)} %bitcast.99), calls=%async_computation.4 | async-start | bytes 8388608
  76.2 14.5 %collective-permute-start.10 = (bf16[128,2048]{1,0:T(8,128)(2,1)S(1)}, bf16[128,2048]{1,0:T(8,128)(2,1)}, u32[]{:S(2)}, u32[]{:S(2)}) collective-permute-start(bf16[128,2048]{1,0:T(8,128)(2,1)S(1)} %fusion.3), channel_id=1, source_target_pairs={{0,16},{1,17},{2,18},{3,19},{4,20},{5,21},{6,22},{7,23},{8,24},{9,... | collective-permute-start | bytes 1572872 | tf_op jit(solution)/shard_map/ppermute | solution.py:20
  76.7 6.8 %copy-start.2 = (bf16[1,32,1,128]{3,2,1,0:T(2,128)(2,1)S(1)}, bf16[1,32,1,128]{3,2,1,0:T(2,128)(2,1)}, u32[]{:S(2)}) copy-start(bf16[1,32,1,128]{3,2,1,0:T(2,128)(2,1)} %copy.41) | copy-start | bytes 24580
  84.3 15.5 %all-to-all-start.2 = ((bf16[1,32,33,128]{3,2,0,1:T(8,128)(2,1)}), bf16[1,32,33,128]{3,2,0,1:T(8,128)(2,1)S(1)}, u32[]{:S(2)}, u32[]{:S(2)}) async-start(bf16[1,32,33,128]{3,2,0,1:T(8,128)(2,1)} %maximum_bitcast_fusion.2), calls=%async_computation.2 | async-start | bytes 655360 | tf_op jit(solution)/shard_map/all_to_all | solution.py:279
  87.7 17.6 %collective-permute-start.7 = (bf16[128,2048]{1,0:T(8,128)(2,1)S(1)}, bf16[128,2048]{1,0:T(8,128)(2,1)S(1)}, u32[]{:S(2)}, u32[]{:S(2)}) collective-permute-start(bf16[128,2048]{1,0:T(8,128)(2,1)S(1)} %get-tuple-element.16), channel_id=1, source_target_pairs={{0,1},{1,0},{2,3},{3,2},{4,5},{5,4},{6,7},{7,6},{8,9},{9,8},{10,11... | collective-permute-start | bytes 1572872 | tf_op jit(solution)/shard_map/ppermute | solution.py:20
  89.6 17.2 %collective-permute-start.9 = (bf16[128,2048]{1,0:T(8,128)(2,1)S(1)}, bf16[128,2048]{1,0:T(8,128)(2,1)}, u32[]{:S(2)}, u32[]{:S(2)}) collective-permute-start(bf16[128,2048]{1,0:T(8,128)(2,1)S(1)} %fusion.3), channel_id=1, source_target_pairs={{0,8},{1,9},{2,10},{3,11},{4,12},{5,13},{6,14},{7,15},{8,0},{9,1},... | collective-permute-start | bytes 1572872 | tf_op jit(solution)/shard_map/ppermute | solution.py:20
  89.6 18.8 %collective-permute-start.6 = (bf16[128,2048]{1,0:T(8,128)(2,1)S(1)}, bf16[128,2048]{1,0:T(8,128)(2,1)}, u32[]{:S(2)}, u32[]{:S(2)}) collective-permute-start(bf16[128,2048]{1,0:T(8,128)(2,1)S(1)} %get-tuple-element.16), channel_id=1, source_target_pairs={{0,8},{1,9},{2,10},{3,11},{4,12},{5,13},{6,14},{7,15},{8,0},{9,1},... | collective-permute-start | bytes 1572872 | tf_op jit(solution)/shard_map/ppermute | solution.py:20
  90.7 16.1 %collective-permute-start.11 = (bf16[128,2048]{1,0:T(8,128)(2,1)}, bf16[128,2048]{1,0:T(8,128)(2,1)}, u32[]{:S(2)}, u32[]{:S(2)}) collective-permute-start(bf16[128,2048]{1,0:T(8,128)(2,1)} %collective-permute-done.10), channel_id=1, source_target_pairs={{0,8},{1,9},{2,10},{3,11},{4,12},{5,13},{6,14},{7,15},{8,0},{9,1},... | collective-permute-start | bytes 1572872 | tf_op jit(solution)/shard_map/ppermute | solution.py:20
  105.4 3.1 %collective-permute-start.8 = (bf16[128,2048]{1,0:T(8,128)(2,1)S(1)}, bf16[128,2048]{1,0:T(8,128)(2,1)S(1)}, u32[]{:S(2)}, u32[]{:S(2)}) collective-permute-start(bf16[128,2048]{1,0:T(8,128)(2,1)S(1)} %collective-permute-done.7), channel_id=1, source_target_pairs={{0,8},{1,9},{2,10},{3,11},{4,12},{5,13},{6,14},{7,15},{8,0},{9,1},... | collective-permute-start | bytes 1572872 | tf_op jit(solution)/shard_map/ppermute | solution.py:20

commit v4 on v3

--- a/solution.py
+++ b/solution.py
@@ -155,7 +155,7 @@
 
 
 def halve(l2, r2, l1, r1, core_bit, both):
-    steps, chunks = len(both[0]), 2
+    steps, chunks = len(both[0]), 4
     rows, depth = l2.shape
     columns = r2.shape[1]
     wide = columns // chunks
@@ -207,7 +207,12 @@
     incoming = lax.all_to_all(
         request_rows, AXES, split_axis=1, concat_axis=0, tiled=True
     ).reshape(peers * slots)
-    served = table[incoming]
+    home = (
+        jnp.arange(table.shape[0], dtype=jnp.int32)[:, None] == incoming[None, :]
+    ).astype(jnp.bfloat16)
+    served = lax.dot_general(
+        home, table, (((0,), (0,)), ((), ())), preferred_element_type=jnp.float32
+    ).astype(jnp.bfloat16)
 
     owner_ids = jnp.arange(peers, dtype=jnp.int32)
     match = lookup_owner[:, None] == owner_ids[None, :]
@@ -254,15 +259,14 @@
     dz2 = (dlogit[:, None] * w_out.astype(jnp.float32)[None, :] * silu_slope(z2)).astype(
         jnp.bfloat16
     )
-    h1_left, dz2 = lax.optimization_barrier((h1_left, dz2))
     head_term = jnp.sum(dlogit[:, None] * h2.astype(jnp.float32), axis=0)
     dz2_all = gather_right(dz2, core_bit, 0)
     back_two = lax.dot_general(
         dz2, w_second, (((1,), (1,)), ((), ())), preferred_element_type=jnp.float32
     )
     dz1 = (back_two * silu_slope(z1)).astype(jnp.bfloat16)
+    h1_left, dz1 = lax.optimization_barrier((h1_left, dz1))
     dz1_all = gather_right(dz1, core_bit, core_bit + 1)
-    grad_second, grad_first = halve(h1_left, dz2_all, x_left, dz1_all, core_bit, both)
     back_one = lax.dot_general(
         dz1, w_first, (((1,), (1,)), ((), ())), preferred_element_type=jnp.float32
     )
@@ -276,11 +280,10 @@
     outgoing = jnp.concatenate(
         [slot_grad.reshape(peers, slots, width), head.reshape(peers, extra, width)], axis=1
     ).astype(jnp.bfloat16)
+    outgoing, dz1_all = lax.optimization_barrier((outgoing, dz1_all))
     returned = lax.all_to_all(outgoing[None], AXES, split_axis=1, concat_axis=0, tiled=True)[:, 0]
+    grad_second, grad_first = halve(h1_left, dz2_all, x_left, dz1_all, core_bit, both)
     grad_out = jnp.sum(returned[:, slots:].astype(jnp.float32), axis=0).reshape(-1)[:share]
-    home = (
-        jnp.arange(table.shape[0], dtype=jnp.int32)[:, None] == incoming[None, :]
-    ).astype(jnp.bfloat16)
     row_grad = jnp.dot(
         home, returned[:, :slots].reshape(peers * slots, width), preferred_element_type=jnp.float32
     )

time: 168 us -> 162 us (0.964)
  waiting for transfers between devices: 21.6 us -> 16.1 us
  matrix products: 32.5 us -> 36 us
  local copies, waits for them, and re-layouts: 12.4 us -> 9.83 us
    all_to_all x1, waiting for transfers between devices: 9.13 us -> 0.01 us  [per_device(): lax.all_to_all(outgoing[None], AXES, split_axis=1, concat_axis=0, tiled=T...]
    gather x1 -> x0, local copies, waits for them, and re-layouts: 4.31 us -> none  [per_device(): served = table[incoming]]
    ppermute x12, waiting for transfers between devices: 9.81 us -> 13.5 us  [swap(): return lax.ppermute(value, AXES, [(d, d ^ mask) for d in range(peers)])]
    dot_general x1, matrix products: 1.44 us -> 4.89 us  [per_device(): z2 = jnp.dot(h1, w_second, preferred_element_type=jnp.float32)]
    dot_general x1, matrix products: 3.08 us -> 6.45 us  [per_device(): lax.dot_general(dz1, w_first, (((1,), (1,)), ((), ())), preferred_element...]
    unnamed x17 -> x21, local copies, waits for them, and re-layouts: 2.92 us -> 6.05 us
    dot_general x1, matrix products: 6.71 us -> 4.03 us  [per_device(): lax.dot_general(dz2, w_second, (((1,), (1,)), ((), ())), preferred_elemen...]
  transfers between devices with their start and end apart: 15 -> 15, of which waited for: 7 -> 3; matrix products, arithmetic and copies ran while one was open for 22% -> 28% of each run, Pallas kernels for 0% -> 34%
where the time goes in v4:
time: 162 us; the launch traced here: 161 us
  Pallas kernels  54.3 us (34%)
  matrix products  36 us (22%)
  starting transfers between devices  23 us (14%)
  other arithmetic  20.2 us (12%)
  waiting for transfers between devices  16.1 us (10%)
  local copies, waits for them, and re-layouts  9.83 us (6%)
    pallas_call x1, Pallas kernels, halve(): pl.pallas_call(functools.partial(halving_kernel, core_bit, both), out_sha...  54.3 us
    ppermute x12, waiting for transfers between devices, swap(): return lax.ppermute(value, AXES, [(d, d ^ mask) for d in range(peers)])  13.5 us
    convert_element_type x1, other arithmetic, per_device(): counted = lax.optimization_barrier(counted.astype(jnp.bfloat16))  8.02 us
    all_to_all x1, starting transfers between devices, per_device(): lax.all_to_all(request_rows, AXES, split_axis=1, concat_axis=0, tiled=True)  7.3 us
    ppermute x12, starting transfers between devices, swap(): return lax.ppermute(value, AXES, [(d, d ^ mask) for d in range(peers)])  6.92 us
    dot_general x1, matrix products, per_device(): lax.dot_general(dz1, w_first, (((1,), (1,)), ((), ())), preferred_element...  6.45 us
    dot_general x1, matrix products, per_device(): lax.dot_general(first, shifted, (((1,), (1,)), ((), ())), preferred_eleme...  6.2 us
    unnamed x21, local copies, waits for them, and re-layouts  6.05 us
  transfers between devices with their start and end apart: 15, of which 3 were waited for; matrix products, arithmetic and copies ran while one was open for 28% of the time, Pallas kernels for 34%

profile of v4, /device:TPU:0, one launch (start us, length us, event | category | flops | bytes accessed | tf_op | source)
XLA Modules:
  0.0 160.7 jit_solution(15220594257872060858)
XLA Ops:
  0.7 7.3 %all-to-all-start = ((s32[1,32,32]{2,0,1:T(1,128)}), s32[1,32,32]{2,0,1:T(1,128)S(1)}, u32[]{:S(2)}, u32[]{:S(2)}) async-start(s32[1,32,32]{2,0,1:T(1,128)} %bitcast.126), calls=%async_computation | async-start | bytes 32768 | tf_op jit(solution)/shard_map/all_to_all | solution.py:207
  8.0 0.7 slice.99
  8.7 1.0 reduce-window.9
  9.7 0.1 slice.129
  9.8 0.1 slice_reduce_fusion
  9.9 0.7 convert_rsqrt_fusion
  10.6 0.8 bitcast_subtract_fusion
  11.4 0.9 select_reduce_fusion
  12.3 0.9 fusion.14
  13.2 0.1 pad_slice_fusion
  13.3 0.1 pad_slice_fusion.7
  13.4 0.7 convert_element_type.118
  14.1 0.7 reshape.149
  15.1 0.4 stack.67
  15.5 0.5 broadcast.34
  16.1 0.7 reduce.10
  16.7 0.1 eq.169
  16.8 1.2 convolution_convert_fusion
  18.0 6.2 %fusion = f32[2048,16]{0,1:T(8,128)S(1)} fusion(bf16[16,4096]{1,0:T(8,128)(2,1)S(1)} %stack.67, s32[2048]{0:T(1024)S(1)} %bitcast_subtract_fusion), kind=kOutput, calls=%fused_computation.1 | convolution fusion | flops 276824064 | bytes 270336 | tf_op jit(solution)/shard_map/dot_general | solution.py:235
  24.3 5.8 %all-to-all-start.1 = ((bf16[32,1,32,128]{3,2,1,0:T(8,128)(2,1)}), bf16[32,1,32,128]{3,2,1,0:T(8,128)(2,1)S(1)}, u32[]{:S(2)}, u32[]{:S(2)}) async-start(bf16[32,1,32,128]{3,2,1,0:T(8,128)(2,1)} %bitcast.14), calls=%async_computation.1 | async-start | bytes 524288 | tf_op jit(solution)/shard_map/all_to_all | solution.py:231
  30.2 8.0 %add_convert_fusion = bf16[2048,1024]{0,1:T(8,128)(2,1)} fusion(f32[2048]{0:T(1024)S(1)} %bitcast.119, f32[2048]{0:T(1024)S(1)} %bitcast.120, f32[2048]{0:T(1024)S(1)} %bitcast.121, f32[2048]{0:T(1024)S(1)} %bitcast.122, f32[2048]{0:T(1024)S(1)} %bitcast.123, f32[2048]{0:T(1024)S(1)} %bitcast.124, f32[2048]{0:T(1024)S(1)} %bitcast.125, ...), kind=kLoop, calls=%fused_computation.3 | loop fusion | flops 50331648 | bytes 4263936 | tf_op jit(solution)/shard_map/convert_element_type | solution.py:245
  38.2 2.6 %all-to-all-done.1 = bf16[32,1,32,128]{3,2,1,0:T(8,128)(2,1)S(1)} async-done(((bf16[32,1,32,128]{3,2,1,0:T(8,128)(2,1)}), bf16[32,1,32,128]{3,2,1,0:T(8,128)(2,1)S(1)}, u32[]{:S(2)}, u32[]{:S(2)}) %all-to-all-start.1) | async-done | bytes 262176 | tf_op jit(solution)/shard_map/all_to_all | solution.py:231
  40.8 3.6 %fusion.2 = bf16[2048,128]{1,0:T(8,128)(2,1)S(1)} fusion(bf16[2048,1024]{0,1:T(8,128)(2,1)} %add_convert_fusion, bf16[1024,128]{1,0:T(8,128)(2,1)S(1)} %bitcast.106, f32[2048]{0:T(1024)S(1)} %convert_rsqrt_fusion), kind=kOutput, calls=%fused_computation.7 | convolution fusion | flops 537395200 | bytes 4988928 | tf_op jit(solution)/shard_map/dot_general | solution.py:247
  44.5 0.2 reshape.141
  44.7 0.3 copy.37
  45.0 0.6 collective-permute-start.2
  45.6 0.8 collective-permute-start.1
  46.5 0.5 collective-permute-start
  46.9 4.7 %multiply_convert_fusion.2 = (bf16[128,2048]{1,0:T(8,128)(2,1)S(1)}, f32[128,2048]{1,0:T(8,128)S(1)}) fusion(bf16[128,2048]{1,0:T(8,128)(2,1)S(1)} %reshape.141, bf16[2048,2048]{1,0:T(8,128)(2,1)} %param.17), kind=kOutput, calls=%fused_computation.24 | convolution fusion | flops 1075052544 | bytes 10485760 | tf_op jit(solution)/shard_map/dot_general | solution.py:251
  51.7 1.8 %collective-permute-done.1 = bf16[1,1,8,64,128]{4,3,2,1,0:T(8,128)(2,1)S(1)} collective-permute-done((bf16[1,1,8,64,128]{4,3,2,1,0:T(8,128)(2,1)S(1)}, bf16[1,1,8,64,128]{4,3,2,1,0:T(8,128)(2,1)S(1)}, u32[]{:S(2)}, u32[]{:S(2)}) %collective-permute-start.1) | collective-permute-done | bytes 131104 | tf_op jit(solution)/shard_map/ppermute | solution.py:20
  53.6 0.1 maximum_bitcast_fusion
  53.7 0.3 copy.39
  53.9 0.1 constant_dynamic-slice_fusion
  54.0 0.7 collective-permute-start.5
  54.7 1.2 collective-permute-start.4
  55.8 0.1 collective-permute-start.3
  56.0 4.9 %multiply_convert_fusion.1 = (bf16[128,2048]{1,0:T(8,128)(2,1)S(1)}, f32[128,2048]{1,0:T(8,128)S(1)}) fusion(bf16[128,2048]{1,0:T(8,128)(2,1)S(1)} %get-tuple-element.16, bf16[2048,2048]{1,0:T(8,128)(2,1)} %param.18), kind=kOutput, calls=%fused_computation.22 | convolution fusion | flops 1075052544 | bytes 10485760 | tf_op jit(solution)/shard_map/dot_general | solution.py:255
  60.9 0.2 fusion.9
  61.1 1.3 multiply_reduce_fusion
  62.4 4.0 %fusion.3 = bf16[128,2048]{1,0:T(8,128)(2,1)S(1)} fusion(bf16[128,2048]{1,0:T(8,128)(2,1)} %get-tuple-element.55, bf16[2048,2048]{1,0:T(8,128)(2,1)S(1)} %bitcast.130, f32[128,2048]{1,0:T(8,128)S(1)} %get-tuple-element.57), kind=kOutput, calls=%fused_computation.8 | convolution fusion | flops 1076101120 | bytes 10485760 | tf_op jit(solution)/shard_map/dot_general | solution.py:264
  66.5 0.1 maximum_bitcast_fusion.1
  66.7 0.9 collective-permute-start.10
  67.6 0.1 rsqrt.15
  67.7 1.0 collective-permute-start.7
  68.7 0.1 reshape.146
  68.8 0.6 collective-permute-start.9
  69.3 11.6 %collective-permute-done.10 = bf16[128,2048]{1,0:T(8,128)(2,1)S(1)} collective-permute-done((bf16[128,2048]{1,0:T(8,128)(2,1)S(1)}, bf16[128,2048]{1,0:T(8,128)(2,1)S(1)}, u32[]{:S(2)}, u32[]{:S(2)}) %collective-permute-start.10) | collective-permute-done | bytes 524320 | tf_op jit(solution)/shard_map/ppermute | solution.py:20
  81.0 0.3 mul.91
  81.3 6.4 %fusion.4 = bf16[128,2048]{1,0:T(8,128)(2,1)S(1)} fusion(bf16[128,2048]{1,0:T(8,128)(2,1)S(1)} %fusion.3, bf16[2048,2048]{1,0:T(8,128)(2,1)} %param.17, f32[16,8,16,128]{3,2,1,0:T(8,128)S(1)} %bitcast.97), kind=kOutput, calls=%fused_computation.9 | convolution fusion | flops 1074266112 | bytes 10485760 | tf_op jit(solution)/shard_map/dot_general | solution.py:270
  87.8 0.2 reshape.151
  88.0 0.6 collective-permute-start.8
  88.6 3.7 %convolution_convert_fusion.1 = bf16[32,32,128]{2,1,0:T(8,128)(2,1)S(1)} fusion(bf16[32,32,2048]{2,1,0:T(8,128)(2,1)} %bitcast.98, bf16[2048,128,1]{1,0,2:T(8,128)(2,1)S(1)} %reshape.151), kind=kOutput, calls=%fused_computation.13 | convolution fusion | flops 537001984 | bytes 4980736 | tf_op jit(solution)/shard_map/dot_general | solution.py:274
  92.3 0.8 pad_maximum_fusion.2
  93.0 1.7 %pad_maximum_fusion.1.r1 = bf16[512,2048]{1,0:T(8,128)(2,1)S(1)} fusion(bf16[128,2048]{1,0:T(8,128)(2,1)} %collective-permute-done.11, bf16[128,2048]{1,0:T(8,128)(2,1)} %copy-done.4, bf16[128,2048]{1,0:T(8,128)(2,1)} %collective-permute-done.9, bf16[128,2048]{1,0:T(8,128)(2,1)} %copy-done.3), kind=kLoop, calls=%fused_computation.11 | loop fusion | flops 8388608 | bytes 4194304 | tf_op jit(solution)/shard_map/concatenate | solution.py:60
  94.7 3.0 %all-to-all-start.2 = ((bf16[1,32,33,128]{3,2,0,1:T(8,128)(2,1)}), bf16[1,32,33,128]{3,2,0,1:T(8,128)(2,1)S(1)}, u32[]{:S(2)}, u32[]{:S(2)}) async-start(bf16[1,32,33,128]{3,2,0,1:T(8,128)(2,1)} %bitcast.44), calls=%async_computation.2 | async-start | bytes 655360 | tf_op jit(solution)/shard_map/all_to_all | solution.py:284
  97.7 1.8 %pad_maximum_fusion.r2 = bf16[512,2048]{1,0:T(8,128)(2,1)S(1)} fusion(bf16[128,2048]{1,0:T(8,128)(2,1)} %collective-permute-done.8, bf16[128,2048]{1,0:T(8,128)(2,1)} %collective-permute-done.7, bf16[128,2048]{1,0:T(8,128)(2,1)} %collective-permute-done.6, bf16[128,2048]{1,0:T(8,128)(2,1)} %get-tuple-element.55), kind=kLoop, calls=%fused_computation.10 | loop fusion | flops 8388608 | bytes 4194304 | tf_op jit(solution)/shard_map/concatenate | solution.py:60
  99.5 54.3 %shard_map.129 = (f32[64,2048]{1,0:T(8,128)S(1)}, f32[64,2048]{1,0:T(8,128)S(1)}) custom-call(bf16[512,512]{1,0:T(8,128)(2,1)S(1)} %bitcast.96, bf16[512,2048]{1,0:T(8,128)(2,1)S(1)} %pad_maximum_fusion.r2, bf16[512,512]{1,0:T(8,128)(2,1)S(1)} %bitcast.95, bf16[512,2048]{1,0:T(8,128)(2,1)S(1)} %pad_maximum_fusion.1.r1), custom_call_target="tpu_custom_call" | custom-call | flops 2147483648 | bytes 5242880 | tf_op jit(solution)/shard_map/pallas_call | solution.py:169
  153.8 0.8 copy-done.1
  154.6 0.8 copy-done.2
  155.4 0.1 fusion.15
  155.5 1.0 fusion.10
  156.4 0.5 slice_bitcast_fusion
  156.9 1.9 %copy.47 = f32[64,2048]{1,0:T(8,128)} copy(f32[64,2048]{1,0:T(8,128)} %copy-done.2) | data formatting | bytes 1048576
  158.8 1.9 %copy.48 = f32[64,2048]{1,0:T(8,128)} copy(f32[64,2048]{1,0:T(8,128)} %copy-done.1) | data formatting | bytes 1048576
  (58 shorter events, 0.6 us)
Async XLA Ops:
  0.6 16.2 %copy-start = (bf16[256,128]{1,0:T(8,128)(2,1)S(1)}, bf16[256,128]{1,0:T(8,128)(2,1)}, u32[]{:S(2)}) copy-start(bf16[256,128]{1,0:T(8,128)(2,1)} %param.10) | copy-start | bytes 196612
  0.6 23.6 %copy-start.5 = (s32[1,2048]{1,0:T(1,128)S(1)}, s32[1,2048]{1,0:T(1,128)}, u32[]{:S(2)}) copy-start(s32[1,2048]{1,0:T(1,128)} %param.15) | copy-start | bytes 24580
  0.7 14.9 %all-to-all-start = ((s32[1,32,32]{2,0,1:T(1,128)}), s32[1,32,32]{2,0,1:T(1,128)S(1)}, u32[]{:S(2)}, u32[]{:S(2)}) async-start(s32[1,32,32]{2,0,1:T(1,128)} %bitcast.126), calls=%async_computation | async-start | bytes 32768 | tf_op jit(solution)/shard_map/all_to_all | solution.py:207
  24.3 16.5 %all-to-all-start.1 = ((bf16[32,1,32,128]{3,2,1,0:T(8,128)(2,1)}), bf16[32,1,32,128]{3,2,1,0:T(8,128)(2,1)S(1)}, u32[]{:S(2)}, u32[]{:S(2)}) async-start(bf16[32,1,32,128]{3,2,1,0:T(8,128)(2,1)} %bitcast.14), calls=%async_computation.1 | async-start | bytes 524288 | tf_op jit(solution)/shard_map/all_to_all | solution.py:231
  45.0 6.7 %collective-permute-start.2 = (bf16[1,1,8,64,128]{4,3,2,1,0:T(8,128)(2,1)S(1)}, bf16[1,1,8,64,128]{4,3,2,1,0:T(8,128)(2,1)S(1)}, u32[]{:S(2)}, u32[]{:S(2)}) collective-permute-start(bf16[1,1,8,64,128]{4,3,2,1,0:T(8,128)(2,1)S(1)} %get-tuple-element.29), channel_id=1, source_target_pairs={{0,24},{1,25},{2,26},{3,27},{4,28},{5,29},{6,30},{7,31},{8,16},{9,... | collective-permute-start | bytes 393224 | tf_op jit(solution)/shard_map/ppermute | solution.py:20
  45.6 7.9 %collective-permute-start.1 = (bf16[1,1,8,64,128]{4,3,2,1,0:T(8,128)(2,1)S(1)}, bf16[1,1,8,64,128]{4,3,2,1,0:T(8,128)(2,1)S(1)}, u32[]{:S(2)}, u32[]{:S(2)}) collective-permute-start(bf16[1,1,8,64,128]{4,3,2,1,0:T(8,128)(2,1)S(1)} %get-tuple-element.30), channel_id=1, source_target_pairs={{0,16},{1,17},{2,18},{3,19},{4,20},{5,21},{6,22},{7,23},{8,24},{9,... | collective-permute-start | bytes 393224 | tf_op jit(solution)/shard_map/ppermute | solution.py:20
  46.5 7.1 %collective-permute-start = (bf16[1,1,8,64,128]{4,3,2,1,0:T(8,128)(2,1)S(1)}, bf16[1,1,8,64,128]{4,3,2,1,0:T(8,128)(2,1)S(1)}, u32[]{:S(2)}, u32[]{:S(2)}) collective-permute-start(bf16[1,1,8,64,128]{4,3,2,1,0:T(8,128)(2,1)S(1)} %get-tuple-element.31), channel_id=1, source_target_pairs={{0,8},{1,9},{2,10},{3,11},{4,12},{5,13},{6,14},{7,15},{8,0},{9,1},... | collective-permute-start | bytes 393224 | tf_op jit(solution)/shard_map/ppermute | solution.py:20
  54.0 12.5 %collective-permute-start.5 = (bf16[2,4,1,64,128]{4,3,1,0,2:T(8,128)(2,1)S(1)}, bf16[2,4,1,64,128]{4,3,1,0,2:T(8,128)(2,1)S(1)}, u32[]{:S(2)}, u32[]{:S(2)}) collective-permute-start(bf16[2,4,1,64,128]{4,3,1,0,2:T(8,128)(2,1)S(1)} %get-tuple-element.25), channel_id=1, source_target_pairs={{0,9},{1,8},{2,11},{3,10},{4,13},{5,12},{6,15},{7,14},{8,1},{9,0},... | collective-permute-start | bytes 393224 | tf_op jit(solution)/shard_map/ppermute | solution.py:20
  54.7 11.9 %collective-permute-start.4 = (bf16[2,4,1,64,128]{4,3,1,0,2:T(8,128)(2,1)S(1)}, bf16[2,4,1,64,128]{4,3,1,0,2:T(8,128)(2,1)S(1)}, u32[]{:S(2)}, u32[]{:S(2)}) collective-permute-start(bf16[2,4,1,64,128]{4,3,1,0,2:T(8,128)(2,1)S(1)} %get-tuple-element.26), channel_id=1, source_target_pairs={{0,1},{1,0},{2,3},{3,2},{4,5},{5,4},{6,7},{7,6},{8,9},{9,8},{10,11... | collective-permute-start | bytes 393224 | tf_op jit(solution)/shard_map/ppermute | solution.py:20
  55.8 6.6 %slice-start = ((s8[8388608]{0:T(1024)(128)(4,1)}), s8[4194304]{0:T(1024)(128)(4,1)S(1)}, s32[]{:S(2)}) async-start(s8[8388608]{0:T(1024)(128)(4,1)} %bitcast.129), calls=%async_computation.3 | async-start | bytes 8388608
  55.8 5.1 %copy-start.6 = (s32[128]{0:T(128)S(1)}, s32[128]{0:T(128)}, u32[]{:S(2)}) copy-start(s32[128]{0:T(128)} %param.16) | copy-start | bytes 1540
  55.8 6.6 %slice-start.1 = ((s8[8388608]{0:T(1024)(128)(4,1)}), s8[4194304]{0:T(1024)(128)(4,1)S(1)}, s32[]{:S(2)}) async-start(s8[8388608]{0:T(1024)(128)(4,1)} %bitcast.129), calls=%async_computation.4 | async-start | bytes 8388608
  55.8 10.7 %collective-permute-start.3 = (bf16[2,4,1,64,128]{4,3,1,0,2:T(8,128)(2,1)S(1)}, bf16[2,4,1,64,128]{4,3,1,0,2:T(8,128)(2,1)S(1)}, u32[]{:S(2)}, u32[]{:S(2)}) collective-permute-start(bf16[2,4,1,64,128]{4,3,1,0,2:T(8,128)(2,1)S(1)} %get-tuple-element.27), channel_id=1, source_target_pairs={{0,8},{1,9},{2,10},{3,11},{4,12},{5,13},{6,14},{7,15},{8,0},{9,1},... | collective-permute-start | bytes 393224 | tf_op jit(solution)/shard_map/ppermute | solution.py:20
  66.5 25.8 %copy-start.3 = (bf16[128,2048]{1,0:T(8,128)(2,1)}, bf16[128,2048]{1,0:T(8,128)(2,1)S(1)}, u32[]{:S(2)}) copy-start(bf16[128,2048]{1,0:T(8,128)(2,1)S(1)} %fusion.3) | copy-start | bytes 1572868
  66.7 14.3 %collective-permute-start.10 = (bf16[128,2048]{1,0:T(8,128)(2,1)S(1)}, bf16[128,2048]{1,0:T(8,128)(2,1)S(1)}, u32[]{:S(2)}, u32[]{:S(2)}) collective-permute-start(bf16[128,2048]{1,0:T(8,128)(2,1)S(1)} %fusion.3), channel_id=1, source_target_pairs={{0,16},{1,17},{2,18},{3,19},{4,20},{5,21},{6,22},{7,23},{8,24},{9,... | collective-permute-start | bytes 1572872 | tf_op jit(solution)/shard_map/ppermute | solution.py:20
  67.7 20.4 %collective-permute-start.7 = (bf16[128,2048]{1,0:T(8,128)(2,1)}, bf16[128,2048]{1,0:T(8,128)(2,1)}, u32[]{:S(2)}, u32[]{:S(2)}) collective-permute-start(bf16[128,2048]{1,0:T(8,128)(2,1)} %get-tuple-element.55), channel_id=1, source_target_pairs={{0,1},{1,0},{2,3},{3,2},{4,5},{5,4},{6,7},{7,6},{8,9},{9,8},{10,11... | collective-permute-start | bytes 1572872 | tf_op jit(solution)/shard_map/ppermute | solution.py:20
  68.7 29.0 %collective-permute-start.6 = (bf16[128,2048]{1,0:T(8,128)(2,1)}, bf16[128,2048]{1,0:T(8,128)(2,1)}, u32[]{:S(2)}, u32[]{:S(2)}) collective-permute-start(bf16[128,2048]{1,0:T(8,128)(2,1)} %get-tuple-element.55), channel_id=1, source_target_pairs={{0,8},{1,9},{2,10},{3,11},{4,12},{5,13},{6,14},{7,15},{8,0},{9,1},... | collective-permute-start | bytes 1572872 | tf_op jit(solution)/shard_map/ppermute | solution.py:20
  68.8 24.3 %collective-permute-start.9 = (bf16[128,2048]{1,0:T(8,128)(2,1)S(1)}, bf16[128,2048]{1,0:T(8,128)(2,1)}, u32[]{:S(2)}, u32[]{:S(2)}) collective-permute-start(bf16[128,2048]{1,0:T(8,128)(2,1)S(1)} %fusion.3), channel_id=1, source_target_pairs={{0,8},{1,9},{2,10},{3,11},{4,12},{5,13},{6,14},{7,15},{8,0},{9,1},... | collective-permute-start | bytes 1572872 | tf_op jit(solution)/shard_map/ppermute | solution.py:20
  81.0 11.3 %copy-start.4 = (bf16[128,2048]{1,0:T(8,128)(2,1)}, bf16[128,2048]{1,0:T(8,128)(2,1)S(1)}, u32[]{:S(2)}) copy-start(bf16[128,2048]{1,0:T(8,128)(2,1)S(1)} %collective-permute-done.10) | copy-start | bytes 1572868
  81.0 12.1 %collective-permute-start.11 = (bf16[128,2048]{1,0:T(8,128)(2,1)S(1)}, bf16[128,2048]{1,0:T(8,128)(2,1)}, u32[]{:S(2)}, u32[]{:S(2)}) collective-permute-start(bf16[128,2048]{1,0:T(8,128)(2,1)S(1)} %collective-permute-done.10), channel_id=1, source_target_pairs={{0,8},{1,9},{2,10},{3,11},{4,12},{5,13},{6,14},{7,15},{8,0},{9,1},... | collective-permute-start | bytes 1572872 | tf_op jit(solution)/shard_map/ppermute | solution.py:20
  88.0 9.7 %collective-permute-start.8 = (bf16[128,2048]{1,0:T(8,128)(2,1)}, bf16[128,2048]{1,0:T(8,128)(2,1)}, u32[]{:S(2)}, u32[]{:S(2)}) collective-permute-start(bf16[128,2048]{1,0:T(8,128)(2,1)} %collective-permute-done.7), channel_id=1, source_target_pairs={{0,8},{1,9},{2,10},{3,11},{4,12},{5,13},{6,14},{7,15},{8,0},{9,1},... | collective-permute-start | bytes 1572872 | tf_op jit(solution)/shard_map/ppermute | solution.py:20
  94.7 60.7 %all-to-all-start.2 = ((bf16[1,32,33,128]{3,2,0,1:T(8,128)(2,1)}), bf16[1,32,33,128]{3,2,0,1:T(8,128)(2,1)S(1)}, u32[]{:S(2)}, u32[]{:S(2)}) async-start(bf16[1,32,33,128]{3,2,0,1:T(8,128)(2,1)} %bitcast.44), calls=%async_computation.2 | async-start | bytes 655360 | tf_op jit(solution)/shard_map/all_to_all | solution.py:284
  153.8 0.8 copy-start.1
  154.6 0.8 copy-start.2

commit v5 on v4

--- a/solution.py
+++ b/solution.py
@@ -54,9 +54,8 @@
     )
 
 
-def gather_right(right, core_bit, side):
-    core, near, _, _ = group(core_bit, side)
-    across = swap(right, near)
+def gather_right(right, across, core_bit):
+    core = 1 << core_bit
     return jnp.concatenate([right, swap(right, core), across, swap(across, core)], axis=0)
 
 
@@ -129,25 +128,27 @@
         for g in range(2):
             mine = flip(both[g][0], core_bit)[0]
             accs[g][0][c] = product(g, c, mine)
-    for k in range(1, steps + 1):
-        for c in range(chunks):
-            for g in range(2):
-                copy(g, k - 1, c).wait_recv()
-                if k == steps:
-                    outs[g][:, c * wide : (c + 1) * wide] = accs[g][k - 1][c] + recvs[g][k - 1][
-                        c
-                    ].astype(jnp.float32)
-                    continue
-                mine = flip(both[g][k], core_bit)[0]
-                half = sends[g][k].shape[1]
-
-                def total(part):
-                    at = pl.ds(pl.multiple_of(part * half, half), half)
-                    return accs[g][k - 1][c, at, :] + recvs[g][k - 1][c, at, :].astype(jnp.float32)
-
-                sends[g][k][c] = total(1 - mine).astype(jnp.bfloat16)
-                copy(g, k, c).start()
-                accs[g][k][c] = total(mine)
+    diagonal = [
+        (k, t - k) for t in range(steps + chunks) for k in range(1, steps + 1) if 0 <= t - k < chunks
+    ]
+    for k, c in diagonal:
+        for g in range(2):
+            copy(g, k - 1, c).wait_recv()
+            if k == steps:
+                outs[g][:, c * wide : (c + 1) * wide] = accs[g][k - 1][c] + recvs[g][k - 1][
+                    c
+                ].astype(jnp.float32)
+                continue
+            mine = flip(both[g][k], core_bit)[0]
+            half = sends[g][k].shape[1]
+
+            def total(part):
+                at = pl.ds(pl.multiple_of(part * half, half), half)
+                return accs[g][k - 1][c, at, :] + recvs[g][k - 1][c, at, :].astype(jnp.float32)
+
+            sends[g][k][c] = total(1 - mine).astype(jnp.bfloat16)
+            copy(g, k, c).start()
+            accs[g][k][c] = total(mine)
     for k in range(steps):
         for c in range(chunks):
             for g in range(2):
@@ -260,17 +261,20 @@
         jnp.bfloat16
     )
     head_term = jnp.sum(dlogit[:, None] * h2.astype(jnp.float32), axis=0)
-    dz2_all = gather_right(dz2, core_bit, 0)
+    across2 = swap(dz2, 1)
     back_two = lax.dot_general(
         dz2, w_second, (((1,), (1,)), ((), ())), preferred_element_type=jnp.float32
     )
     dz1 = (back_two * silu_slope(z1)).astype(jnp.bfloat16)
     h1_left, dz1 = lax.optimization_barrier((h1_left, dz1))
-    dz1_all = gather_right(dz1, core_bit, core_bit + 1)
+    across1 = swap(dz1, 2 << core_bit)
     back_one = lax.dot_general(
         dz1, w_first, (((1,), (1,)), ((), ())), preferred_element_type=jnp.float32
     )
     bag_grad = (back_one.reshape(bags, width) * scale).astype(jnp.bfloat16)
+    across2, across1, bag_grad = lax.optimization_barrier((across2, across1, bag_grad))
+    dz2_all = gather_right(dz2, across2, core_bit)
+    dz1_all = gather_right(dz1, across1, core_bit)
     slot_grad = lax.dot_general(
         counted, bag_grad, (((0,), (0,)), ((), ())), preferred_element_type=jnp.float32
     )

time: 162 us -> 161 us (level)
  waiting for transfers between devices: 16.1 us -> 20.5 us
  Pallas kernels: 54.3 us -> 50.2 us
    ppermute x12, waiting for transfers between devices: 13.5 us -> 17.8 us  [swap(): return lax.ppermute(value, AXES, [(d, d ^ mask) for d in range(peers)])]
    pallas_call x1, Pallas kernels: 54.3 us -> 50.2 us  [halve(): pl.pallas_call(functools.partial(halving_kernel, core_bit, both), out_sha...]
    dot_general x1, matrix products: 4.89 us -> 1.43 us  [per_device(): z2 = jnp.dot(h1, w_second, preferred_element_type=jnp.float32)]
    dot_general x1, matrix products: 4.03 us -> 7.32 us  [per_device(): lax.dot_general(dz2, w_second, (((1,), (1,)), ((), ())), preferred_elemen...]
    unnamed x21 -> x17, local copies, waits for them, and re-layouts: 6.05 us -> 6.04 us
  transfers between devices with their start and end apart: 15 -> 15, of which waited for: 3 -> 5; matrix products, arithmetic and copies ran while one was open for 28% -> 27% of each run, Pallas kernels for 34% -> 31%
where the time goes in v5:
time: 161 us; the launch traced here: 160 us
  Pallas kernels  50.2 us (31%)
  matrix products  35.7 us (22%)
  starting transfers between devices  22.2 us (14%)
  other arithmetic  20.5 us (13%)
  waiting for transfers between devices  20.5 us (13%)
  local copies, waits for them, and re-layouts  9.33 us (6%)
    pallas_call x1, Pallas kernels, halve(): pl.pallas_call(functools.partial(halving_kernel, core_bit, both), out_sha...  50.2 us
    ppermute x12, waiting for transfers between devices, swap(): return lax.ppermute(value, AXES, [(d, d ^ mask) for d in range(peers)])  17.8 us
    convert_element_type x1, other arithmetic, per_device(): counted = lax.optimization_barrier(counted.astype(jnp.bfloat16))  7.99 us
    dot_general x1, matrix products, per_device(): lax.dot_general(dz2, w_second, (((1,), (1,)), ((), ())), preferred_elemen...  7.32 us
    all_to_all x1, starting transfers between devices, per_device(): lax.all_to_all(request_rows, AXES, split_axis=1, concat_axis=0, tiled=True)  7.3 us
    dot_general x1, matrix products, per_device(): lax.dot_general(dz1, w_first, (((1,), (1,)), ((), ())), preferred_element...  6.43 us
    dot_general x1, matrix products, per_device(): lax.dot_general(first, shifted, (((1,), (1,)), ((), ())), preferred_eleme...  6.2 us
    ppermute x12, starting transfers between devices, swap(): return lax.ppermute(value, AXES, [(d, d ^ mask) for d in range(peers)])  6.12 us
  transfers between devices with their start and end apart: 15, of which 5 were waited for; matrix products, arithmetic and copies ran while one was open for 27% of the time, Pallas kernels for 31%

profile of v5, /device:TPU:0, one launch (start us, length us, event | category | flops | bytes accessed | tf_op | source)
XLA Modules:
  0.0 159.6 jit_solution(5848417779777023089)
XLA Ops:
  0.7 7.3 %all-to-all-start = ((s32[1,32,32]{2,0,1:T(1,128)}), s32[1,32,32]{2,0,1:T(1,128)S(1)}, u32[]{:S(2)}, u32[]{:S(2)}) async-start(s32[1,32,32]{2,0,1:T(1,128)} %bitcast.118), calls=%async_computation | async-start | bytes 32768 | tf_op jit(solution)/shard_map/all_to_all | solution.py:208
  8.0 0.7 slice.99
  8.7 0.7 convert_rsqrt_fusion
  9.4 1.0 reduce-window.9
  10.4 0.1 slice.129
  10.5 0.1 slice_reduce_fusion
  10.6 0.8 bitcast_subtract_fusion
  11.4 0.9 select_reduce_fusion
  12.3 0.9 fusion.13
  13.2 0.1 pad_slice_fusion
  13.3 0.1 pad_slice_fusion.7
  13.4 0.7 convert_element_type.111
  14.1 0.7 reshape.148
  15.1 0.4 stack.67
  15.5 0.5 broadcast.30
  16.1 0.7 reduce.6
  16.7 0.1 eq.169
  16.8 1.2 convolution_convert_fusion
  18.0 6.2 %fusion = f32[2048,16]{0,1:T(8,128)S(1)} fusion(bf16[16,4096]{1,0:T(8,128)(2,1)S(1)} %stack.67, s32[2048]{0:T(1024)S(1)} %bitcast_subtract_fusion), kind=kOutput, calls=%fused_computation.1 | convolution fusion | flops 276824064 | bytes 270336 | tf_op jit(solution)/shard_map/dot_general | solution.py:236
  24.3 5.8 %all-to-all-start.1 = ((bf16[32,1,32,128]{3,2,1,0:T(8,128)(2,1)}), bf16[32,1,32,128]{3,2,1,0:T(8,128)(2,1)S(1)}, u32[]{:S(2)}, u32[]{:S(2)}) async-start(bf16[32,1,32,128]{3,2,1,0:T(8,128)(2,1)} %bitcast.14), calls=%async_computation.1 | async-start | bytes 524288 | tf_op jit(solution)/shard_map/all_to_all | solution.py:232
  30.2 8.0 %add_convert_fusion = bf16[2048,1024]{1,0:T(8,128)(2,1)} fusion(f32[1024]{0:T(1024)S(1)} %iota_convert_fusion, f32[2048]{0:T(1024)S(1)} %bitcast.111, f32[2048]{0:T(1024)S(1)} %bitcast.112, f32[2048]{0:T(1024)S(1)} %bitcast.113, f32[2048]{0:T(1024)S(1)} %bitcast.114, f32[2048]{0:T(1024)S(1)} %bitcast.115, f32[2048]{0:T(1024)S(1)} %bitcast.116, ...), kind=kLoop, calls=%fused_computation.3 | loop fusion | flops 50331648 | bytes 4263936 | tf_op jit(solution)/shard_map/convert_element_type | solution.py:246
  38.2 2.7 %all-to-all-done.1 = bf16[32,1,32,128]{3,2,1,0:T(8,128)(2,1)S(1)} async-done(((bf16[32,1,32,128]{3,2,1,0:T(8,128)(2,1)}), bf16[32,1,32,128]{3,2,1,0:T(8,128)(2,1)S(1)}, u32[]{:S(2)}, u32[]{:S(2)}) %all-to-all-start.1) | async-done | bytes 262176 | tf_op jit(solution)/shard_map/all_to_all | solution.py:232
  40.8 3.4 %fusion.2 = bf16[2048,128]{1,0:T(8,128)(2,1)S(1)} fusion(bf16[2048,1024]{1,0:T(8,128)(2,1)} %add_convert_fusion, bf16[1024,128]{1,0:T(8,128)(2,1)S(1)} %bitcast.98, f32[2048]{0:T(1024)S(1)} %convert_rsqrt_fusion), kind=kOutput, calls=%fused_computation.6 | convolution fusion | flops 537395200 | bytes 4988928 | tf_op jit(solution)/shard_map/dot_general | solution.py:248
  44.3 0.2 reshape.138
  44.5 0.3 copy.35
  44.8 0.6 collective-permute-start.2
  45.5 0.8 collective-permute-start.1
  46.3 0.5 collective-permute-start
  46.8 5.0 %multiply_convert_fusion.3 = (bf16[128,2048]{1,0:T(8,128)(2,1)S(1)}, f32[128,2048]{1,0:T(8,128)S(1)}) fusion(bf16[128,2048]{1,0:T(8,128)(2,1)S(1)} %reshape.138, bf16[2048,2048]{1,0:T(8,128)(2,1)} %param.17), kind=kOutput, calls=%fused_computation.23 | convolution fusion | flops 1075052544 | bytes 10485760 | tf_op jit(solution)/shard_map/dot_general | solution.py:252
  51.7 1.6 %collective-permute-done.1 = bf16[1,1,8,64,128]{4,3,2,1,0:T(8,128)(2,1)S(1)} collective-permute-done((bf16[1,1,8,64,128]{4,3,2,1,0:T(8,128)(2,1)S(1)}, bf16[1,1,8,64,128]{4,3,2,1,0:T(8,128)(2,1)S(1)}, u32[]{:S(2)}, u32[]{:S(2)}) %collective-permute-start.1) | collective-permute-done | bytes 131104 | tf_op jit(solution)/shard_map/ppermute | solution.py:20
  53.4 0.1 maximum_bitcast_fusion
  53.5 1.4 multiply_convert_fusion.2
  55.0 0.2 fusion.8
  55.2 1.3 multiply_reduce_fusion
  56.5 1.2 collective-permute-start.7
  57.7 0.3 copy.37
  58.0 0.1 constant_dynamic-slice_fusion
  58.0 1.0 collective-permute-start.5
  59.1 1.2 collective-permute-start.4
  60.2 7.3 %fusion.3 = bf16[128,2048]{1,0:T(8,128)(2,1)} fusion(bf16[128,2048]{1,0:T(8,128)(2,1)} %get-tuple-element.61, bf16[2048,2048]{1,0:T(8,128)(2,1)} %param.18, f32[128,2048]{1,0:T(8,128)S(1)} %get-tuple-element.63), kind=kOutput, calls=%fused_computation.7 | convolution fusion | flops 1076101120 | bytes 10485760 | tf_op jit(solution)/shard_map/dot_general | solution.py:265
  67.5 0.1 reshape.145
  67.6 5.4 %collective-permute-done.5 = bf16[2,4,1,64,128]{4,3,1,0,2:T(8,128)(2,1)S(1)} collective-permute-done((bf16[2,4,1,64,128]{4,3,1,0,2:T(8,128)(2,1)S(1)}, bf16[2,4,1,64,128]{4,3,1,0,2:T(8,128)(2,1)S(1)}, u32[]{:S(2)}, u32[]{:S(2)}) %collective-permute-start.5) | collective-permute-done | bytes 131104 | tf_op jit(solution)/shard_map/ppermute | solution.py:20
  73.0 3.3 %collective-permute-done.4 = bf16[2,4,1,64,128]{4,3,1,0,2:T(8,128)(2,1)S(1)} collective-permute-done((bf16[2,4,1,64,128]{4,3,1,0,2:T(8,128)(2,1)S(1)}, bf16[2,4,1,64,128]{4,3,1,0,2:T(8,128)(2,1)S(1)}, u32[]{:S(2)}, u32[]{:S(2)}) %collective-permute-start.4) | collective-permute-done | bytes 131104 | tf_op jit(solution)/shard_map/ppermute | solution.py:20
  76.3 0.1 maximum_bitcast_fusion.1
  76.4 0.1 collective-permute-start.10
  76.5 0.2 collective-permute-start.8
  76.7 6.4 %fusion.16 = f32[128,2048]{1,0:T(8,128)S(1)} fusion(bf16[128,2048]{1,0:T(8,128)(2,1)} %fusion.3, bf16[2048,2048]{1,0:T(8,128)(2,1)} %param.17), kind=kOutput, calls=%fused_computation.72 | convolution fusion | flops 1073741824 | bytes 9961472 | tf_op jit(solution)/shard_map/dot_general | solution.py:271
  83.1 0.2 reshape.143
  83.3 0.3 multiply_convert_fusion
  83.6 7.5 %collective-permute-done.8 = bf16[128,2048]{1,0:T(8,128)(2,1)} collective-permute-done((bf16[128,2048]{1,0:T(8,128)(2,1)}, bf16[128,2048]{1,0:T(8,128)(2,1)}, u32[]{:S(2)}, u32[]{:S(2)}) %collective-permute-start.8) | collective-permute-done | bytes 524320 | tf_op jit(solution)/shard_map/ppermute | solution.py:20
  91.2 0.6 collective-permute-start.9
  91.8 3.5 %convolution_convert_fusion.1 = bf16[1024,128]{1,0:T(8,128)(2,1)S(1)} fusion(bf16[2048,1024]{1,0:T(8,128)(2,1)} %add_convert_fusion, bf16[2048,128]{1,0:T(8,128)(2,1)S(1)} %multiply_convert_fusion), kind=kOutput, calls=%fused_computation.11 | convolution fusion | flops 537001984 | bytes 4980736 | tf_op jit(solution)/shard_map/dot_general | solution.py:278
  95.2 1.0 pad_maximum_fusion.2
  96.2 1.5 pad_maximum_fusion.1.r1
  97.7 3.0 %all-to-all-start.2 = ((bf16[1,32,33,128]{3,2,0,1:T(8,128)(2,1)}), bf16[1,32,33,128]{3,2,0,1:T(8,128)(2,1)S(1)}, u32[]{:S(2)}, u32[]{:S(2)}) async-start(bf16[1,32,33,128]{3,2,0,1:T(8,128)(2,1)} %bitcast.42), calls=%async_computation.2 | async-start | bytes 655360 | tf_op jit(solution)/shard_map/all_to_all | solution.py:288
  100.7 1.8 %pad_maximum_fusion.r2 = bf16[512,2048]{1,0:T(8,128)(2,1)S(1)} fusion(bf16[128,2048]{1,0:T(8,128)(2,1)} %collective-permute-done.9, bf16[128,2048]{1,0:T(8,128)(2,1)} %collective-permute-done.7, bf16[128,2048]{1,0:T(8,128)(2,1)} %collective-permute-done.6, bf16[128,2048]{1,0:T(8,128)(2,1)} %get-tuple-element.61), kind=kLoop, calls=%fused_computation.8 | loop fusion | flops 8388608 | bytes 4194304 | tf_op jit(solution)/shard_map/concatenate | solution.py:59
  102.5 50.2 %shard_map.129 = (f32[64,2048]{1,0:T(8,128)S(1)}, f32[64,2048]{1,0:T(8,128)S(1)}) custom-call(bf16[512,512]{1,0:T(8,128)(2,1)S(1)} %bitcast.89, bf16[512,2048]{1,0:T(8,128)(2,1)S(1)} %pad_maximum_fusion.r2, bf16[512,512]{1,0:T(8,128)(2,1)S(1)} %bitcast.88, bf16[512,2048]{1,0:T(8,128)(2,1)S(1)} %pad_maximum_fusion.1.r1), custom_call_target="tpu_custom_call" | custom-call | flops 2147483648 | bytes 5242880 | tf_op jit(solution)/shard_map/pallas_call | solution.py:170
  152.7 0.8 copy-done.1
  153.5 0.8 copy-done.2
  154.3 0.1 fusion.14
  154.4 1.0 fusion.9
  155.3 0.5 slice_bitcast_fusion
  155.9 1.9 %copy.42 = f32[64,2048]{1,0:T(8,128)} copy(f32[64,2048]{1,0:T(8,128)} %copy-done.2) | data formatting | bytes 1048576
  157.7 1.9 %copy.43 = f32[64,2048]{1,0:T(8,128)} copy(f32[64,2048]{1,0:T(8,128)} %copy-done.1) | data formatting | bytes 1048576
  (52 shorter events, 0.5 us)
Async XLA Ops:
  0.6 16.2 %copy-start = (bf16[256,128]{1,0:T(8,128)(2,1)S(1)}, bf16[256,128]{1,0:T(8,128)(2,1)}, u32[]{:S(2)}) copy-start(bf16[256,128]{1,0:T(8,128)(2,1)} %param.10) | copy-start | bytes 196612
  0.6 23.6 %copy-start.3 = (s32[1,2048]{1,0:T(1,128)S(1)}, s32[1,2048]{1,0:T(1,128)}, u32[]{:S(2)}) copy-start(s32[1,2048]{1,0:T(1,128)} %param.15) | copy-start | bytes 24580
  0.7 14.9 %all-to-all-start = ((s32[1,32,32]{2,0,1:T(1,128)}), s32[1,32,32]{2,0,1:T(1,128)S(1)}, u32[]{:S(2)}, u32[]{:S(2)}) async-start(s32[1,32,32]{2,0,1:T(1,128)} %bitcast.118), calls=%async_computation | async-start | bytes 32768 | tf_op jit(solution)/shard_map/all_to_all | solution.py:208
  24.3 16.5 %all-to-all-start.1 = ((bf16[32,1,32,128]{3,2,1,0:T(8,128)(2,1)}), bf16[32,1,32,128]{3,2,1,0:T(8,128)(2,1)S(1)}, u32[]{:S(2)}, u32[]{:S(2)}) async-start(bf16[32,1,32,128]{3,2,1,0:T(8,128)(2,1)} %bitcast.14), calls=%async_computation.1 | async-start | bytes 524288 | tf_op jit(solution)/shard_map/all_to_all | solution.py:232
  44.8 6.9 %collective-permute-start.2 = (bf16[1,1,8,64,128]{4,3,2,1,0:T(8,128)(2,1)S(1)}, bf16[1,1,8,64,128]{4,3,2,1,0:T(8,128)(2,1)S(1)}, u32[]{:S(2)}, u32[]{:S(2)}) collective-permute-start(bf16[1,1,8,64,128]{4,3,2,1,0:T(8,128)(2,1)S(1)} %get-tuple-element.35), channel_id=1, source_target_pairs={{0,24},{1,25},{2,26},{3,27},{4,28},{5,29},{6,30},{7,31},{8,16},{9,... | collective-permute-start | bytes 393224 | tf_op jit(solution)/shard_map/ppermute | solution.py:20
  45.5 7.9 %collective-permute-start.1 = (bf16[1,1,8,64,128]{4,3,2,1,0:T(8,128)(2,1)S(1)}, bf16[1,1,8,64,128]{4,3,2,1,0:T(8,128)(2,1)S(1)}, u32[]{:S(2)}, u32[]{:S(2)}) collective-permute-start(bf16[1,1,8,64,128]{4,3,2,1,0:T(8,128)(2,1)S(1)} %get-tuple-element.36), channel_id=1, source_target_pairs={{0,16},{1,17},{2,18},{3,19},{4,20},{5,21},{6,22},{7,23},{8,24},{9,... | collective-permute-start | bytes 393224 | tf_op jit(solution)/shard_map/ppermute | solution.py:20
  46.3 7.2 %slice-start = ((s8[8388608]{0:T(1024)(128)(4,1)}), s8[4194304]{0:T(1024)(128)(4,1)S(1)}, s32[]{:S(2)}) async-start(s8[8388608]{0:T(1024)(128)(4,1)} %bitcast.121), calls=%async_computation.3 | async-start | bytes 8388608
  46.3 7.2 %slice-start.1 = ((s8[8388608]{0:T(1024)(128)(4,1)}), s8[4194304]{0:T(1024)(128)(4,1)S(1)}, s32[]{:S(2)}) async-start(s8[8388608]{0:T(1024)(128)(4,1)} %bitcast.121), calls=%async_computation.4 | async-start | bytes 8388608
  46.3 7.1 %collective-permute-start = (bf16[1,1,8,64,128]{4,3,2,1,0:T(8,128)(2,1)S(1)}, bf16[1,1,8,64,128]{4,3,2,1,0:T(8,128)(2,1)S(1)}, u32[]{:S(2)}, u32[]{:S(2)}) collective-permute-start(bf16[1,1,8,64,128]{4,3,2,1,0:T(8,128)(2,1)S(1)} %get-tuple-element.37), channel_id=1, source_target_pairs={{0,8},{1,9},{2,10},{3,11},{4,12},{5,13},{6,14},{7,15},{8,0},{9,1},... | collective-permute-start | bytes 393224 | tf_op jit(solution)/shard_map/ppermute | solution.py:20
  53.5 1.5 copy-start.4
  56.5 27.1 %collective-permute-start.7 = (bf16[128,2048]{1,0:T(8,128)(2,1)}, bf16[128,2048]{1,0:T(8,128)(2,1)}, u32[]{:S(2)}, u32[]{:S(2)}) collective-permute-start(bf16[128,2048]{1,0:T(8,128)(2,1)} %get-tuple-element.61), channel_id=1, source_target_pairs={{0,1},{1,0},{2,3},{3,2},{4,5},{5,4},{6,7},{7,6},{8,9},{9,8},{10,11... | collective-permute-start | bytes 1572872 | tf_op jit(solution)/shard_map/ppermute | solution.py:20
  57.7 43.0 %collective-permute-start.6 = (bf16[128,2048]{1,0:T(8,128)(2,1)}, bf16[128,2048]{1,0:T(8,128)(2,1)}, u32[]{:S(2)}, u32[]{:S(2)}) collective-permute-start(bf16[128,2048]{1,0:T(8,128)(2,1)} %get-tuple-element.61), channel_id=1, source_target_pairs={{0,8},{1,9},{2,10},{3,11},{4,12},{5,13},{6,14},{7,15},{8,0},{9,1},... | collective-permute-start | bytes 1572872 | tf_op jit(solution)/shard_map/ppermute | solution.py:20
  58.0 15.0 %collective-permute-start.5 = (bf16[2,4,1,64,128]{4,3,1,0,2:T(8,128)(2,1)S(1)}, bf16[2,4,1,64,128]{4,3,1,0,2:T(8,128)(2,1)S(1)}, u32[]{:S(2)}, u32[]{:S(2)}) collective-permute-start(bf16[2,4,1,64,128]{4,3,1,0,2:T(8,128)(2,1)S(1)} %get-tuple-element.31), channel_id=1, source_target_pairs={{0,9},{1,8},{2,11},{3,10},{4,13},{5,12},{6,15},{7,14},{8,1},{9,0},... | collective-permute-start | bytes 393224 | tf_op jit(solution)/shard_map/ppermute | solution.py:20
  59.1 17.2 %collective-permute-start.4 = (bf16[2,4,1,64,128]{4,3,1,0,2:T(8,128)(2,1)S(1)}, bf16[2,4,1,64,128]{4,3,1,0,2:T(8,128)(2,1)S(1)}, u32[]{:S(2)}, u32[]{:S(2)}) collective-permute-start(bf16[2,4,1,64,128]{4,3,1,0,2:T(8,128)(2,1)S(1)} %get-tuple-element.32), channel_id=1, source_target_pairs={{0,1},{1,0},{2,3},{3,2},{4,5},{5,4},{6,7},{7,6},{8,9},{9,8},{10,11... | collective-permute-start | bytes 393224 | tf_op jit(solution)/shard_map/ppermute | solution.py:20
  60.2 16.1 %collective-permute-start.3 = (bf16[2,4,1,64,128]{4,3,1,0,2:T(8,128)(2,1)S(1)}, bf16[2,4,1,64,128]{4,3,1,0,2:T(8,128)(2,1)S(1)}, u32[]{:S(2)}, u32[]{:S(2)}) collective-permute-start(bf16[2,4,1,64,128]{4,3,1,0,2:T(8,128)(2,1)S(1)} %get-tuple-element.33), channel_id=1, source_target_pairs={{0,8},{1,9},{2,10},{3,11},{4,12},{5,13},{6,14},{7,15},{8,0},{9,1},... | collective-permute-start | bytes 393224 | tf_op jit(solution)/shard_map/ppermute | solution.py:20
  76.4 19.8 %collective-permute-start.10 = (bf16[128,2048]{1,0:T(8,128)(2,1)}, bf16[128,2048]{1,0:T(8,128)(2,1)}, u32[]{:S(2)}, u32[]{:S(2)}) collective-permute-start(bf16[128,2048]{1,0:T(8,128)(2,1)} %fusion.3), channel_id=1, source_target_pairs={{0,8},{1,9},{2,10},{3,11},{4,12},{5,13},{6,14},{7,15},{8,0},{9,1},... | collective-permute-start | bytes 1572872 | tf_op jit(solution)/shard_map/ppermute | solution.py:20
  76.5 14.7 %collective-permute-start.8 = (bf16[128,2048]{1,0:T(8,128)(2,1)}, bf16[128,2048]{1,0:T(8,128)(2,1)}, u32[]{:S(2)}, u32[]{:S(2)}) collective-permute-start(bf16[128,2048]{1,0:T(8,128)(2,1)} %fusion.3), channel_id=1, source_target_pairs={{0,16},{1,17},{2,18},{3,19},{4,20},{5,21},{6,22},{7,23},{8,24},{9,... | collective-permute-start | bytes 1572872 | tf_op jit(solution)/shard_map/ppermute | solution.py:20
  91.2 5.1 %collective-permute-start.11 = (bf16[128,2048]{1,0:T(8,128)(2,1)}, bf16[128,2048]{1,0:T(8,128)(2,1)S(1)}, u32[]{:S(2)}, u32[]{:S(2)}) collective-permute-start(bf16[128,2048]{1,0:T(8,128)(2,1)} %collective-permute-done.8), channel_id=1, source_target_pairs={{0,8},{1,9},{2,10},{3,11},{4,12},{5,13},{6,14},{7,15},{8,0},{9,1},... | collective-permute-start | bytes 1572872 | tf_op jit(solution)/shard_map/ppermute | solution.py:20
  91.2 9.5 %collective-permute-start.9 = (bf16[128,2048]{1,0:T(8,128)(2,1)}, bf16[128,2048]{1,0:T(8,128)(2,1)}, u32[]{:S(2)}, u32[]{:S(2)}) collective-permute-start(bf16[128,2048]{1,0:T(8,128)(2,1)} %collective-permute-done.7), channel_id=1, source_target_pairs={{0,8},{1,9},{2,10},{3,11},{4,12},{5,13},{6,14},{7,15},{8,0},{9,1},... | collective-permute-start | bytes 1572872 | tf_op jit(solution)/shard_map/ppermute | solution.py:20
  97.7 56.6 %all-to-all-start.2 = ((bf16[1,32,33,128]{3,2,0,1:T(8,128)(2,1)}), bf16[1,32,33,128]{3,2,0,1:T(8,128)(2,1)S(1)}, u32[]{:S(2)}, u32[]{:S(2)}) async-start(bf16[1,32,33,128]{3,2,0,1:T(8,128)(2,1)} %bitcast.42), calls=%async_computation.2 | async-start | bytes 655360 | tf_op jit(solution)/shard_map/all_to_all | solution.py:288
  152.7 0.8 copy-start.1
  153.5 0.8 copy-start.2

commit v6 on v5

--- a/solution.py
+++ b/solution.py
@@ -266,13 +266,14 @@
         dz2, w_second, (((1,), (1,)), ((), ())), preferred_element_type=jnp.float32
     )
     dz1 = (back_two * silu_slope(z1)).astype(jnp.bfloat16)
-    h1_left, dz1 = lax.optimization_barrier((h1_left, dz1))
     across1 = swap(dz1, 2 << core_bit)
     back_one = lax.dot_general(
         dz1, w_first, (((1,), (1,)), ((), ())), preferred_element_type=jnp.float32
     )
     bag_grad = (back_one.reshape(bags, width) * scale).astype(jnp.bfloat16)
-    across2, across1, bag_grad = lax.optimization_barrier((across2, across1, bag_grad))
+    across2, across1, h1_left, bag_grad = lax.optimization_barrier(
+        (across2, across1, h1_left, bag_grad)
+    )
     dz2_all = gather_right(dz2, across2, core_bit)
     dz1_all = gather_right(dz1, across1, core_bit)
     slot_grad = lax.dot_general(

time: 161 us -> 147 us (0.913)
  waiting for transfers between devices: 20.5 us -> 10.1 us
  matrix products: 35.7 us -> 29.3 us
  starting transfers between devices: 22.2 us -> 24.2 us
    ppermute x12, waiting for transfers between devices: 17.8 us -> 7.41 us  [swap(): return lax.ppermute(value, AXES, [(d, d ^ mask) for d in range(peers)])]
    dot_general x1, matrix products: 6.43 us -> 2.88 us  [per_device(): lax.dot_general(dz1, w_first, (((1,), (1,)), ((), ())), preferred_element...]
    dot_general x1, matrix products: 7.32 us -> 4.19 us  [per_device(): lax.dot_general(dz2, w_second, (((1,), (1,)), ((), ())), preferred_elemen...]
    ppermute x12, starting transfers between devices: 6.12 us -> 7.96 us  [swap(): return lax.ppermute(value, AXES, [(d, d ^ mask) for d in range(peers)])]
    unnamed x17 -> x23, local copies, waits for them, and re-layouts: 6.04 us -> 6.06 us
  transfers between devices with their start and end apart: 15 -> 15, of which waited for: 5 -> 4; matrix products, arithmetic and copies ran while one was open for 27% -> 26% of each run, Pallas kernels for 31% -> 34%
where the time goes in v6:
time: 147 us; the launch traced here: 146 us
  Pallas kernels  50.2 us (34%)
  matrix products  29.3 us (20%)
  starting transfers between devices  24.2 us (16%)
  other arithmetic  21.1 us (14%)
  local copies, waits for them, and re-layouts  10.1 us (7%)
  waiting for transfers between devices  10.1 us (7%)
    pallas_call x1, Pallas kernels, halve(): pl.pallas_call(functools.partial(halving_kernel, core_bit, both), out_sha...  50.2 us
    convert_element_type x1, other arithmetic, per_device(): counted = lax.optimization_barrier(counted.astype(jnp.bfloat16))  7.98 us
    ppermute x12, starting transfers between devices, swap(): return lax.ppermute(value, AXES, [(d, d ^ mask) for d in range(peers)])  7.96 us
    ppermute x12, waiting for transfers between devices, swap(): return lax.ppermute(value, AXES, [(d, d ^ mask) for d in range(peers)])  7.41 us
    all_to_all x1, starting transfers between devices, per_device(): lax.all_to_all(request_rows, AXES, split_axis=1, concat_axis=0, tiled=True)  7.3 us
    dot_general x1, matrix products, per_device(): lax.dot_general(first, shifted, (((1,), (1,)), ((), ())), preferred_eleme...  6.2 us
    unnamed x23, local copies, waits for them, and re-layouts  6.06 us
    all_to_all x1, starting transfers between devices, per_device(): lax.all_to_all(served.reshape(peers, 1, slots, width), AXES, split_axis=0...  5.84 us
  transfers between devices with their start and end apart: 15, of which 4 were waited for; matrix products, arithmetic and copies ran while one was open for 26% of the time, Pallas kernels for 34%

profile of v6, /device:TPU:0, one launch (start us, length us, event | category | flops | bytes accessed | tf_op | source)
XLA Modules:
  0.0 146.1 jit_solution(9933735415489020558)
XLA Ops:
  0.7 7.3 %all-to-all-start = ((s32[1,32,32]{2,0,1:T(1,128)}), s32[1,32,32]{2,0,1:T(1,128)S(1)}, u32[]{:S(2)}, u32[]{:S(2)}) async-start(s32[1,32,32]{2,0,1:T(1,128)} %bitcast.117), calls=%async_computation | async-start | bytes 32768 | tf_op jit(solution)/shard_map/all_to_all | solution.py:208
  8.0 0.7 slice.99
  8.7 0.7 convert_rsqrt_fusion
  9.4 1.0 reduce-window.9
  10.4 0.1 slice.129
  10.5 0.1 slice_reduce_fusion
  10.6 0.8 bitcast_subtract_fusion
  11.4 0.9 select_reduce_fusion
  12.3 0.9 fusion.13
  13.2 0.1 pad_slice_fusion
  13.3 0.1 pad_slice_fusion.7
  13.4 0.7 convert_element_type.111
  14.1 0.7 reshape.148
  15.1 0.4 stack.67
  15.5 0.5 broadcast.30
  16.1 0.7 reduce.6
  16.7 0.1 eq.169
  16.8 1.2 convolution_convert_fusion
  18.0 6.2 %fusion = f32[2048,16]{0,1:T(8,128)S(1)} fusion(bf16[16,4096]{1,0:T(8,128)(2,1)S(1)} %stack.67, s32[2048]{0:T(1024)S(1)} %bitcast_subtract_fusion), kind=kOutput, calls=%fused_computation.1 | convolution fusion | flops 276824064 | bytes 270336 | tf_op jit(solution)/shard_map/dot_general | solution.py:236
  24.3 5.8 %all-to-all-start.1 = ((bf16[32,1,32,128]{3,2,1,0:T(8,128)(2,1)}), bf16[32,1,32,128]{3,2,1,0:T(8,128)(2,1)S(1)}, u32[]{:S(2)}, u32[]{:S(2)}) async-start(bf16[32,1,32,128]{3,2,1,0:T(8,128)(2,1)} %bitcast.14), calls=%async_computation.1 | async-start | bytes 524288 | tf_op jit(solution)/shard_map/all_to_all | solution.py:232
  30.2 8.0 %add_convert_fusion = bf16[2048,1024]{1,0:T(8,128)(2,1)} fusion(f32[1024]{0:T(1024)S(1)} %iota_convert_fusion, f32[2048]{0:T(1024)S(1)} %bitcast.110, f32[2048]{0:T(1024)S(1)} %bitcast.111, f32[2048]{0:T(1024)S(1)} %bitcast.112, f32[2048]{0:T(1024)S(1)} %bitcast.113, f32[2048]{0:T(1024)S(1)} %bitcast.114, f32[2048]{0:T(1024)S(1)} %bitcast.115, ...), kind=kLoop, calls=%fused_computation.3 | loop fusion | flops 50331648 | bytes 4263936 | tf_op jit(solution)/shard_map/convert_element_type | solution.py:246
  38.1 2.7 %all-to-all-done.1 = bf16[32,1,32,128]{3,2,1,0:T(8,128)(2,1)S(1)} async-done(((bf16[32,1,32,128]{3,2,1,0:T(8,128)(2,1)}), bf16[32,1,32,128]{3,2,1,0:T(8,128)(2,1)S(1)}, u32[]{:S(2)}, u32[]{:S(2)}) %all-to-all-start.1) | async-done | bytes 262176 | tf_op jit(solution)/shard_map/all_to_all | solution.py:232
  40.8 3.4 %fusion.2 = bf16[2048,128]{1,0:T(8,128)(2,1)S(1)} fusion(bf16[2048,1024]{1,0:T(8,128)(2,1)} %add_convert_fusion, bf16[1024,128]{1,0:T(8,128)(2,1)S(1)} %bitcast.100, f32[2048]{0:T(1024)S(1)} %convert_rsqrt_fusion), kind=kOutput, calls=%fused_computation.6 | convolution fusion | flops 537395200 | bytes 4988928 | tf_op jit(solution)/shard_map/dot_general | solution.py:248
  44.3 0.2 reshape.138
  44.5 0.3 copy.35
  44.8 0.6 collective-permute-start.2
  45.5 0.8 collective-permute-start.1
  46.3 0.5 collective-permute-start
  46.8 5.0 %multiply_convert_fusion.3 = (bf16[128,2048]{1,0:T(8,128)(2,1)S(1)}, f32[128,2048]{1,0:T(8,128)S(1)}) fusion(bf16[128,2048]{1,0:T(8,128)(2,1)S(1)} %reshape.138, bf16[2048,2048]{1,0:T(8,128)(2,1)} %param.17), kind=kOutput, calls=%fused_computation.23 | convolution fusion | flops 1075052544 | bytes 10485760 | tf_op jit(solution)/shard_map/dot_general | solution.py:252
  51.7 1.6 %collective-permute-done.1 = bf16[1,1,8,64,128]{4,3,2,1,0:T(8,128)(2,1)S(1)} collective-permute-done((bf16[1,1,8,64,128]{4,3,2,1,0:T(8,128)(2,1)S(1)}, bf16[1,1,8,64,128]{4,3,2,1,0:T(8,128)(2,1)S(1)}, u32[]{:S(2)}, u32[]{:S(2)}) %collective-permute-start.1) | collective-permute-done | bytes 131104 | tf_op jit(solution)/shard_map/ppermute | solution.py:20
  53.4 0.1 maximum_bitcast_fusion
  53.5 1.4 multiply_convert_fusion.2
  55.0 0.2 fusion.8
  55.2 1.3 multiply_reduce_fusion
  56.5 1.2 collective-permute-start.3
  57.7 4.2 %fusion.3 = bf16[128,2048]{1,0:T(8,128)(2,1)S(1)} fusion(bf16[128,2048]{1,0:T(8,128)(2,1)} %get-tuple-element.59, bf16[2048,2048]{1,0:T(8,128)(2,1)S(1)} %bitcast.121, f32[128,2048]{1,0:T(8,128)S(1)} %get-tuple-element.61), kind=kOutput, calls=%fused_computation.7 | convolution fusion | flops 1076101120 | bytes 10485760 | tf_op jit(solution)/shard_map/dot_general | solution.py:265
  61.9 0.6 collective-permute-start.4
  62.5 2.9 %fusion.16 = f32[128,2048]{1,0:T(8,128)S(1)} fusion(bf16[128,2048]{1,0:T(8,128)(2,1)S(1)} %fusion.3, bf16[2048,2048]{1,0:T(8,128)(2,1)S(1)} %bitcast.91), kind=kOutput, calls=%fused_computation.72 | convolution fusion | flops 1073741824 | bytes 9961472 | tf_op jit(solution)/shard_map/dot_general | solution.py:270
  65.4 0.3 copy.37
  65.7 0.8 constant_dynamic-slice_fusion
  66.5 1.0 collective-permute-start.6
  67.5 0.8 collective-permute-start.5
  68.3 0.2 reshape.143
  68.5 0.3 multiply_convert_fusion
  68.8 0.1 reshape.145
  68.9 3.9 %collective-permute-done.7 = bf16[2,4,1,64,128]{4,3,1,0,2:T(8,128)(2,1)} collective-permute-done((bf16[2,4,1,64,128]{4,3,1,0,2:T(8,128)(2,1)}, bf16[2,4,1,64,128]{4,3,1,0,2:T(8,128)(2,1)}, u32[]{:S(2)}, u32[]{:S(2)}) %collective-permute-start.7) | collective-permute-done | bytes 131104 | tf_op jit(solution)/shard_map/ppermute | solution.py:20
  72.8 1.7 %collective-permute-start.10 = (bf16[128,2048]{1,0:T(8,128)(2,1)S(1)}, bf16[128,2048]{1,0:T(8,128)(2,1)S(1)}, u32[]{:S(2)}, u32[]{:S(2)}) collective-permute-start(bf16[128,2048]{1,0:T(8,128)(2,1)S(1)} %fusion.3), channel_id=1, source_target_pairs={{0,8},{1,9},{2,10},{3,11},{4,12},{5,13},{6,14},{7,15},{8,0},{9,1},... | collective-permute-start | bytes 1572872 | tf_op jit(solution)/shard_map/ppermute | solution.py:20
  74.6 1.9 %collective-permute-done.6 = bf16[2,4,1,64,128]{4,3,1,0,2:T(8,128)(2,1)} collective-permute-done((bf16[2,4,1,64,128]{4,3,1,0,2:T(8,128)(2,1)}, bf16[2,4,1,64,128]{4,3,1,0,2:T(8,128)(2,1)}, u32[]{:S(2)}, u32[]{:S(2)}) %collective-permute-start.6) | collective-permute-done | bytes 131104 | tf_op jit(solution)/shard_map/ppermute | solution.py:20
  76.4 1.1 maximum_bitcast_fusion.1
  77.6 0.6 collective-permute-start.11
  78.2 0.1 collective-permute-start.9
  78.3 3.7 %convolution_convert_fusion.1 = bf16[1024,128]{1,0:T(8,128)(2,1)S(1)} fusion(bf16[2048,1024]{1,0:T(8,128)(2,1)} %add_convert_fusion, bf16[2048,128]{1,0:T(8,128)(2,1)S(1)} %multiply_convert_fusion), kind=kOutput, calls=%fused_computation.11 | convolution fusion | flops 537001984 | bytes 4980736 | tf_op jit(solution)/shard_map/dot_general | solution.py:279
  82.0 0.8 pad_maximum_fusion.2
  82.8 1.3 pad_maximum_fusion.1.r1
  84.1 3.1 %all-to-all-start.2 = ((bf16[1,32,33,128]{3,2,0,1:T(8,128)(2,1)}), bf16[1,32,33,128]{3,2,0,1:T(8,128)(2,1)S(1)}, u32[]{:S(2)}, u32[]{:S(2)}) async-start(bf16[1,32,33,128]{3,2,0,1:T(8,128)(2,1)} %bitcast.42), calls=%async_computation.2 | async-start | bytes 655360 | tf_op jit(solution)/shard_map/all_to_all | solution.py:289
  87.2 1.8 %pad_maximum_fusion.r2 = bf16[512,2048]{1,0:T(8,128)(2,1)S(1)} fusion(bf16[128,2048]{1,0:T(8,128)(2,1)} %collective-permute-done.9, bf16[128,2048]{1,0:T(8,128)(2,1)} %collective-permute-done.3, bf16[128,2048]{1,0:T(8,128)(2,1)} %collective-permute-done.8, bf16[128,2048]{1,0:T(8,128)(2,1)} %get-tuple-element.59), kind=kLoop, calls=%fused_computation.8 | loop fusion | flops 8388608 | bytes 4194304 | tf_op jit(solution)/shard_map/concatenate | solution.py:59
  89.0 50.2 %shard_map.129 = (f32[64,2048]{1,0:T(8,128)S(1)}, f32[64,2048]{1,0:T(8,128)S(1)}) custom-call(bf16[512,512]{1,0:T(8,128)(2,1)S(1)} %bitcast.89, bf16[512,2048]{1,0:T(8,128)(2,1)S(1)} %pad_maximum_fusion.r2, bf16[512,512]{1,0:T(8,128)(2,1)S(1)} %bitcast.88, bf16[512,2048]{1,0:T(8,128)(2,1)S(1)} %pad_maximum_fusion.1.r1), custom_call_target="tpu_custom_call" | custom-call | flops 2147483648 | bytes 5242880 | tf_op jit(solution)/shard_map/pallas_call | solution.py:170
  139.2 0.8 copy-done.1
  140.0 0.8 copy-done.2
  140.8 0.1 fusion.14
  140.9 1.0 fusion.9
  141.8 0.5 slice_bitcast_fusion
  142.4 1.9 %copy.42 = f32[64,2048]{1,0:T(8,128)} copy(f32[64,2048]{1,0:T(8,128)} %copy-done.2) | data formatting | bytes 1048576
  144.2 1.9 %copy.43 = f32[64,2048]{1,0:T(8,128)} copy(f32[64,2048]{1,0:T(8,128)} %copy-done.1) | data formatting | bytes 1048576
  (59 shorter events, 0.5 us)
Async XLA Ops:
  0.6 16.2 %copy-start = (bf16[256,128]{1,0:T(8,128)(2,1)S(1)}, bf16[256,128]{1,0:T(8,128)(2,1)}, u32[]{:S(2)}) copy-start(bf16[256,128]{1,0:T(8,128)(2,1)} %param.10) | copy-start | bytes 196612
  0.6 23.6 %copy-start.4 = (s32[1,2048]{1,0:T(1,128)S(1)}, s32[1,2048]{1,0:T(1,128)}, u32[]{:S(2)}) copy-start(s32[1,2048]{1,0:T(1,128)} %param.15) | copy-start | bytes 24580
  0.7 14.9 %all-to-all-start = ((s32[1,32,32]{2,0,1:T(1,128)}), s32[1,32,32]{2,0,1:T(1,128)S(1)}, u32[]{:S(2)}, u32[]{:S(2)}) async-start(s32[1,32,32]{2,0,1:T(1,128)} %bitcast.117), calls=%async_computation | async-start | bytes 32768 | tf_op jit(solution)/shard_map/all_to_all | solution.py:208
  24.3 16.5 %all-to-all-start.1 = ((bf16[32,1,32,128]{3,2,1,0:T(8,128)(2,1)}), bf16[32,1,32,128]{3,2,1,0:T(8,128)(2,1)S(1)}, u32[]{:S(2)}, u32[]{:S(2)}) async-start(bf16[32,1,32,128]{3,2,1,0:T(8,128)(2,1)} %bitcast.14), calls=%async_computation.1 | async-start | bytes 524288 | tf_op jit(solution)/shard_map/all_to_all | solution.py:232
  44.8 6.9 %collective-permute-start.2 = (bf16[1,1,8,64,128]{4,3,2,1,0:T(8,128)(2,1)S(1)}, bf16[1,1,8,64,128]{4,3,2,1,0:T(8,128)(2,1)S(1)}, u32[]{:S(2)}, u32[]{:S(2)}) collective-permute-start(bf16[1,1,8,64,128]{4,3,2,1,0:T(8,128)(2,1)S(1)} %get-tuple-element.33), channel_id=1, source_target_pairs={{0,24},{1,25},{2,26},{3,27},{4,28},{5,29},{6,30},{7,31},{8,16},{9,... | collective-permute-start | bytes 393224 | tf_op jit(solution)/shard_map/ppermute | solution.py:20
  45.5 7.9 %collective-permute-start.1 = (bf16[1,1,8,64,128]{4,3,2,1,0:T(8,128)(2,1)S(1)}, bf16[1,1,8,64,128]{4,3,2,1,0:T(8,128)(2,1)S(1)}, u32[]{:S(2)}, u32[]{:S(2)}) collective-permute-start(bf16[1,1,8,64,128]{4,3,2,1,0:T(8,128)(2,1)S(1)} %get-tuple-element.34), channel_id=1, source_target_pairs={{0,16},{1,17},{2,18},{3,19},{4,20},{5,21},{6,22},{7,23},{8,24},{9,... | collective-permute-start | bytes 393224 | tf_op jit(solution)/shard_map/ppermute | solution.py:20
  46.3 7.2 %slice-start.2 = ((s8[8388608]{0:T(1024)(128)(4,1)}), s8[4194304]{0:T(1024)(128)(4,1)S(1)}, s32[]{:S(2)}) async-start(s8[8388608]{0:T(1024)(128)(4,1)} %bitcast.120), calls=%async_computation.5 | async-start | bytes 8388608
  46.3 7.2 %slice-start.3 = ((s8[8388608]{0:T(1024)(128)(4,1)}), s8[4194304]{0:T(1024)(128)(4,1)S(1)}, s32[]{:S(2)}) async-start(s8[8388608]{0:T(1024)(128)(4,1)} %bitcast.120), calls=%async_computation.6 | async-start | bytes 8388608
  46.3 7.1 %collective-permute-start = (bf16[1,1,8,64,128]{4,3,2,1,0:T(8,128)(2,1)S(1)}, bf16[1,1,8,64,128]{4,3,2,1,0:T(8,128)(2,1)S(1)}, u32[]{:S(2)}, u32[]{:S(2)}) collective-permute-start(bf16[1,1,8,64,128]{4,3,2,1,0:T(8,128)(2,1)S(1)} %get-tuple-element.35), channel_id=1, source_target_pairs={{0,8},{1,9},{2,10},{3,11},{4,12},{5,13},{6,14},{7,15},{8,0},{9,1},... | collective-permute-start | bytes 393224 | tf_op jit(solution)/shard_map/ppermute | solution.py:20
  53.5 1.5 %copy-start.5 = (s32[128]{0:T(128)S(1)}, s32[128]{0:T(128)}, u32[]{:S(2)}) copy-start(s32[128]{0:T(128)} %param.16) | copy-start | bytes 1540
  55.0 7.6 %slice-start = ((s8[8388608]{0:T(1024)(128)(4,1)}), s8[4194304]{0:T(1024)(128)(4,1)S(1)}, s32[]{:S(2)}) async-start(s8[8388608]{0:T(1024)(128)(4,1)} %bitcast.90), calls=%async_computation.3 | async-start | bytes 8388608
  56.5 21.1 %collective-permute-start.3 = (bf16[128,2048]{1,0:T(8,128)(2,1)}, bf16[128,2048]{1,0:T(8,128)(2,1)}, u32[]{:S(2)}, u32[]{:S(2)}) collective-permute-start(bf16[128,2048]{1,0:T(8,128)(2,1)} %get-tuple-element.59), channel_id=1, source_target_pairs={{0,1},{1,0},{2,3},{3,2},{4,5},{5,4},{6,7},{7,6},{8,9},{9,8},{10,11... | collective-permute-start | bytes 1572872 | tf_op jit(solution)/shard_map/ppermute | solution.py:20
  57.7 4.8 %slice-start.1 = ((s8[8388608]{0:T(1024)(128)(4,1)}), s8[4194304]{0:T(1024)(128)(4,1)S(1)}, s32[]{:S(2)}) async-start(s8[8388608]{0:T(1024)(128)(4,1)} %bitcast.90), calls=%async_computation.4 | async-start | bytes 8388608
  61.9 15.6 %copy-start.3 = (bf16[128,2048]{1,0:T(8,128)(2,1)}, bf16[128,2048]{1,0:T(8,128)(2,1)S(1)}, u32[]{:S(2)}) copy-start(bf16[128,2048]{1,0:T(8,128)(2,1)S(1)} %fusion.3) | copy-start | bytes 1572868
  61.9 15.7 %collective-permute-start.4 = (bf16[128,2048]{1,0:T(8,128)(2,1)S(1)}, bf16[128,2048]{1,0:T(8,128)(2,1)}, u32[]{:S(2)}, u32[]{:S(2)}) collective-permute-start(bf16[128,2048]{1,0:T(8,128)(2,1)S(1)} %fusion.3), channel_id=1, source_target_pairs={{0,16},{1,17},{2,18},{3,19},{4,20},{5,21},{6,22},{7,23},{8,24},{9,... | collective-permute-start | bytes 1572872 | tf_op jit(solution)/shard_map/ppermute | solution.py:20
  66.4 6.4 %collective-permute-start.7 = (bf16[2,4,1,64,128]{4,3,1,0,2:T(8,128)(2,1)}, bf16[2,4,1,64,128]{4,3,1,0,2:T(8,128)(2,1)}, u32[]{:S(2)}, u32[]{:S(2)}) collective-permute-start(bf16[2,4,1,64,128]{4,3,1,0,2:T(8,128)(2,1)} %get-tuple-element.29), channel_id=1, source_target_pairs={{0,9},{1,8},{2,11},{3,10},{4,13},{5,12},{6,15},{7,14},{8,1},{9,0},... | collective-permute-start | bytes 393224 | tf_op jit(solution)/shard_map/ppermute | solution.py:20
  66.5 10.0 %collective-permute-start.6 = (bf16[2,4,1,64,128]{4,3,1,0,2:T(8,128)(2,1)}, bf16[2,4,1,64,128]{4,3,1,0,2:T(8,128)(2,1)}, u32[]{:S(2)}, u32[]{:S(2)}) collective-permute-start(bf16[2,4,1,64,128]{4,3,1,0,2:T(8,128)(2,1)} %get-tuple-element.30), channel_id=1, source_target_pairs={{0,1},{1,0},{2,3},{3,2},{4,5},{5,4},{6,7},{7,6},{8,9},{9,8},{10,11... | collective-permute-start | bytes 393224 | tf_op jit(solution)/shard_map/ppermute | solution.py:20
  67.5 8.9 %collective-permute-start.5 = (bf16[2,4,1,64,128]{4,3,1,0,2:T(8,128)(2,1)S(1)}, bf16[2,4,1,64,128]{4,3,1,0,2:T(8,128)(2,1)}, u32[]{:S(2)}, u32[]{:S(2)}) collective-permute-start(bf16[2,4,1,64,128]{4,3,1,0,2:T(8,128)(2,1)S(1)} %get-tuple-element.31), channel_id=1, source_target_pairs={{0,8},{1,9},{2,10},{3,11},{4,12},{5,13},{6,14},{7,15},{8,0},{9,1},... | collective-permute-start | bytes 393224 | tf_op jit(solution)/shard_map/ppermute | solution.py:20
  72.8 10.0 %collective-permute-start.10 = (bf16[128,2048]{1,0:T(8,128)(2,1)S(1)}, bf16[128,2048]{1,0:T(8,128)(2,1)S(1)}, u32[]{:S(2)}, u32[]{:S(2)}) collective-permute-start(bf16[128,2048]{1,0:T(8,128)(2,1)S(1)} %fusion.3), channel_id=1, source_target_pairs={{0,8},{1,9},{2,10},{3,11},{4,12},{5,13},{6,14},{7,15},{8,0},{9,1},... | collective-permute-start | bytes 1572872 | tf_op jit(solution)/shard_map/ppermute | solution.py:20
  76.4 10.8 %collective-permute-start.8 = (bf16[128,2048]{1,0:T(8,128)(2,1)}, bf16[128,2048]{1,0:T(8,128)(2,1)}, u32[]{:S(2)}, u32[]{:S(2)}) collective-permute-start(bf16[128,2048]{1,0:T(8,128)(2,1)} %get-tuple-element.59), channel_id=1, source_target_pairs={{0,8},{1,9},{2,10},{3,11},{4,12},{5,13},{6,14},{7,15},{8,0},{9,1},... | collective-permute-start | bytes 1572872 | tf_op jit(solution)/shard_map/ppermute | solution.py:20
  77.6 5.2 %collective-permute-start.11 = (bf16[128,2048]{1,0:T(8,128)(2,1)}, bf16[128,2048]{1,0:T(8,128)(2,1)S(1)}, u32[]{:S(2)}, u32[]{:S(2)}) collective-permute-start(bf16[128,2048]{1,0:T(8,128)(2,1)} %collective-permute-done.4), channel_id=1, source_target_pairs={{0,8},{1,9},{2,10},{3,11},{4,12},{5,13},{6,14},{7,15},{8,0},{9,1},... | collective-permute-start | bytes 1572872 | tf_op jit(solution)/shard_map/ppermute | solution.py:20
  78.2 9.0 %collective-permute-start.9 = (bf16[128,2048]{1,0:T(8,128)(2,1)}, bf16[128,2048]{1,0:T(8,128)(2,1)}, u32[]{:S(2)}, u32[]{:S(2)}) collective-permute-start(bf16[128,2048]{1,0:T(8,128)(2,1)} %collective-permute-done.3), channel_id=1, source_target_pairs={{0,8},{1,9},{2,10},{3,11},{4,12},{5,13},{6,14},{7,15},{8,0},{9,1},... | collective-permute-start | bytes 1572872 | tf_op jit(solution)/shard_map/ppermute | solution.py:20
  84.1 56.7 %all-to-all-start.2 = ((bf16[1,32,33,128]{3,2,0,1:T(8,128)(2,1)}), bf16[1,32,33,128]{3,2,0,1:T(8,128)(2,1)S(1)}, u32[]{:S(2)}, u32[]{:S(2)}) async-start(bf16[1,32,33,128]{3,2,0,1:T(8,128)(2,1)} %bitcast.42), calls=%async_computation.2 | async-start | bytes 655360 | tf_op jit(solution)/shard_map/all_to_all | solution.py:289
  139.2 0.8 copy-start.1
  140.0 0.8 copy-start.2
